TPU v7x, 32 devices: a whole 2x2x4 slice. The times are simulated.
32 devices in a mesh: dp: 2 (over y), seq: 16 (over z, x, core).
Axes of the slice: x: 2, y: 2, z: 4, core: 2. Of those that a mesh axis runs over, the one named last changes fastest.
Arguments:
- tokens: bfloat16 [4096, 2048], P(('dp', 'seq')), may hold values from -6 to 6
- gain_attn: bfloat16 [2048], P(('dp', 'seq')), may hold values from 0.5 to 1.5
- w_query: bfloat16 [2048, 2048], P(('dp', 'seq')), may hold values from -0.125 to 0.125
- w_key: bfloat16 [2048, 256], P(('dp', 'seq')), may hold values from -0.125 to 0.125
- w_value: bfloat16 [2048, 256], P(('dp', 'seq')), may hold values from -0.125 to 0.125
- w_out: bfloat16 [2048, 2048], P(('dp', 'seq')), may hold values from -1 to 1
- gain_mlp: bfloat16 [2048], P(('dp', 'seq')), may hold values from 0.5 to 1.5
- w_gate: bfloat16 [2048, 5632], P(None, ('dp', 'seq')), may hold values from -0.125 to 0.125
- w_up: bfloat16 [2048, 5632], P(None, ('dp', 'seq')), may hold values from -0.125 to 0.125
- w_down: bfloat16 [5632, 2048], P(('dp', 'seq')), may hold values from -0.078125 to 0.078125
- doc_ids: int32 [2, 2048], P('dp'), may hold values from 0 to 2, never falling along the last dimension, each value on 1 to 2000 neighbouring positions
- cotangent: bfloat16 [4096, 2048], P(('dp', 'seq')), may hold values from -6 to 6
Outputs:
- block_out: bfloat16 [4096, 2048], P(('dp', 'seq'))
- input_grad: float32 [4096, 2048], P(('dp', 'seq'))
- grad_gain_attn: float32 [2048], P(('dp', 'seq'))
- grad_w_query: float32 [2048, 2048], P(('dp', 'seq'))
- grad_w_key: float32 [2048, 256], P(('dp', 'seq'))
- grad_w_value: float32 [2048, 256], P(('dp', 'seq'))
- grad_w_out: float32 [2048, 2048], P(('dp', 'seq'))
- grad_gain_mlp: float32 [2048], P(('dp', 'seq'))
- grad_w_gate: float32 [2048, 5632], P(None, ('dp', 'seq'))
- grad_w_up: float32 [2048, 5632], P(None, ('dp', 'seq'))
- grad_w_down: float32 [5632, 2048], P(('dp', 'seq'))
Inputs may be any that keep to these rules, and one draw needn't show every extreme that they name: `doc_ids`: within each sequence the ids never fall, every id covers at most 2000 consecutive tokens, and some document has exactly 2000 tokens.
All inputs are finite; a program needn't handle non-finite values.
Results may differ from a plain program's by a relative error of at most 0.019.
Values may be sent and summed in bfloat16 or wider, within the bound.
A program may use at most 384 MiB of HBM per device.

v0:
```python
import jax
import jax.numpy as jnp
from jax import lax
from jax.sharding import PartitionSpec as P

HEADS = 32
KV_HEADS = 4
HEAD_DIM = 64


NORM_EPS = 1e-05
MASKED = -1e30


def angles(positions):
    half_dim = HEAD_DIM // 2
    frequency = 10000.0 ** (-jnp.arange(half_dim, dtype=jnp.float32) / half_dim)
    phases = positions.astype(jnp.float32)[:, None] * frequency[None, :]
    return (jnp.cos(phases), jnp.sin(phases))


def rotate(field, cosines, sine_vals):
    half_dim = field.shape[-1] // 2
    front_half = field[..., :half_dim]
    back_half = field[..., half_dim:]
    return jnp.concatenate(
        [
            front_half * cosines - back_half * sine_vals,
            back_half * cosines + front_half * sine_vals,
        ],
        axis=-1,
    )


def rotate_back(field, cosines, sine_vals):
    half_dim = field.shape[-1] // 2
    front_half = field[..., :half_dim]
    back_half = field[..., half_dim:]
    return jnp.concatenate(
        [
            front_half * cosines + back_half * sine_vals,
            back_half * cosines - front_half * sine_vals,
        ],
        axis=-1,
    )


def rms_norm(field, gain_vec):
    inv_rms = lax.rsqrt(jnp.mean(field * field, axis=-1, keepdims=True) + NORM_EPS)
    return field * inv_rms * gain_vec


def plain_dot(left, right):
    return jnp.dot(left, right, preferred_element_type=jnp.float32)


def matmul_nt(left, right):
    return lax.dot_general(
        left, right, (((1,), (1,)), ((), ())), preferred_element_type=jnp.float32
    )


def matmul_tn(left, right):
    return lax.dot_general(
        left, right, (((0,), (0,)), ((), ())), preferred_element_type=jnp.float32
    )


def masked_scores(query_head, key_head, allowed, score_scale):
    raw_scores = (
        jnp.einsum("tgd,sd->tgs", query_head, key_head, preferred_element_type=jnp.float32)
        * score_scale
    )
    return jnp.where(allowed[:, None, :], raw_scores, MASKED)


def attend_forward(query_head, key_head, value_head, allowed, score_scale):
    scores = masked_scores(query_head, key_head, allowed, score_scale)
    row_max = jnp.max(scores, axis=2, keepdims=True)
    exp_scores = jnp.exp(scores - row_max)
    exp_total = jnp.sum(exp_scores, axis=2, keepdims=True)
    prob_rows = (exp_scores / exp_total).astype(jnp.bfloat16)
    head_out = jnp.einsum("tgs,sd->tgd", prob_rows, value_head, preferred_element_type=jnp.float32)
    return (head_out, (row_max + jnp.log(exp_total))[..., 0])


def attend_backward(query_head, key_head, value_head, log_total, grad_head, allowed, score_scale):
    scores = masked_scores(query_head, key_head, allowed, score_scale)
    prob_rows = jnp.exp(scores - log_total[..., None])
    grad_probs = jnp.einsum(
        "tgd,sd->tgs", grad_head, value_head, preferred_element_type=jnp.float32
    )
    row_delta = jnp.sum(prob_rows * grad_probs, axis=2, keepdims=True)
    grad_scores = (prob_rows * (grad_probs - row_delta)).astype(jnp.bfloat16)
    grad_query = (
        jnp.einsum("tgs,sd->tgd", grad_scores, key_head, preferred_element_type=jnp.float32)
        * score_scale
    )
    grad_key = (
        jnp.einsum("tgs,tgd->sd", grad_scores, query_head, preferred_element_type=jnp.float32)
        * score_scale
    )
    grad_value = jnp.einsum(
        "tgs,tgd->sd", prob_rows.astype(jnp.bfloat16), grad_head, preferred_element_type=jnp.float32
    )
    return (grad_query, grad_key, grad_value)


def swiglu(gate_in, up_in):
    return jax.nn.silu(gate_in) * up_in


def local(
    tokens,
    gain_attn,
    w_query,
    w_key,
    w_value,
    w_out,
    gain_mlp,
    w_gate,
    w_up,
    w_down,
    doc_ids,
    cotangent,
):
    tok_count = tokens.shape[0]
    group_size = HEADS // KV_HEADS
    score_scale = HEAD_DIM ** (-0.5)
    seq_ids = doc_ids[0]
    length = seq_ids.shape[0]
    first_row = lax.axis_index("seq") * tok_count
    own_ids = lax.dynamic_slice_in_dim(seq_ids, first_row, tok_count, 0)
    query_pos = first_row + jnp.arange(tok_count, dtype=jnp.int32)
    key_pos = jnp.arange(length, dtype=jnp.int32)
    doc_starts = jnp.sum((seq_ids[None, :] < own_ids[:, None]).astype(jnp.int32), axis=1)
    cosines, sine_vals = angles(query_pos - doc_starts)
    cos_heads = cosines[:, None, :]
    sin_heads = sine_vals[:, None, :]
    allowed = (seq_ids[None, :] == own_ids[:, None]) & (key_pos[None, :] <= query_pos[:, None])
    attn_full = (
        lax.all_gather(gain_attn, ("dp", "seq"), axis=0, tiled=True),
        lax.all_gather(w_query, ("dp", "seq"), axis=0, tiled=True),
        lax.all_gather(w_key, ("dp", "seq"), axis=0, tiled=True),
        lax.all_gather(w_value, ("dp", "seq"), axis=0, tiled=True),
        lax.all_gather(w_out, ("dp", "seq"), axis=0, tiled=True),
        lax.all_gather(gain_mlp, ("dp", "seq"), axis=0, tiled=True),
    )
    gain_mlp_full = attn_full[5].astype(jnp.float32)
    inputs = tokens.astype(jnp.float32)
    normed = rms_norm(inputs, attn_full[0].astype(jnp.float32)).astype(jnp.bfloat16)
    query_raw = plain_dot(normed, attn_full[1]).reshape(tok_count, HEADS, HEAD_DIM)
    key_raw = plain_dot(normed, attn_full[2]).reshape(tok_count, KV_HEADS, HEAD_DIM)
    value_own = plain_dot(normed, attn_full[3]).astype(jnp.bfloat16)
    queries = rotate(query_raw, cos_heads, sin_heads).astype(jnp.bfloat16)
    key_own = (
        rotate(key_raw, cos_heads, sin_heads)
        .astype(jnp.bfloat16)
        .reshape(tok_count, KV_HEADS * HEAD_DIM)
    )
    key_all, value_all = (
        lax.all_gather(key_own, "seq", axis=0, tiled=True),
        lax.all_gather(value_own, "seq", axis=0, tiled=True),
    )
    query_heads = queries.reshape(tok_count, KV_HEADS, group_size, HEAD_DIM).transpose(1, 0, 2, 3)
    key_heads = key_all.reshape(length, KV_HEADS, HEAD_DIM).transpose(1, 0, 2)
    value_heads = value_all.reshape(length, KV_HEADS, HEAD_DIM).transpose(1, 0, 2)
    head_outs, log_totals = lax.map(
        lambda head_items: attend_forward(
            head_items[0], head_items[1], head_items[2], allowed, score_scale
        ),
        (query_heads, key_heads, value_heads),
    )
    attn_in = (
        head_outs.transpose(1, 0, 2, 3).reshape(tok_count, HEADS * HEAD_DIM).astype(jnp.bfloat16)
    )
    middle = inputs + plain_dot(attn_in, attn_full[4])
    normed_mlp = rms_norm(middle, gain_mlp_full).astype(jnp.bfloat16)
    slices = (
        lax.all_gather(w_gate, "dp", axis=1, tiled=True),
        lax.all_gather(w_up, "dp", axis=1, tiled=True),
        lax.all_gather(w_down, "dp", axis=0, tiled=True),
    )
    rows_all, cot_all = (
        lax.all_gather(normed_mlp, "seq", axis=0, tiled=True),
        lax.all_gather(cotangent, "seq", axis=0, tiled=True),
    )
    gate_pre = plain_dot(rows_all, slices[0])
    up_pre = plain_dot(rows_all, slices[1])
    hidden = swiglu(gate_pre, up_pre).astype(jnp.bfloat16)
    down_part = plain_dot(hidden, slices[2])
    down_own = lax.psum_scatter(
        down_part.astype(jnp.bfloat16), "seq", scatter_dimension=0, tiled=True
    ).astype(jnp.float32)
    block_out = (middle + down_own).astype(jnp.bfloat16)
    grad_w_down = matmul_tn(hidden, cot_all)
    grad_hidden = matmul_nt(cot_all, slices[2])
    swiglu_value, swiglu_pull = jax.vjp(swiglu, gate_pre, up_pre)
    grad_gate, grad_up = swiglu_pull(grad_hidden)
    grad_gate = grad_gate.astype(jnp.bfloat16)
    grad_up = grad_up.astype(jnp.bfloat16)
    gate_grad_rows = matmul_tn(grad_gate, rows_all)
    up_grad_rows = matmul_tn(grad_up, rows_all)
    normed_part = matmul_nt(grad_gate, slices[0]) + matmul_nt(grad_up, slices[1])
    grad_normed_mlp = lax.psum_scatter(
        normed_part.astype(jnp.bfloat16), "seq", scatter_dimension=0, tiled=True
    ).astype(jnp.float32)
    mlp_grads = (
        lax.psum_scatter(
            gate_grad_rows.astype(jnp.bfloat16), "dp", scatter_dimension=0, tiled=True
        ).astype(jnp.float32),
        lax.psum_scatter(
            up_grad_rows.astype(jnp.bfloat16), "dp", scatter_dimension=0, tiled=True
        ).astype(jnp.float32),
        lax.psum_scatter(
            grad_w_down.astype(jnp.bfloat16), "dp", scatter_dimension=0, tiled=True
        ).astype(jnp.float32),
    )
    norm_mlp_value, norm_mlp_pull = jax.vjp(rms_norm, middle, gain_mlp_full)
    grad_middle_norm, grad_gain_mlp = norm_mlp_pull(grad_normed_mlp)
    grad_middle = cotangent.astype(jnp.float32) + grad_middle_norm
    attn_back = (
        lax.all_gather(gain_attn, ("dp", "seq"), axis=0, tiled=True),
        lax.all_gather(w_query, ("dp", "seq"), axis=0, tiled=True),
        lax.all_gather(w_key, ("dp", "seq"), axis=0, tiled=True),
        lax.all_gather(w_value, ("dp", "seq"), axis=0, tiled=True),
        lax.all_gather(w_out, ("dp", "seq"), axis=0, tiled=True),
    )
    grad_attn = grad_middle.astype(jnp.bfloat16)
    grad_w_out = matmul_tn(attn_in, grad_attn)
    grad_attn_in = matmul_nt(grad_attn, attn_back[4]).astype(jnp.bfloat16)
    grad_heads = grad_attn_in.reshape(tok_count, KV_HEADS, group_size, HEAD_DIM).transpose(
        1, 0, 2, 3
    )
    grad_query, grad_key, grad_value = lax.map(
        lambda head_items: attend_backward(
            head_items[0],
            head_items[1],
            head_items[2],
            head_items[3],
            head_items[4],
            allowed,
            score_scale,
        ),
        (query_heads, key_heads, value_heads, log_totals, grad_heads),
    )
    key_grad_all = grad_key.transpose(1, 0, 2).reshape(length, KV_HEADS * HEAD_DIM)
    value_grad_all = grad_value.transpose(1, 0, 2).reshape(length, KV_HEADS * HEAD_DIM)
    key_grad, value_grad = (
        lax.psum_scatter(
            key_grad_all.astype(jnp.bfloat16), "seq", scatter_dimension=0, tiled=True
        ).astype(jnp.float32),
        lax.psum_scatter(
            value_grad_all.astype(jnp.bfloat16), "seq", scatter_dimension=0, tiled=True
        ).astype(jnp.float32),
    )
    grad_key_raw = (
        rotate_back(key_grad.reshape(tok_count, KV_HEADS, HEAD_DIM), cos_heads, sin_heads)
        .reshape(tok_count, KV_HEADS * HEAD_DIM)
        .astype(jnp.bfloat16)
    )
    query_grad_rows = grad_query.transpose(1, 0, 2, 3).reshape(tok_count, HEADS, HEAD_DIM)
    grad_query_raw = (
        rotate_back(query_grad_rows, cos_heads, sin_heads)
        .reshape(tok_count, HEADS * HEAD_DIM)
        .astype(jnp.bfloat16)
    )
    grad_value_raw = value_grad.astype(jnp.bfloat16)
    grad_w_query = matmul_tn(normed, grad_query_raw)
    grad_w_key = matmul_tn(normed, grad_key_raw)
    grad_w_value = matmul_tn(normed, grad_value_raw)
    grad_normed = (
        matmul_nt(grad_query_raw, attn_back[1])
        + matmul_nt(grad_key_raw, attn_back[2])
        + matmul_nt(grad_value_raw, attn_back[3])
    )
    norm_attn_value, norm_attn_pull = jax.vjp(rms_norm, inputs, attn_back[0].astype(jnp.float32))
    grad_input_norm, grad_gain_attn = norm_attn_pull(grad_normed)
    attn_grads = (
        lax.psum_scatter(grad_gain_attn, ("dp", "seq"), scatter_dimension=0, tiled=True),
        lax.psum_scatter(grad_w_query, ("dp", "seq"), scatter_dimension=0, tiled=True),
        lax.psum_scatter(grad_w_key, ("dp", "seq"), scatter_dimension=0, tiled=True),
        lax.psum_scatter(grad_w_value, ("dp", "seq"), scatter_dimension=0, tiled=True),
        lax.psum_scatter(grad_w_out, ("dp", "seq"), scatter_dimension=0, tiled=True),
        lax.psum_scatter(grad_gain_mlp, ("dp", "seq"), scatter_dimension=0, tiled=True),
    )
    input_grad = grad_middle + grad_input_norm
    return (
        block_out,
        input_grad,
        attn_grads[0],
        attn_grads[1],
        attn_grads[2],
        attn_grads[3],
        attn_grads[4],
        attn_grads[5],
        mlp_grads[0].T,
        mlp_grads[1].T,
        mlp_grads[2],
    )


def solution(mesh):
    return jax.shard_map(
        local,
        mesh=mesh,
        in_specs=(
            P(("dp", "seq"), None),
            P(("dp", "seq")),
            P(("dp", "seq"), None),
            P(("dp", "seq"), None),
            P(("dp", "seq"), None),
            P(("dp", "seq"), None),
            P(("dp", "seq")),
            P(None, ("dp", "seq")),
            P(None, ("dp", "seq")),
            P(("dp", "seq"), None),
            P("dp", None),
            P(("dp", "seq"), None),
        ),
        out_specs=(
            P(("dp", "seq"), None),
            P(("dp", "seq"), None),
            P(("dp", "seq")),
            P(("dp", "seq"), None),
            P(("dp", "seq"), None),
            P(("dp", "seq"), None),
            P(("dp", "seq"), None),
            P(("dp", "seq")),
            P(None, ("dp", "seq")),
            P(None, ("dp", "seq")),
            P(("dp", "seq"), None),
        ),
        check_vma=False,
    )
```

profile of v0, /device:TPU:1, one launch (start us, length us, event | category | flops | bytes accessed | tf_op | source)
XLA Modules:
  0.0 1759.5 jit_solution(12673869527432979326)
XLA Ops:
  10.4 40.8 %all-reduce.5 = (bf16[2048]{0:T(1024)(128)(2,1)S(1)}, bf16[2048]{0:T(1024)(128)(2,1)S(1)}) all-reduce(bf16[2048]{0:T(1024)(128)(2,1)S(1)} %dynamic-update-slice, bf16[2048]{0:T(1024)(128)(2,1)S(1)} %dynamic-update-slice.1), channel_id=1, replica_groups=mesh['dp'=2,'seq'=16] {'dp','seq'}, use_global_device_ids=true, to_apply=%add | all-reduce | flops 4096 | bytes 16384
  52.6 14.6 all-gather.18.cloned.1.call-done
  67.1 2.4 convolution_convert_fusion.5
  72.0 50.7 %all-gather.14.cloned.1.call-done = bf16[2048,256]{1,0:T(8,128)(2,1)} async-done(((bf16[64,256]{1,0:T(8,128)(2,1)}), bf16[2048,256]{1,0:T(8,128)(2,1)}) %all-gather.14.cloned.1.call-update) | async-done | bytes 1048592 | tf_op jit(solution)/shard_map/all_gather | solution.py:144
  127.0 35.3 %all-gather.20.cloned.1.call-done = bf16[2048,256]{1,0:T(8,128)(2,1)} async-done(((bf16[128,256]{1,0:T(8,128)(2,1)}), bf16[2048,256]{1,0:T(8,128)(2,1)}) %all-gather.20.cloned.1.call-update) | async-done | bytes 1048592 | tf_op jit(solution)/shard_map/all_gather | solution.py:163
  163.8 77.6 %all-gather.12.cloned.1.call-done = bf16[2048,2048]{1,0:T(8,128)(2,1)} async-done(((bf16[64,2048]{1,0:T(8,128)(2,1)}), bf16[2048,2048]{1,0:T(8,128)(2,1)}) %all-gather.12.cloned.1.call-update) | async-done | bytes 8388624 | tf_op jit(solution)/shard_map/all_gather | solution.py:143
  241.5 6.8 fusion.90
  248.6 30.9 %all-gather.16.cloned.1.call-done = bf16[2048,256]{0,1:T(8,128)(2,1)} async-done(((bf16[128,256]{0,1:T(8,128)(2,1)}), bf16[2048,256]{0,1:T(8,128)(2,1)}) %all-gather.16.cloned.1.call-update) | async-done | bytes 1048592 | tf_op jit(solution)/shard_map/all_gather | solution.py:162
  279.5 32.4 %while.30 = (s32[]{:T(128)}, bf16[4,128,8,64]{1,3,2,0:T(8,128)(2,1)S(1)}, f32[4,128,8]{1,2,0:T(8,128)}, bf16[4,128,8,64]{1,3,2,0:T(8,128)(2,1)S(1)}, bf16[4,2048...) while((s32[]{:T(128)}, ...), condition=%wide.region_5.6_spmd.clone.clone, body=%wide.region_2.5_spmd.clone.sunk.clone | while | flops 562822144 | bytes 27176040 | solution.py:168
  279.9 2.6 fusion.170
  284.6 2.3 fusion.172
  288.0 2.5 fusion.170
  292.7 2.3 fusion.172
  296.1 2.5 fusion.170
  300.8 2.3 fusion.172
  304.2 2.5 fusion.170
  308.9 2.3 fusion.172
  311.9 47.4 %all-gather.22.cloned.1.call-done = bf16[2048,2048]{1,0:T(8,128)(2,1)} async-done(((bf16[64,2048]{1,0:T(8,128)(2,1)}), bf16[2048,2048]{1,0:T(8,128)(2,1)}) %all-gather.22.cloned.1.call-update) | async-done | bytes 8388624 | tf_op jit(solution)/shard_map/all_gather | solution.py:146
  359.3 4.7 multiply_reduce_fusion.1
  367.4 17.4 all-gather.28.cloned.1.call-done
  384.8 78.1 %all-gather.24.cloned.1.call-done = bf16[2048,2048]{1,0:T(8,128)(2,1)} async-done(((bf16[128,2048]{1,0:T(8,128)(2,1)}), bf16[2048,2048]{1,0:T(8,128)(2,1)}) %all-gather.24.cloned.1.call-update) | async-done | bytes 8388624 | tf_op jit(solution)/shard_map/all_gather | solution.py:185
  462.9 8.5 fusion.93
  471.4 16.6 all-gather.26.cloned.1.call-done
  488.0 8.5 fusion.92
  496.5 18.7 %all-gather.30.cloned.1.call-done = bf16[352,2048]{1,0:T(8,128)(2,1)} async-done(((bf16[176,2048]{1,0:T(8,128)(2,1)}), bf16[352,2048]{1,0:T(8,128)(2,1)}) %all-gather.30.cloned.1.call-update) | async-done | bytes 1441808 | tf_op jit(solution)/shard_map/all_gather | solution.py:182
  515.2 77.5 %all-gather.32.cloned.1.call-done = bf16[2048,2048]{1,0:T(8,128)(2,1)} async-done(((bf16[128,2048]{1,0:T(8,128)(2,1)}), bf16[2048,2048]{1,0:T(8,128)(2,1)}) %all-gather.32.cloned.1.call-update) | async-done | bytes 8388624 | tf_op jit(solution)/shard_map/all_gather | solution.py:186
  592.7 10.8 multiply_convert_fusion.1
  603.5 8.5 fusion.94
  612.0 10.3 add_convert_fusion
  623.7 8.2 convolution_convert_fusion
  632.0 93.0 %reduce-scatter.18.cloned.1.call-done = bf16[128,2048]{1,0:T(8,128)(2,1)} async-done(((bf16[2048,2048]{1,0:T(8,128)(2,1)}), bf16[128,2048]{1,0:T(8,128)(2,1)}) %reduce-scatter.18.cloned.1.call-update) | async-done | bytes 524304 | tf_op jit(solution)/shard_map/reduce_scatter | solution.py:205
  727.0 106.6 %reduce-scatter.16.cloned.1.call-done = bf16[128,2048]{1,0:T(8,128)(2,1)} async-done(((bf16[2048,2048]{1,0:T(8,128)(2,1)}), bf16[128,2048]{1,0:T(8,128)(2,1)}) %reduce-scatter.16.cloned.1.call-update) | async-done | bytes 524304 | tf_op jit(solution)/shard_map/reduce_scatter | solution.py:192
  833.6 2.5 fusion.72
  836.1 6.3 convolution_convert_fusion.4
  842.7 63.8 %while.31 = (s32[]{:T(128)}, f32[4,128,8,64]{1,3,2,0:T(8,128)}, bf16[4,2048,64]{1,2,0:T(8,128)(2,1)}, bf16[4,2048,64]{1,2,0:T(8,128)(2,1)}, bf16[4,128,8,64]{1,3...) while((s32[]{:T(128)}, f32[4,128,8,64]{1,3,2,0:T(8,128)}, ...), condition=%wide.region_12.13_spmd.clone.clone, body=%wide.region_10.12_spmd.clone.sunk.clone | while | flops 1374616576 | bytes 83405040 | solution.py:235
  848.5 3.9 multiply_reduce_fusion.4
  852.5 2.4 multiply_convert_fusion.6
  864.5 3.9 multiply_reduce_fusion.4
  868.4 2.4 multiply_convert_fusion.6
  880.4 3.9 multiply_reduce_fusion.4
  884.3 2.4 multiply_convert_fusion.6
  896.3 3.9 multiply_reduce_fusion.4
  900.2 2.4 multiply_convert_fusion.6
  908.9 2.3 copy.45
  911.3 8.2 convolution_convert_fusion.1
  919.6 7.9 convolution_convert_fusion.2
  927.7 8.1 convolution_convert_fusion.3
  935.8 28.4 %reduce-scatter.36.cloned.1.call-done = bf16[128,256]{1,0:T(8,128)(2,1)} async-done(((bf16[2048,256]{1,0:T(8,128)(2,1)}), bf16[128,256]{1,0:T(8,128)(2,1)}) %reduce-scatter.36.cloned.1.call-update) | async-done | bytes 65552
  964.3 2.7 fusion.81
  967.1 57.6 %reduce-scatter.34.cloned.1.call-done = bf16[128,256]{1,0:T(8,128)(2,1)} async-done(((bf16[2048,256]{1,0:T(8,128)(2,1)}), bf16[128,256]{1,0:T(8,128)(2,1)}) %reduce-scatter.34.cloned.1.call-update) | async-done | bytes 65552
  1027.7 8.4 fusion.76
  1037.5 8.2 fusion.85
  1045.7 6.5 reduce-scatter.32.cloned.1.call-done
  1052.3 2.4 convert_element_type.164
  1054.7 24.5 %reduce-scatter.30.cloned.1.call-done = bf16[176,2048]{1,0:T(8,128)(2,1)} async-done(((bf16[352,2048]{1,0:T(8,128)(2,1)}), bf16[176,2048]{1,0:T(8,128)(2,1)}) %reduce-scatter.30.cloned.1.call-update) | async-done | bytes 720912 | tf_op jit(solution)/shard_map/reduce_scatter | solution.py:212
  1079.1 2.4 convert_bitcast_fusion
  1081.5 25.0 %reduce-scatter.28.cloned.1.call-done = bf16[176,2048]{1,0:T(8,128)(2,1)} async-done(((bf16[352,2048]{1,0:T(8,128)(2,1)}), bf16[176,2048]{1,0:T(8,128)(2,1)}) %reduce-scatter.28.cloned.1.call-update) | async-done | bytes 720912 | tf_op jit(solution)/shard_map/reduce_scatter | solution.py:209
  1106.5 2.5 convert_bitcast_fusion.1
  1109.0 6.3 fusion.95
  1116.5 39.7 %all-reduce.4 = (f32[2048]{0:T(1024)S(1)}, f32[2048]{0:T(1024)S(1)}) all-reduce(f32[2048]{0:T(1024)S(1)} %get-tuple-element.162, f32[2048]{0:T(1024)S(1)} %copy-done.31), channel_id=6, replica_groups=mesh['dp'=2,'seq'=16] {'dp','seq'}, use_global_device_ids=true, to_apply=%region_17.18.clone | all-reduce | flops 4096 | bytes 32768
  1158.7 82.4 %reduce-scatter.24.cloned.1.call-done = f32[64,256]{1,0:T(8,128)} async-done(((f32[2048,256]{1,0:T(8,128)}), f32[64,256]{1,0:T(8,128)}) %reduce-scatter.24.cloned.1.call-update) | async-done | bytes 65552 | tf_op jit(solution)/shard_map/reduce_scatter | solution.py:283
  1241.0 135.4 %reduce-scatter.22.cloned.1.call-done = f32[64,256]{1,0:T(8,128)} async-done(((f32[2048,256]{1,0:T(8,128)}), f32[64,256]{1,0:T(8,128)}) %reduce-scatter.22.cloned.1.call-update) | async-done | bytes 65552 | tf_op jit(solution)/shard_map/reduce_scatter | solution.py:282
  1376.4 188.5 %reduce-scatter.26.cloned.1.call-done = f32[64,2048]{1,0:T(8,128)} async-done(((f32[2048,2048]{1,0:T(8,128)}), f32[64,2048]{1,0:T(8,128)}) %reduce-scatter.26.cloned.1.call-update) | async-done | bytes 524304 | tf_op jit(solution)/shard_map/reduce_scatter | solution.py:284
  1564.9 187.5 %reduce-scatter.20.cloned.1.call-done = f32[64,2048]{1,0:T(8,128)} async-done(((f32[2048,2048]{1,0:T(8,128)}), f32[64,2048]{1,0:T(8,128)}) %reduce-scatter.20.cloned.1.call-update) | async-done | bytes 524304 | tf_op jit(solution)/shard_map/reduce_scatter | solution.py:281
  (228 shorter events, 81.3 us)
Async XLA Ops:
  7.2 234.3 %copy-start = (bf16[128,2048]{1,0:T(8,128)(2,1)S(1)}, bf16[128,2048]{1,0:T(8,128)(2,1)}, u32[]{:S(2)}) copy-start(bf16[128,2048]{1,0:T(8,128)(2,1)} %param.16) | copy-start | bytes 1572868
  7.2 59.9 %all-gather.18.cloned.1.call-start = ((), (), s32[]{:S(2)}) async-start(), calls=%async_computation.14 | async-start | bytes 1081344 | tf_op jit(solution)/shard_map/all_gather | solution.py:145
  7.9 114.8 %all-gather.14.cloned.1.call-start = ((), (), s32[]{:S(2)}) async-start(), calls=%async_computation.12 | async-start | bytes 1081344 | tf_op jit(solution)/shard_map/all_gather | solution.py:144
  8.7 153.7 %all-gather.20.cloned.1.call-start = ((), (), s32[]{:S(2)}) async-start(), calls=%async_computation.15 | async-start | bytes 1114112 | tf_op jit(solution)/shard_map/all_gather | solution.py:163
  51.3 197.0 %copy-start.20 = (f32[2048]{0:T(1024)}, f32[2048]{0:T(1024)S(1)}, u32[]{:S(2)}) copy-start(f32[2048]{0:T(1024)S(1)} %convert_element_type.131) | copy-start | bytes 24580
  52.5 19.2 %copy-start.37 = (f32[128]{0:T(128)}, f32[128]{0:T(128)S(1)}, u32[]{:S(2)}) copy-start(f32[128]{0:T(128)S(1)} %fusion.74) | copy-start | bytes 1540
  52.6 195.8 %copy-start.32 = (f32[128]{0:T(128)}, f32[128]{0:T(128)S(1)}, u32[]{:S(2)}) copy-start(f32[128]{0:T(128)S(1)} %fusion.79) | copy-start | bytes 1540
  69.5 171.9 %all-gather.12.cloned.1.call-start = ((), (), s32[]{:S(2)}) async-start(), calls=%async_computation.11 | async-start | bytes 8650752 | tf_op jit(solution)/shard_map/all_gather | solution.py:143
  70.1 209.4 %all-gather.16.cloned.1.call-start = ((), (), s32[]{:S(2)}) async-start(), calls=%async_computation.13 | async-start | bytes 1114112 | tf_op jit(solution)/shard_map/all_gather | solution.py:162
  72.0 176.6 %copy-start.22 = (f32[128,32]{0,1:T(8,128)}, f32[128,32]{0,1:T(8,128)S(1)}, u32[]{:S(2)}) copy-start(f32[128,32]{0,1:T(8,128)S(1)} %get-tuple-element.227) | copy-start | bytes 49156
  72.0 176.6 %copy-start.24 = (f32[128,32]{0,1:T(8,128)}, f32[128,32]{0,1:T(8,128)S(1)}, u32[]{:S(2)}) copy-start(f32[128,32]{0,1:T(8,128)S(1)} %get-tuple-element.228) | copy-start | bytes 49156
  124.6 154.8 %copy-start.19 = (s32[1,2048]{1,0:T(1,128)S(1)}, s32[1,2048]{1,0:T(1,128)}, u32[]{:S(2)}) copy-start(s32[1,2048]{1,0:T(1,128)} %param.26) | copy-start | bytes 24580
  125.3 234.0 %all-gather.22.cloned.1.call-start = ((), (), s32[]{:S(2)}) async-start(), calls=%async_computation.16 | async-start | bytes 8650752 | tf_op jit(solution)/shard_map/all_gather | solution.py:146
  125.9 258.9 %all-gather.28.cloned.1.call-start = ((), (), s32[]{:S(2)}) async-start(), calls=%async_computation.19 | async-start | bytes 2162688 | tf_op jit(solution)/shard_map/all_gather | solution.py:181
  126.7 336.2 %all-gather.24.cloned.1.call-start = ((), (), s32[]{:S(2)}) async-start(), calls=%async_computation.17 | async-start | bytes 8912896 | tf_op jit(solution)/shard_map/all_gather | solution.py:185
  311.9 47.4 %copy-start.6 = (bf16[4,2048,64]{1,2,0:T(8,128)(2,1)}, bf16[4,2048,64]{1,2,0:T(8,128)(2,1)S(1)}, u32[]{:S(2)}) copy-start(bf16[4,2048,64]{1,2,0:T(8,128)(2,1)S(1)} %get-tuple-element.520) | copy-start | bytes 3145732
  311.9 52.2 %copy-start.3 = (bf16[4,128,8,64]{1,3,2,0:T(8,128)(2,1)}, bf16[4,128,8,64]{1,3,2,0:T(8,128)(2,1)S(1)}, u32[]{:S(2)}) copy-start(bf16[4,128,8,64]{1,3,2,0:T(8,128)(2,1)S(1)} %get-tuple-element.513) | copy-start | bytes 1572868
  311.9 52.2 %copy-start.4 = (bf16[4,128,8,64]{1,3,2,0:T(8,128)(2,1)}, bf16[4,128,8,64]{1,3,2,0:T(8,128)(2,1)S(1)}, u32[]{:S(2)}) copy-start(bf16[4,128,8,64]{1,3,2,0:T(8,128)(2,1)S(1)} %get-tuple-element.103) | copy-start | bytes 1572868
  311.9 52.2 %copy-start.27 = (s32[128]{0:T(128)}, s32[128]{0:T(128)S(1)}, u32[]{:S(2)}) copy-start(s32[128]{0:T(128)S(1)} %get-tuple-element.562) | copy-start | bytes 1540
  311.9 52.2 %copy-start.29 = (s32[128]{0:T(128)}, s32[128]{0:T(128)S(1)}, u32[]{:S(2)}) copy-start(s32[128]{0:T(128)S(1)} %get-tuple-element.563) | copy-start | bytes 1540
  364.1 107.3 %copy-start.35 = (f32[128]{0:T(128)}, f32[128]{0:T(128)S(1)}, u32[]{:S(2)}) copy-start(f32[128]{0:T(128)S(1)} %get-tuple-element.229) | copy-start | bytes 1540
  364.1 360.9 %copy-start.34 = (f32[128]{0:T(128)}, f32[128]{0:T(128)S(1)}, u32[]{:S(2)}) copy-start(f32[128]{0:T(128)S(1)} %fusion.80) | copy-start | bytes 1540
  365.1 122.9 %all-gather.26.cloned.1.call-start = ((), (), s32[]{:S(2)}) async-start(), calls=%async_computation.18 | async-start | bytes 2162688 | tf_op jit(solution)/shard_map/all_gather | solution.py:180
  365.8 149.4 %all-gather.30.cloned.1.call-start = ((), (), s32[]{:S(2)}) async-start(), calls=%async_computation.20 | async-start | bytes 2162688 | tf_op jit(solution)/shard_map/all_gather | solution.py:182
  366.4 226.3 %all-gather.32.cloned.1.call-start = ((), (), s32[]{:S(2)}) async-start(), calls=%async_computation.22 | async-start | bytes 8912896 | tf_op jit(solution)/shard_map/all_gather | solution.py:186
  367.2 357.9 %reduce-scatter.18.cloned.1.call-start = ((), (), s32[]{:S(2)}) async-start(), calls=%async_computation.23 | async-start | bytes 8912896 | tf_op jit(solution)/shard_map/reduce_scatter | solution.py:205
  496.5 107.0 %copy-start.11 = (bf16[2048,352]{0,1:T(8,128)(2,1)S(1)}, bf16[2048,352]{0,1:T(8,128)(2,1)}, u32[]{:S(2)}) copy-start(bf16[2048,352]{0,1:T(8,128)(2,1)} %all-gather.26.cloned.1.call-done) | copy-start | bytes 4325380
  603.5 8.5 copy-start.9
  603.5 8.6 copy-start.7
  603.5 8.5 copy-start.10
  622.3 211.3 %reduce-scatter.16.cloned.1.call-start = ((), (), s32[]{:S(2)}) async-start(), calls=%async_computation.21 | async-start | bytes 8912896 | tf_op jit(solution)/shard_map/reduce_scatter | solution.py:192
  631.9 95.1 %copy-start.36 = (f32[128]{0:T(128)S(1)}, f32[128]{0:T(128)}, u32[]{:S(2)}) copy-start(f32[128]{0:T(128)} %copy-done.35) | copy-start | bytes 1540
  631.9 332.3 %reduce-scatter.36.cloned.1.call-start = ((), (), s32[]{:S(2)}) async-start(), calls=%async_computation.32 | async-start | bytes 1114112
  632.0 210.7 %copy-start.2 = (bf16[4,2048,64]{1,2,0:T(8,128)(2,1)S(1)}, bf16[4,2048,64]{1,2,0:T(8,128)(2,1)}, u32[]{:S(2)}) copy-start(bf16[4,2048,64]{1,2,0:T(8,128)(2,1)} %get-tuple-element.512) | copy-start | bytes 3145732
  632.0 210.7 %copy-start.28 = (s32[128]{0:T(128)S(1)}, s32[128]{0:T(128)}, u32[]{:S(2)}) copy-start(s32[128]{0:T(128)} %copy-done.27) | copy-start | bytes 1540
  632.0 210.7 %copy-start.30 = (s32[128]{0:T(128)S(1)}, s32[128]{0:T(128)}, u32[]{:S(2)}) copy-start(s32[128]{0:T(128)} %copy-done.29) | copy-start | bytes 1540
  842.9 3.4 copy-start.14
  848.5 3.9 copy-start.15
  858.8 3.4 copy-start.14
  864.5 3.9 copy-start.15
  874.7 3.4 copy-start.14
  880.4 3.9 copy-start.15
  890.6 3.4 copy-start.14
  896.3 3.9 copy-start.15
  908.8 115.8 %reduce-scatter.34.cloned.1.call-start = ((), (), s32[]{:S(2)}) async-start(), calls=%async_computation.31 | async-start | bytes 1114112
  911.2 8.4 copy-start.8
  911.2 141.1 %reduce-scatter.32.cloned.1.call-start = ((), (), s32[]{:S(2)}) async-start(), calls=%async_computation.30 | async-start | bytes 2162688 | tf_op jit(solution)/shard_map/reduce_scatter | solution.py:215
  919.5 159.6 %reduce-scatter.30.cloned.1.call-start = ((), (), s32[]{:S(2)}) async-start(), calls=%async_computation.29 | async-start | bytes 2162688 | tf_op jit(solution)/shard_map/reduce_scatter | solution.py:212
  927.6 36.7 %copy-start.1 = (bf16[128,2048]{1,0:T(8,128)(2,1)S(1)}, bf16[128,2048]{1,0:T(8,128)(2,1)}, u32[]{:S(2)}) copy-start(bf16[128,2048]{1,0:T(8,128)(2,1)} %param.16) | copy-start | bytes 1572868
  927.6 36.7 %copy-start.21 = (f32[2048]{0:T(1024)S(1)}, f32[2048]{0:T(1024)}, u32[]{:S(2)}) copy-start(f32[2048]{0:T(1024)} %copy-done.20) | copy-start | bytes 24580
  927.6 36.7 %copy-start.33 = (f32[128]{0:T(128)S(1)}, f32[128]{0:T(128)}, u32[]{:S(2)}) copy-start(f32[128]{0:T(128)} %copy-done.32) | copy-start | bytes 1540
  927.6 98.0 %copy-start.23 = (f32[128,32]{0,1:T(8,128)S(1)}, f32[128,32]{0,1:T(8,128)}, u32[]{:S(2)}) copy-start(f32[128,32]{0,1:T(8,128)} %copy-done.22) | copy-start | bytes 49156
  927.6 98.0 %copy-start.25 = (f32[128,32]{0,1:T(8,128)S(1)}, f32[128,32]{0,1:T(8,128)}, u32[]{:S(2)}) copy-start(f32[128,32]{0,1:T(8,128)} %copy-done.24) | copy-start | bytes 49156
  927.6 178.9 %reduce-scatter.28.cloned.1.call-start = ((), (), s32[]{:S(2)}) async-start(), calls=%async_computation.28 | async-start | bytes 2162688 | tf_op jit(solution)/shard_map/reduce_scatter | solution.py:209
  935.8 91.9 %copy-start.5 = (bf16[4,128,8,64]{1,3,2,0:T(8,128)(2,1)S(1)}, bf16[4,128,8,64]{1,3,2,0:T(8,128)(2,1)}, u32[]{:S(2)}) copy-start(bf16[4,128,8,64]{1,3,2,0:T(8,128)(2,1)} %copy-done.4) | copy-start | bytes 1572868
  935.8 305.2 %reduce-scatter.24.cloned.1.call-start = ((), (), s32[]{:S(2)}) async-start(), calls=%async_computation.26 | async-start | bytes 2162688 | tf_op jit(solution)/shard_map/reduce_scatter | solution.py:283
  967.0 409.4 %reduce-scatter.22.cloned.1.call-start = ((), (), s32[]{:S(2)}) async-start(), calls=%async_computation.25 | async-start | bytes 2162688 | tf_op jit(solution)/shard_map/reduce_scatter | solution.py:282
  1027.6 537.3 %reduce-scatter.26.cloned.1.call-start = ((), (), s32[]{:S(2)}) async-start(), calls=%async_computation.27 | async-start | bytes 17301504 | tf_op jit(solution)/shard_map/reduce_scatter | solution.py:284
  1036.1 716.4 %reduce-scatter.20.cloned.1.call-start = ((), (), s32[]{:S(2)}) async-start(), calls=%async_computation.24 | async-start | bytes 17301504 | tf_op jit(solution)/shard_map/reduce_scatter | solution.py:281
  1045.7 69.6 %copy-start.12 = (bf16[2048,256]{1,0:T(8,128)(2,1)S(1)}, bf16[2048,256]{1,0:T(8,128)(2,1)}, u32[]{:S(2)}) copy-start(bf16[2048,256]{1,0:T(8,128)(2,1)} %all-gather.14.cloned.1.call-done) | copy-start | bytes 3145732
  1054.7 61.1 %copy-start.26 = (bf16[128,256]{1,0:T(8,128)(2,1)S(1)}, bf16[128,256]{1,0:T(8,128)(2,1)}, u32[]{:S(2)}) copy-start(bf16[128,256]{1,0:T(8,128)(2,1)} %reduce-scatter.36.cloned.1.call-done) | copy-start | bytes 196612
  1106.5 9.3 copy-start.18
  1109.0 7.5 copy-start.31
  1109.0 48.4 %copy-start.38 = (f32[128]{0:T(128)S(1)}, f32[128]{0:T(128)}, u32[]{:S(2)}) copy-start(f32[128]{0:T(128)} %copy-done.37) | copy-start | bytes 1540
  (10 other events, 20.8 us)
Sparse Core Ops, SparseCore 0:
  10.9 56.2 all-gather.17
  70.0 52.6 all-gather.13
  125.4 36.8 all-gather.19
  165.0 76.3 all-gather.11
  244.1 35.3 all-gather.15
  282.2 77.0 all-gather.21
  360.8 23.9 all-gather.27
  387.5 75.3 all-gather.23
  464.4 23.5 all-gather.25
  489.4 25.7 all-gather.29
  517.4 75.3 all-gather.31
  622.4 102.5 reduce-scatter.17
  729.1 104.4 reduce-scatter.15
  909.0 55.2 reduce-scatter.35
  968.2 56.4 reduce-scatter.33
  1026.7 25.5 reduce-scatter.31
  1054.5 24.6 reduce-scatter.29
  1081.8 24.6 reduce-scatter.27
  1109.4 131.5 reduce-scatter.23
  1243.7 132.6 reduce-scatter.21
  1379.4 185.4 reduce-scatter.25
  1567.9 184.4 reduce-scatter.19
where the time goes:
time: 1760 us
  waiting for transfers between devices  1410 us (80%)
  matrix products  198 us (11%)
  blocking collectives  80.6 us (5%)
  other arithmetic  41.7 us (2%)
    reduce_scatter x1, waiting for transfers between devices, local(): lax.psum_scatter(grad_w_out, ('dp', 'seq'), scatter_dimension=0, tiled=True)  188 us
    reduce_scatter x1, waiting for transfers between devices, local(): lax.psum_scatter(grad_w_query, ('dp', 'seq'), scatter_dimension=0, tiled=...  187 us
    reduce_scatter x1, waiting for transfers between devices, local(): lax.psum_scatter(grad_w_key, ('dp', 'seq'), scatter_dimension=0, tiled=True)  135 us
    reduce_scatter x1, waiting for transfers between devices, local(): lax.psum_scatter(down_part.astype(jnp.bfloat16), 'seq', scatter_dimension...  107 us
    reduce_scatter x1, waiting for transfers between devices, local(): lax.psum_scatter(normed_part.astype(jnp.bfloat16), 'seq', scatter_dimensi...  93 us
    unnamed x24, waiting for transfers between devices  91.2 us
    reduce_scatter x1, waiting for transfers between devices, local(): lax.psum_scatter(grad_w_value, ('dp', 'seq'), scatter_dimension=0, tiled=...  82.4 us
    unnamed x2, blocking collectives  80.6 us
  transfers between devices with their start and end apart: 22, of which 22 were waited for; matrix products, arithmetic and copies ran while one was open for 9% of the time, Pallas kernels for 0%

commit v1 on v0

v1 whole, which is shorter than its diff:
```python
import jax
import jax.numpy as jnp
from jax import lax
from jax.experimental import pallas as pl
from jax.experimental.pallas import tpu as pltpu
from jax.sharding import Mesh, PartitionSpec as P

HEADS = 32
KV_HEADS = 4
HEAD_DIM = 64
GROUP = HEADS // KV_HEADS
NORM_EPS = 1e-05
MASKED = -1e30
AXES = ("dh", "dl", "zh", "zl", "x", "c")
T = ("x", "c")
Z = ("zh", "zl")
DP = ("dh", "dl")
CUBE = ("dl", "zl", "x", "c")
REST = ("dh", "zh")
BF = jnp.bfloat16
F32 = jnp.float32


def nn(a, b):
    return jnp.dot(a, b, preferred_element_type=F32)


def nt(a, b):
    return lax.dot_general(a, b, (((1,), (1,)), ((), ())), preferred_element_type=F32)


def tn(a, b):
    return lax.dot_general(a, b, (((0,), (0,)), ((), ())), preferred_element_type=F32)


def rotate(v, cos, sin, sign):
    h = v.shape[-1] // 2
    a, b = v[..., :h], v[..., h:]
    s = sin * sign
    return jnp.concatenate([a * cos - b * s, b * cos + a * s], axis=-1)


PARTS = ((0, 768), (768, 640), (1408, 640))
MESH = pl.DeviceIdType.MESH


def place():
    return {a: lax.axis_index(a) for a in AXES}


def other(at, *flip):
    return tuple(1 - at[a] if a in flip else at[a] for a in AXES)


def greet(at, partners):
    barrier = pltpu.get_barrier_semaphore()
    for flip in partners:
        pl.semaphore_signal(barrier, inc=1, device_id=other(at, *flip), device_id_type=MESH)
    pl.semaphore_wait(barrier, len(partners))


CDIMS = ("x", "zl", "dl")
MASKS = ((), ("x",), ("zl",), ("dl",), ("x", "zl"), ("zl", "dl"), ("dl", "x"), ("x", "zl", "dl"))


def cube_index(at, mask):
    return tuple(1 - at[a] if a in mask else at[a] for a in ("dl", "zl", "x"))


def order_of(p):
    return tuple(CDIMS[(p + s) % 3] for s in range(3))


class Gather:
    def __init__(self, at, buf, ssem, rsem, csend, crecv):
        self.at, self.buf, self.ssem, self.rsem, self.csend, self.crecv = at, buf, ssem, rsem, csend, crecv
        self.rows = buf.shape[3] // 2
        self.open = []

    def block(self, mask, core, p=None):
        i = cube_index(self.at, mask)
        r = pl.ds(pl.multiple_of(core * self.rows, self.rows), self.rows)
        if p is None:
            return self.buf.at[i[0], i[1], i[2], r, :]
        lo, w = PARTS[p]
        return self.buf.at[i[0], i[1], i[2], r, lo:lo + w]

    def send(self, p, mask, dim):
        ref = self.block(mask, self.at["c"], p)
        k = MASKS.index(tuple(a for a in mask_sorted(mask + (dim,))))
        cp = pltpu.make_async_remote_copy(ref, ref, self.ssem.at[p, k], self.rsem.at[p, k],
                                          device_id=other(self.at, dim), device_id_type=MESH)
        cp.start()
        self.open.append(cp)

    def arrived(self, p, mask):
        k = MASKS.index(mask)
        ref = self.block(mask, self.at["c"], p)
        pltpu.make_async_remote_copy(ref, ref, self.ssem.at[p, k], self.rsem.at[p, k],
                                     device_id=other(self.at, "x"), device_id_type=MESH).wait_recv()

    def pass_on(self, mask):
        k = MASKS.index(mask)
        ref = self.block(mask, self.at["c"])
        cp = pltpu.make_async_remote_copy(ref, ref, self.csend.at[k], self.crecv.at[k],
                                          device_id=other(self.at, "c"), device_id_type=MESH)
        cp.start()
        self.open.append(cp)

    def sibling_arrived(self, mask):
        k = MASKS.index(mask)
        ref = self.block(mask, 1 - self.at["c"])
        pltpu.make_async_remote_copy(ref, ref, self.csend.at[k], self.crecv.at[k],
                                     device_id=other(self.at, "c"), device_id_type=MESH).wait_recv()

    def first(self):
        for p in range(3):
            self.send(p, (), order_of(p)[0])
        self.pass_on(())

    def second(self):
        for p in range(3):
            a, b, _ = order_of(p)
            self.send(p, (), b)
        for p in range(3):
            a, b, _ = order_of(p)
            self.arrived(p, (a,))
            self.send(p, (a,), b)

    def third(self):
        for p in range(3):
            a, b, c = order_of(p)
            self.send(p, (), c)
        for p in range(3):
            a, b, c = order_of(p)
            self.send(p, (a,), c)
        for p in range(3):
            a, b, c = order_of(p)
            self.arrived(p, (b,))
            self.send(p, (b,), c)
        for p in range(3):
            a, b, c = order_of(p)
            self.arrived(p, mask_sorted((a, b)))
            self.send(p, mask_sorted((a, b)), c)

    def complete(self, mask):
        for p in range(3):
            if order_of(p)[2] in mask:
                self.arrived(p, mask)

    def close(self):
        for cp in self.open:
            cp.wait_send()


def mask_sorted(mask):
    for m in MASKS:
        if set(m) == set(mask):
            return m
    raise ValueError(mask)


class Scatter:
    def __init__(self, at, full, core_in, r0, r1, r2, ssem, rsem):
        self.at, self.full, self.core_in, self.r = at, full, core_in, (r0, r1, r2)
        self.ssem, self.rsem = ssem, rsem
        self.rows = full.shape[3] // 2
        self.open = []

    def own(self, core):
        return pl.ds(pl.multiple_of(core * self.rows, self.rows), self.rows)

    def core_copy(self, p):
        lo, w = PARTS[p]
        return pltpu.make_async_remote_copy(
            self.full.at[:, :, :, self.own(1 - self.at["c"]), lo:lo + w], self.core_in.at[:, :, :, :, lo:lo + w],
            self.ssem.at[p, 3], self.rsem.at[p, 3], device_id=other(self.at, "c"), device_id_type=MESH)

    def stage_copy(self, p, s):
        lo, w = PARTS[p]
        dims = order_of(p)
        ix = []
        for a in ("dl", "zl", "x"):
            if a == dims[s]:
                ix.append(1 - self.at[a])
            elif a in dims[:s]:
                ix.append(self.at[a])
            else:
                ix.append(slice(None))
        dst = self.r[s]
        dst = dst.at[(slice(None),) * (len(dst.shape) - 1) + (slice(lo, lo + w),)]
        return pltpu.make_async_remote_copy(
            self.full.at[ix[0], ix[1], ix[2], self.own(self.at["c"]), lo:lo + w], dst,
            self.ssem.at[p, s], self.rsem.at[p, s], device_id=other(self.at, dims[s]), device_id_type=MESH)

    def start(self, cp):
        cp.start()
        self.open.append(cp)

    def blocks(self, p, s):
        dims = order_of(p)
        rest = dims[s:]
        out = []
        for m in MASKS:
            if set(m) <= set(rest):
                out.append(m)
        if rest:
            out.sort(key=lambda m: 0 if rest[0] in m else 1)
        return out

    def add_core(self, p):
        lo, w = PARTS[p]
        cp = self.core_copy(p)
        cp.wait_recv()
        self.add_loop(p, 0, None)
        self.start(self.stage_copy(p, 0))
        self.add_loop(p, 0, None, tail=True)

    def add_loop(self, p, s, src, tail=False):
        lo, w = PARTS[p]
        dims = order_of(p)
        for m in self.blocks(p, s):
            first = s < 3 and dims[s] in m
            if first == tail:
                continue
            i = cube_index(self.at, m)
            ref = self.full.at[i[0], i[1], i[2], self.own(self.at["c"]), lo:lo + w]
            if src is None:
                val = self.core_in[i[0], i[1], i[2], :, lo:lo + w]
            else:
                ix = [j for a, j in zip(("dl", "zl", "x"), i) if a in dims[s:]]
                val = src[tuple(ix) + (slice(None), slice(lo, lo + w))]
            ref[...] = (ref[...].astype(F32) + val.astype(F32)).astype(BF)

    def step(self, p, s):
        self.stage_copy(p, s).wait_recv()
        self.add_loop(p, s + 1, self.r[s])
        if s < 2:
            self.start(self.stage_copy(p, s + 1))
            self.add_loop(p, s + 1, self.r[s], tail=True)

    def finish(self, p, out):
        lo, w = PARTS[p]
        self.stage_copy(p, 2).wait_recv()
        i = cube_index(self.at, ())
        ref = self.full.at[i[0], i[1], i[2], self.own(self.at["c"]), lo:lo + w]
        out[:, lo:lo + w] = (ref[...].astype(F32) + self.r[2][:, lo:lo + w].astype(F32)).astype(out.dtype)

    def close(self):
        for cp in self.open:
            cp.wait_send()


def mlp_kernel(n2_ref, cot_ref, wg_ref, wu_ref, wd_ref, down_out, dn2_out, gwd_out, gwg_out, gwu_out,
               rows, wgu, zb, dgu, fa, fb, core_in, a0, a1, a2, b0, b1, b2,
               lsem, gs, gr, gcs, gcr, sas, sar, sbs, sbr, credit):
    at = place()
    units = wd_ref.shape[0]
    brows = n2_ref.shape[0]
    copies = [pltpu.make_async_copy(wg_ref, wgu.at[:units, :], lsem.at[0]),
              pltpu.make_async_copy(wu_ref, wgu.at[units:, :], lsem.at[1])]
    for cp in copies:
        cp.start()
    greet(at, (("c",), ("x",), ("zl",), ("dl",)))
    g = Gather(at, rows, gs, gr, gcs, gcr)
    own = pl.ds(pl.multiple_of(at["c"] * brows, brows), brows)
    rows[at["dl"], at["zl"], at["x"], own, :] = n2_ref[...]
    g.first()
    for cp in copies:
        cp.wait()

    def units_of(mask):
        i = cube_index(at, mask)
        r = rows[i[0], i[1], i[2]]
        gu = nt(wgu[...], r)
        dz = nt(wd_ref[...], cot_ref[i[0], i[1], i[2]])
        gate, up = gu[:units], gu[units:]
        sg = jax.nn.sigmoid(gate)
        sl = gate * sg
        zb[i[0], i[1], i[2]] = (sl * up).astype(BF)
        dgu[i[0], i[1], i[2], :units, :] = (dz * up * (sg * (1.0 + gate * (1.0 - sg)))).astype(BF)
        dgu[i[0], i[1], i[2], units:, :] = (dz * sl).astype(BF)

    g.second()
    g.sibling_arrived(())
    units_of(())
    g.third()
    last = None
    for m in MASKS[1:]:
        g.complete(m)
        g.pass_on(m)
        if last is not None:
            g.sibling_arrived(last)
            units_of(last)
        last = m
    g.sibling_arrived(last)
    units_of(last)

    def partial(dst, lhs, rhs, p):
        lo, w = PARTS[p]

        @pl.loop(0, 8)
        def _(q):
            a, b, c = q // 4, (q // 2) % 2, q % 2
            dst[a, b, c, :, lo:lo + w] = tn(lhs[a, b, c], rhs[:, lo:lo + w]).astype(BF)

    sa = Scatter(at, fa, core_in, a0, a1, a2, sas, sar)
    sb = Scatter(at, fb, core_in, b0, b1, b2, sbs, sbr)
    for p in range(3):
        partial(fa, dgu, wgu, p)
        sa.start(sa.core_copy(p))
        if p:
            sa.add_core(p - 1)
    sa.add_core(2)
    pl.semaphore_signal(credit, inc=1, device_id=other(at, "c"), device_id_type=MESH)
    for p in range(3):
        partial(fb, zb, wd_ref, p)
    for p in range(3):
        sa.step(p, 0)
    pl.semaphore_wait(credit, 1)
    for p in range(3):
        sb.start(sb.core_copy(p))
    cw = 512

    def grads(lhs_list):
        @pl.loop(0, rows.shape[4] // cw)
        def _(n):
            s = pl.ds(pl.multiple_of(n * cw, cw), cw)
            for lhs, rhs, outs in lhs_list:
                acc = None
                for q in range(8):
                    a, b, c = q // 4, (q // 2) % 2, q % 2
                    v = nn(lhs[a, b, c], rhs[a, b, c, :, s])
                    acc = v if acc is None else acc + v
                for k, o in enumerate(outs):
                    o[:, s] = acc[k * units:(k + 1) * units].astype(BF)

    for p in range(3):
        sb.add_core(p)
    for p in range(3):
        sa.step(p, 1)
    grads([(zb, cot_ref, (gwd_out,))])
    for p in range(3):
        sa.finish(p, dn2_out)
    grads([(dgu, rows, (gwg_out, gwu_out))])
    for p in range(3):
        sb.step(p, 0)
    for p in range(3):
        sb.step(p, 1)
    for p in range(3):
        sb.finish(p, down_out)
    g.close()
    sa.close()
    sb.close()


def mlp(n2, cot_all, wg, wu, wd):
    rows, d = n2.shape
    units = wd.shape[0]
    vm = pl.BlockSpec(memory_space=pltpu.VMEM)
    hbm = pl.BlockSpec(memory_space=pl.ANY)
    cube = (2, 2, 2)
    dma = pltpu.SemaphoreType.DMA
    return pl.pallas_call(
        mlp_kernel,
        out_shape=(jax.ShapeDtypeStruct((rows, d), BF), jax.ShapeDtypeStruct((rows, d), F32))
        + (jax.ShapeDtypeStruct((units, d), BF),) * 3,
        in_specs=[vm, vm, hbm, hbm, vm],
        out_specs=(vm,) * 5,
        scratch_shapes=[
            pltpu.VMEM(cube + (2 * rows, d), BF),
            pltpu.VMEM((2 * units, d), BF),
            pltpu.VMEM(cube + (units, 2 * rows), BF),
            pltpu.VMEM(cube + (2 * units, 2 * rows), BF),
            pltpu.VMEM(cube + (2 * rows, d), BF),
            pltpu.VMEM(cube + (2 * rows, d), BF),
            pltpu.VMEM(cube + (rows, d), BF),
            pltpu.VMEM((2, 2, rows, d), BF), pltpu.VMEM((2, rows, d), BF), pltpu.VMEM((rows, d), BF),
            pltpu.VMEM((2, 2, rows, d), BF), pltpu.VMEM((2, rows, d), BF), pltpu.VMEM((rows, d), BF),
            dma((2,)), dma((3, 8)), dma((3, 8)), dma((8,)), dma((8,)),
            dma((3, 4)), dma((3, 4)), dma((3, 4)), dma((3, 4)), pltpu.SemaphoreType.REGULAR,
        ],
        compiler_params=pltpu.CompilerParams(collective_id=1, has_side_effects=True, vmem_limit_bytes=63 * 2**20),
        cost_estimate=pl.CostEstimate(flops=18 * 16 * rows * d * units, bytes_accessed=40 * 2**20, transcendentals=16 * rows * units),
        name="mlp",
    )(n2, cot_all.reshape(cube + (2 * rows, d)), wg, wu, wd)


def local(tokens, gain_attn, w_query, w_key, w_value, w_out, gain_mlp, w_gate_t, w_up_t, w_down, doc_ids, cotangent):
    rows, d = tokens.shape
    wrows = w_query.shape[0]
    grows = rows * 4
    seq_ids = doc_ids[0]
    length = seq_ids.shape[0]
    t = lax.axis_index(T)
    zi = lax.axis_index(Z)
    hd = HEAD_DIM
    qc = GROUP * hd
    gains = lax.all_gather(jnp.stack([gain_attn, gain_mlp]), AXES, axis=1, tiled=True).astype(F32)
    ga, gm = gains[0], gains[1]
    wall = jnp.concatenate([w_query.reshape(wrows, 4, qc), w_key.reshape(wrows, 4, hd), w_value.reshape(wrows, 4, hd)], axis=2).transpose(1, 0, 2)
    wsl = lax.all_to_all(wall, T, 0, 0, tiled=True)
    wqkv = lax.all_gather(wsl.reshape(4 * wrows, qc + 2 * hd), DP + Z, axis=0, tiled=True)
    wo = lax.dynamic_slice_in_dim(lax.all_gather(w_out, AXES, axis=0, tiled=True), t * qc, qc, 0)
    first = zi * grows
    own_ids = lax.dynamic_slice_in_dim(seq_ids, first, grows, 0)
    qpos = first + jnp.arange(grows, dtype=jnp.int32)
    kpos = jnp.arange(length, dtype=jnp.int32)
    starts = jnp.sum((seq_ids[None, :] < own_ids[:, None]).astype(jnp.int32), axis=1)
    freq = 10000.0 ** (-jnp.arange(hd // 2, dtype=F32) / (hd // 2))
    ph = (qpos - starts).astype(F32)[:, None] * freq[None, :]
    cos, sin = jnp.cos(ph), jnp.sin(ph)
    allowed = (seq_ids[None, :] == own_ids[:, None]) & (kpos[None, :] <= qpos[:, None])
    x = tokens.astype(F32)
    inv1 = lax.rsqrt(jnp.mean(x * x, axis=-1, keepdims=True) + NORM_EPS)
    n1 = (x * inv1 * ga).astype(BF)
    n1g = lax.all_gather(n1, T, axis=0, tiled=True)
    qkv = nn(n1g, wqkv)
    q = rotate(qkv[:, :qc].reshape(grows, GROUP, hd), cos[:, None], sin[:, None], 1.0).astype(BF)
    k = rotate(qkv[:, qc:qc + hd], cos, sin, 1.0).astype(BF)
    v = qkv[:, qc + hd:].astype(BF)
    kv = lax.all_gather(jnp.concatenate([k, v], axis=1), Z, axis=0, tiled=True)
    ka, va = kv[:, :hd], kv[:, hd:]
    scale = hd ** -0.5
    qh = q.transpose(1, 0, 2)

    def fwd(qq):
        s = jnp.where(allowed, nt(qq, ka) * scale, MASKED)
        mx = jnp.max(s, axis=1, keepdims=True)
        e = jnp.exp(s - mx)
        tot = jnp.sum(e, axis=1, keepdims=True)
        return nn((e / tot).astype(BF), va), mx + jnp.log(tot)

    o, lse = lax.map(fwd, qh)
    o = o.transpose(1, 0, 2).reshape(grows, qc).astype(BF)
    part = nn(o, wo).astype(BF)
    m = x + lax.psum_scatter(part, T, scatter_dimension=0, tiled=True).astype(F32)
    inv2 = lax.rsqrt(jnp.mean(m * m, axis=-1, keepdims=True) + NORM_EPS)
    n2 = (m * inv2 * gm).astype(BF)
    wgt = lax.all_gather(w_gate_t, REST, axis=0, tiled=True)
    wut = lax.all_gather(w_up_t, REST, axis=0, tiled=True)
    wdn = lax.all_gather(w_down, REST, axis=0, tiled=True)
    cot_all = lax.all_gather(cotangent, CUBE, axis=0, tiled=True)
    down, dn2, gwd, gwg, gwu = mlp(n2, cot_all, wgt, wut, wdn)
    rs = lambda a: lax.psum_scatter(a, REST, scatter_dimension=0, tiled=True).astype(F32)
    gwd, gwg, gwu = rs(gwd), rs(gwg), rs(gwu)
    block_out = (m + down.astype(F32)).astype(BF)
    ggm = jnp.sum(dn2 * m * inv2, axis=0)
    dy = dn2 * gm
    dm = cotangent.astype(F32) + inv2 * (dy - m * (inv2 * inv2) * jnp.mean(dy * m, axis=-1, keepdims=True))
    da = lax.all_gather(dm.astype(BF), T, axis=0, tiled=True)
    do = nt(da, wo).astype(BF)
    gwo = tn(o, da)
    doh = do.reshape(grows, GROUP, hd).transpose(1, 0, 2)

    def bwd(a):
        qq, dd, ls = a
        s = jnp.where(allowed, nt(qq, ka) * scale, MASKED)
        p = jnp.exp(s - ls)
        dp = nt(dd, va)
        ds = (p * (dp - jnp.sum(p * dp, axis=1, keepdims=True))).astype(BF)
        return nn(ds, ka) * scale, tn(ds, qq) * scale, tn(p.astype(BF), dd)

    dq, dk, dv = lax.map(bwd, (qh, doh, lse))
    dkv = jnp.concatenate([jnp.sum(dk, 0), jnp.sum(dv, 0)], axis=1).astype(BF)
    dkv = lax.psum_scatter(dkv, Z, scatter_dimension=0, tiled=True).astype(F32)
    dqr = rotate(dq.transpose(1, 0, 2), cos[:, None], sin[:, None], -1.0).reshape(grows, qc).astype(BF)
    dkr = rotate(dkv[:, :hd], cos, sin, -1.0).astype(BF)
    dqkv = jnp.concatenate([dqr, dkr, dkv[:, hd:].astype(BF)], axis=1)
    gw = lax.psum_scatter(tn(n1g, dqkv).astype(BF), DP + Z, scatter_dimension=0, tiled=True)
    gw = lax.all_to_all(gw.reshape(4, wrows, qc + 2 * hd), T, 0, 0, tiled=True).transpose(1, 0, 2).astype(F32)
    gwq = gw[:, :, :qc].reshape(wrows, 4 * qc)
    gwk = gw[:, :, qc:qc + hd].reshape(wrows, 4 * hd)
    gwv = gw[:, :, qc + hd:].reshape(wrows, 4 * hd)
    full = lax.dynamic_update_slice(jnp.zeros((4 * qc, d), BF), gwo.astype(BF), (t * qc, 0))
    gwo = lax.psum_scatter(full, AXES, scatter_dimension=0, tiled=True).astype(F32)
    dn1 = lax.psum_scatter(nt(dqkv, wqkv).astype(BF), T, scatter_dimension=0, tiled=True).astype(F32)
    gga = jnp.sum(dn1 * x * inv1, axis=0)
    dy1 = dn1 * ga
    dx1 = inv1 * (dy1 - x * (inv1 * inv1) * jnp.mean(dy1 * x, axis=-1, keepdims=True))
    gg = lax.psum_scatter(jnp.stack([gga, ggm]), AXES, scatter_dimension=1, tiled=True)
    return block_out, dm + dx1, gg[0], gwq, gwk, gwv, gwo, gg[1], gwg, gwu, gwd


def solution(mesh):
    dp, seq = mesh.shape["dp"], mesh.shape["seq"]
    m6 = Mesh(mesh.devices.reshape(dp // 2, 2, seq // 8, 2, 2, 2), AXES)
    row = P(AXES, None)
    vec = P(AXES)
    col = P(None, AXES)
    inner = jax.shard_map(
        local, mesh=m6,
        in_specs=(row, vec, row, row, row, row, vec, row, row, row, P(DP, None), row),
        out_specs=(row, row, vec, row, row, row, row, vec, row, row, row),
        check_vma=False,
    )

    def run(tokens, gain_attn, w_query, w_key, w_value, w_out, gain_mlp, w_gate, w_up, w_down, doc_ids, cotangent):
        outs = inner(tokens, gain_attn, w_query, w_key, w_value, w_out, gain_mlp, w_gate.T, w_up.T, w_down, doc_ids, cotangent)
        return outs[:8] + (outs[8].T, outs[9].T, outs[10])

    return run
```

time: 1760 us -> 1200 us (0.68)
  waiting for transfers between devices: 1410 us -> 777 us
  Pallas kernels: 0 us -> 123 us
  matrix products: 198 us -> 114 us
    reduce_scatter x9 -> x8, waiting for transfers between devices: 849 us -> 397 us  [the longest x1 143 us: local(): lax.psum_scatter(full, AXES, scatter_dimension=0, tiled=True).astype(F32)]
    all_gather x11 -> x8, waiting for transfers between devices: 465 us -> 251 us  [the longest x1 52.4 us: local(): lax.all_gather(wsl.reshape(4 * wrows, qc + 2 * hd), DP + Z, axis=0, tiled...]
    pallas_call x0 -> x1, Pallas kernels: none -> 123 us  [mlp(): pl.pallas_call(mlp_kernel, out_shape=(jax.ShapeDtypeStruct((rows, d), BF)...]
    dot_general x49 -> x62, matrix products: 198 us -> 114 us  [the longest x26 49 us: nt(): lax.dot_general(a, b, (((1,), (1,)), ((), ())), preferred_element_type=F32)]
    unnamed x2 -> x0, blocking collectives: 80.6 us -> none
    all_gather x0 -> x2, blocking collectives: none -> 61 us  [the longest x1 42.9 us: local(): lax.all_gather(jnp.stack([gain_attn, gain_mlp]), AXES, axis=1, tiled=True)]
    unnamed x24 -> x18, waiting for transfers between devices: 91.2 us -> 129 us
  transfers between devices with their start and end apart: 22 -> 18, of which waited for: 22 -> 17; matrix products, arithmetic and copies ran while one was open for 9% -> 6% of each run, Pallas kernels for 0% -> 0%
where the time goes in v1:
time: 1200 us; the launch traced here: 1190 us
  waiting for transfers between devices  777 us (65%)
  Pallas kernels  123 us (10%)
  matrix products  114 us (10%)
  blocking collectives  73.9 us (6%)
  other arithmetic  47.1 us (4%)
  local copies, waits for them, and re-layouts  27.9 us (2%)
  between operations  16.9 us (1%)
    reduce_scatter x1, waiting for transfers between devices, local(): lax.psum_scatter(full, AXES, scatter_dimension=0, tiled=True).astype(F32)  143 us
    unnamed x18, waiting for transfers between devices  129 us
    pallas_call x1, Pallas kernels, mlp(): pl.pallas_call(mlp_kernel, out_shape=(jax.ShapeDtypeStruct((rows, d), BF)...  123 us
    reduce_scatter x3, waiting for transfers between devices, local(): lax.psum_scatter(a, REST, scatter_dimension=0, tiled=True).astype(F32)  113 us
    reduce_scatter x1, waiting for transfers between devices, local(): lax.psum_scatter(tn(n1g, dqkv).astype(BF), DP + Z, scatter_dimension=0, t...  69.8 us
    all_gather x1, waiting for transfers between devices, local(): lax.all_gather(wsl.reshape(4 * wrows, qc + 2 * hd), DP + Z, axis=0, tiled...  52.4 us
    all_gather x1, waiting for transfers between devices, local(): cot_all = lax.all_gather(cotangent, CUBE, axis=0, tiled=True)  50.8 us
    dot_general x26, matrix products, nt(): lax.dot_general(a, b, (((1,), (1,)), ((), ())), preferred_element_type=F32)  49 us
  transfers between devices with their start and end apart: 18, of which 17 were waited for; matrix products, arithmetic and copies ran while one was open for 6% of the time, Pallas kernels for 0%

profile of v1, /device:TPU:1, one launch (start us, length us, event | category | flops | bytes accessed | tf_op | source)
XLA Modules:
  0.0 1186.9 jit_solution(14815280260178729271)
XLA Ops:
  10.6 42.9 %all-gather = bf16[32,64,2]{1,2,0:T(2,128)(2,1)S(1)} all-gather(bf16[1,64,2]{1,2,0:T(2,128)(2,1)S(1)} %maximum_bitcast_fusion.2), channel_id=1, replica_groups=mesh['dh'=1,'dl'=2,'zh'=2,'zl'=2,'x'=2,'c'=2] {'dh','dl','zh','zl','x','c'}, dimensions={0}, use_global_device_ids=true | all-gather | bytes 8448 | tf_op jit(solution)/shard_map/all_gather | solution.py:399
  53.6 2.0 fusion.44
  58.8 12.9 %all_to_all.10 = bf16[4,64,640]{2,1,0:T(8,128)(2,1)} all-to-all(bf16[4,64,640]{2,1,0:T(8,128)(2,1)S(1)} %copy.101), channel_id=1, replica_groups=mesh['dh'=1,'dl'=2,'zh'=2,'zl'=2,'x'=2,'c'=2] {'x','c'}, dimensions={0} | all-to-all | bytes 655360 | tf_op jit(solution)/shard_map/all_to_all | solution.py:402
  75.7 2.4 all-gather.10.cloned.1.call-done
  78.1 52.4 %all-gather.12.cloned.1.call-done = bf16[2048,640]{1,0:T(8,128)(2,1)} async-done(((bf16[256,640]{1,0:T(8,128)(2,1)}), bf16[2048,640]{1,0:T(8,128)(2,1)}) %all-gather.12.cloned.1.call-update) | async-done | bytes 2621456 | tf_op jit(solution)/shard_map/all_gather | solution.py:403
  130.5 4.2 fusion.77
  137.8 18.1 %all_gather.33 = bf16[2048,128]{1,0:T(8,128)(2,1)S(1)} all-gather(bf16[512,128]{1,0:T(8,128)(2,1)S(1)} %pad_maximum_fusion.3), channel_id=1, replica_groups=mesh['dh'=1,'dl'=2,'zh'=2,'zl'=2,'x'=2,'c'=2] {'zh','zl'}, dimensions={0}, use_global_device_ids=true | all-gather | bytes 655360 | tf_op jit(solution)/shard_map/all_gather | solution.py:422
  156.2 29.3 %while.30 = (s32[]{:T(128)}, bf16[8,512,64]{1,2,0:T(8,128)(2,1)S(1)}, f32[8,512,1]{1,2,0:T(1,128)}, bf16[8,512,64]{2,1,0:T(8,128)(2,1)S(1)}, bf16[2048,64]{1,0:T...) while((s32[]{:T(128)}, ...), condition=%wide.region_5.6_spmd.clone.clone, body=%wide.region_2.5_spmd.clone.sunk.clone | while | flops 279969280 | bytes 13926513 | solution.py:434
  185.5 27.5 %all-gather.14.cloned.1.call-done = bf16[2048,2048]{1,0:T(8,128)(2,1)} async-done(((bf16[64,2048]{1,0:T(8,128)(2,1)}), bf16[2048,2048]{1,0:T(8,128)(2,1)}) %all-gather.14.cloned.1.call-update) | async-done | bytes 8388624 | tf_op jit(solution)/shard_map/all_gather | solution.py:404
  213.0 4.4 convolution_convert_fusion.2
  220.2 27.4 %reduce-scatter.12.cloned.1.call-done = bf16[128,2048]{1,0:T(8,128)(2,1)} async-done(((bf16[512,2048]{1,0:T(8,128)(2,1)}), bf16[128,2048]{1,0:T(8,128)(2,1)}) %reduce-scatter.12.cloned.1.call-update) | async-done | bytes 524304 | tf_op jit(solution)/shard_map/reduce_scatter | solution.py:437
  248.8 2.0 multiply_convert_fusion.1.n2_ref
  250.9 9.1 all-gather.18.cloned.1.call-done.wg_ref
  259.9 42.5 %all-gather.20.cloned.1.call-done.wu_ref = bf16[352,2048]{1,0:T(8,128)(2,1)} async-done(((bf16[176,2048]{1,0:T(8,128)(2,1)}), bf16[352,2048]{1,0:T(8,128)(2,1)}) %all-gather.20.cloned.1.call-update) | async-done | bytes 1441808 | tf_op jit(solution)/shard_map/all_gather | solution.py:441
  302.4 42.5 %all-gather.22.cloned.1.call-done.wd_ref = bf16[352,2048]{1,0:T(8,128)(2,1)} async-done(((bf16[176,2048]{1,0:T(8,128)(2,1)}), bf16[352,2048]{1,0:T(8,128)(2,1)}) %all-gather.22.cloned.1.call-update) | async-done | bytes 1441808 | tf_op jit(solution)/shard_map/all_gather | solution.py:442
  344.9 50.8 %all-gather.16.cloned.1.call-done = bf16[2048,2048]{1,0:T(8,128)(2,1)} async-done(((bf16[128,2048]{1,0:T(8,128)(2,1)}), bf16[2048,2048]{1,0:T(8,128)(2,1)}) %all-gather.16.cloned.1.call-update) | async-done | bytes 8388624 | tf_op jit(solution)/shard_map/all_gather | solution.py:443
  395.7 123.2 %mlp.1 = (bf16[128,2048]{1,0:T(8,128)(2,1)}, f32[128,2048]{1,0:T(8,128)}, bf16[352,2048]{1,0:T(8,128)(2,1)}, bf16[352,2048]{1,0:T(8,128)(2,1)}, bf16[352,2048]{1,0:T(8,128)(2,1)}) custom-call(bf16[128,2048]{1,0:T(8,128)(2,1)} %multiply_convert_fusion.1.n2_ref, bf16[2,2,2,256,2048]{4,3,2,1,0:T(8,128)(2,1)} %bitcast.182, ...), custom_call_target="tpu_custom_call" | custom-call | flops 26575110144 | bytes 41943040 | tf_op jit(solution)/shard_map/mlp/pallas_call | solution.py:364
  518.9 1.7 multiply_reduce_fusion.1
  520.6 2.9 fusion.70
  523.8 24.3 %all-gather.24.cloned.1.call-done = bf16[512,2048]{1,0:T(8,128)(2,1)} async-done(((bf16[128,2048]{1,0:T(8,128)(2,1)}), bf16[512,2048]{1,0:T(8,128)(2,1)}) %all-gather.24.cloned.1.call-update) | async-done | bytes 2097168 | tf_op jit(solution)/shard_map/all_gather | solution.py:451
  548.1 4.3 fusion.36
  552.4 1.5 copy.108
  553.9 78.8 %while.31 = (s32[]{:T(128)}, f32[8,512,64]{1,2,0:T(8,128)}, f32[8,2048,64]{1,2,0:T(8,128)}, f32[8,2048,64]{1,2,0:T(8,128)}, bf16[8,512,64]{2,1,0:T(8,128)(2,1)},...) while((s32[]{:T(128)}, f32[8,512,64]{1,2,0:T(8,128)}, ...), condition=%wide.region_11.12_spmd.clone.clone, body=%wide.region_9.11_spmd.clone.sunk.clone | while | flops 683834880 | bytes 34234508 | solution.py:464
  555.4 3.0 multiply_reduce_fusion.6
  561.6 2.3 fusion.145
  565.2 3.0 multiply_reduce_fusion.6
  571.4 2.2 fusion.145
  575.0 3.0 multiply_reduce_fusion.6
  581.2 2.2 fusion.145
  584.9 3.0 multiply_reduce_fusion.6
  589.6 1.4 fusion.144
  591.1 2.2 fusion.145
  594.7 3.0 multiply_reduce_fusion.6
  599.5 1.4 fusion.144
  600.9 2.2 fusion.145
  604.5 3.0 multiply_reduce_fusion.6
  609.3 1.4 fusion.144
  610.7 2.3 fusion.145
  614.4 3.0 multiply_reduce_fusion.6
  619.2 1.4 fusion.144
  620.6 2.3 fusion.145
  624.3 3.0 multiply_reduce_fusion.6
  629.1 1.4 fusion.144
  630.5 2.3 fusion.145
  632.7 2.6 reduce_sum.104
  635.4 2.5 reduce_sum.103
  639.0 19.3 %reduce-scatter.14.cloned.1.call-done = bf16[512,128]{0,1:T(8,128)(2,1)} async-done(((bf16[2048,128]{0,1:T(8,128)(2,1)}), bf16[512,128]{0,1:T(8,128)(2,1)}) %reduce-scatter.14.cloned.1.call-update) | async-done | bytes 131088 | tf_op jit(solution)/shard_map/reduce_scatter | solution.py:466
  660.5 4.9 convolution_convert_fusion.3
  667.7 4.9 convolution_convert_fusion
  672.7 24.3 %reduce-scatter.16.cloned.1.call-done = bf16[128,2048]{1,0:T(8,128)(2,1)} async-done(((bf16[512,2048]{1,0:T(8,128)(2,1)}), bf16[128,2048]{1,0:T(8,128)(2,1)}) %reduce-scatter.16.cloned.1.call-update) | async-done | bytes 524304 | tf_op jit(solution)/shard_map/reduce_scatter | solution.py:477
  700.1 4.3 broadcast_in_dim.47
  704.4 2.6 fusion.32
  707.1 33.2 %reduce-scatter.26.cloned.1.call-done = bf16[176,2048]{1,0:T(8,128)(2,1)} async-done(((bf16[352,2048]{1,0:T(8,128)(2,1)}), bf16[176,2048]{1,0:T(8,128)(2,1)}) %reduce-scatter.26.cloned.1.call-update) | async-done | bytes 720912 | tf_op jit(solution)/shard_map/reduce_scatter | solution.py:445
  740.3 2.4 convert_element_type.131
  742.7 40.0 %reduce-scatter.24.cloned.1.call-done = bf16[176,2048]{1,0:T(8,128)(2,1)} async-done(((bf16[352,2048]{1,0:T(8,128)(2,1)}), bf16[176,2048]{1,0:T(8,128)(2,1)}) %reduce-scatter.24.cloned.1.call-update) | async-done | bytes 720912 | tf_op jit(solution)/shard_map/reduce_scatter | solution.py:445
  782.7 2.4 convert_bitcast_fusion
  785.0 39.9 %reduce-scatter.22.cloned.1.call-done = bf16[176,2048]{1,0:T(8,128)(2,1)} async-done(((bf16[352,2048]{1,0:T(8,128)(2,1)}), bf16[176,2048]{1,0:T(8,128)(2,1)}) %reduce-scatter.22.cloned.1.call-update) | async-done | bytes 720912 | tf_op jit(solution)/shard_map/reduce_scatter | solution.py:445
  825.0 2.4 convert_bitcast_fusion.1
  827.4 69.8 %reduce-scatter.18.cloned.1.call-done = bf16[256,640]{1,0:T(8,128)(2,1)} async-done(((bf16[2048,640]{1,0:T(8,128)(2,1)}), bf16[256,640]{1,0:T(8,128)(2,1)}) %reduce-scatter.18.cloned.1.call-update) | async-done | bytes 327696 | tf_op jit(solution)/shard_map/reduce_scatter | solution.py:470
  897.2 5.1 all-to-all-start.1
  902.3 3.1 fusion.41
  905.5 123.8 %reduce-scatter.28.cloned.1.call-done = f32[64,2]{1,0:T(8,128)} async-done(((f32[2048,2]{1,0:T(8,128)}), f32[64,2]{1,0:T(8,128)}) %reduce-scatter.28.cloned.1.call-update) | async-done | bytes 528
  1034.1 142.9 %reduce-scatter.20.cloned.1.call-done = bf16[64,2048]{1,0:T(8,128)(2,1)} async-done(((bf16[2048,2048]{1,0:T(8,128)(2,1)}), bf16[64,2048]{1,0:T(8,128)(2,1)}) %reduce-scatter.20.cloned.1.call-update) | async-done | bytes 262160 | tf_op jit(solution)/shard_map/reduce_scatter | solution.py:476
  1177.0 1.8 convert_element_type.128
  (217 shorter events, 89.4 us)
Async XLA Ops:
  8.0 65.7 %copy-start.14 = (s32[1,2048]{1,0:T(1,128)S(1)}, s32[1,2048]{1,0:T(1,128)}, u32[]{:S(2)}) copy-start(s32[1,2048]{1,0:T(1,128)} %param.26) | copy-start | bytes 24580
  8.0 70.1 %all-gather.10.cloned.1.call-start = ((), (), s32[]{:S(2)}) async-start(), calls=%async_computation.11 | async-start | bytes 2621440 | tf_op jit(solution)/shard_map/all_gather | solution.py:417
  9.9 46.6 %copy-start.18 = (f32[128]{0:T(128)}, f32[128]{0:T(128)S(1)}, u32[]{:S(2)}) copy-start(f32[128]{0:T(128)S(1)} %get-tuple-element.372) | copy-start | bytes 1540
  55.6 74.9 %all-gather.12.cloned.1.call-start = ((), (), s32[]{:S(2)}) async-start(), calls=%async_computation.12 | async-start | bytes 2949120 | tf_op jit(solution)/shard_map/all_gather | solution.py:403
  71.8 141.2 %all-gather.14.cloned.1.call-start = ((), (), s32[]{:S(2)}) async-start(), calls=%async_computation.13 | async-start | bytes 8650752 | tf_op jit(solution)/shard_map/all_gather | solution.py:404
  72.5 175.0 %reduce-scatter.12.cloned.1.call-start = ((), (), s32[]{:S(2)}) async-start(), calls=%async_computation.14 | async-start | bytes 2621440 | tf_op jit(solution)/shard_map/reduce_scatter | solution.py:437
  73.7 61.0 %copy-start.16 = (s32[1,512]{1,0:T(1,128)}, s32[1,512]{1,0:T(1,128)S(1)}, u32[]{:S(2)}) copy-start(s32[1,512]{1,0:T(1,128)S(1)} %constant_dynamic-slice_fusion.1) | copy-start | bytes 6148
  135.6 20.5 %copy-start.9 = (bf16[8,512,64]{1,2,0:T(8,128)(2,1)S(1)}, bf16[8,512,64]{1,2,0:T(8,128)(2,1)}, u32[]{:S(2)}) copy-start(bf16[8,512,64]{1,2,0:T(8,128)(2,1)} %broadcast_convert_fusion) | copy-start | bytes 1572868
  135.6 20.5 %copy-start.15 = (s32[1,2048]{1,0:T(1,128)S(1)}, s32[1,2048]{1,0:T(1,128)}, u32[]{:S(2)}) copy-start(s32[1,2048]{1,0:T(1,128)} %param.26) | copy-start | bytes 24580
  135.6 20.5 %copy-start.17 = (s32[1,512]{1,0:T(1,128)S(1)}, s32[1,512]{1,0:T(1,128)}, u32[]{:S(2)}) copy-start(s32[1,512]{1,0:T(1,128)} %copy-done.16) | copy-start | bytes 6148
  135.6 20.5 %copy-start.21 = (s32[512]{0:T(512)S(1)}, s32[512]{0:T(512)}, u32[]{:S(2)}) copy-start(s32[512]{0:T(512)} %iota_add_fusion) | copy-start | bytes 6148
  185.5 27.5 %copy-start.10 = (bf16[8,512,64]{1,2,0:T(8,128)(2,1)}, bf16[8,512,64]{1,2,0:T(8,128)(2,1)S(1)}, u32[]{:S(2)}) copy-start(bf16[8,512,64]{1,2,0:T(8,128)(2,1)S(1)} %get-tuple-element.108) | copy-start | bytes 1572868
  185.5 33.7 %copy-start.1 = (bf16[2048,64]{1,0:T(8,128)(2,1)}, bf16[2048,64]{1,0:T(8,128)(2,1)S(1)}, u32[]{:S(2)}) copy-start(bf16[2048,64]{1,0:T(8,128)(2,1)S(1)} %get-tuple-element.641) | copy-start | bytes 786436
  185.5 33.7 %copy-start.3 = (bf16[2048,64]{1,0:T(8,128)(2,1)}, bf16[2048,64]{1,0:T(8,128)(2,1)S(1)}, u32[]{:S(2)}) copy-start(bf16[2048,64]{1,0:T(8,128)(2,1)S(1)} %get-tuple-element.642) | copy-start | bytes 786436
  185.5 33.7 %copy-start.8 = (bf16[8,512,64]{2,1,0:T(8,128)(2,1)}, bf16[8,512,64]{2,1,0:T(8,128)(2,1)S(1)}, u32[]{:S(2)}) copy-start(bf16[8,512,64]{2,1,0:T(8,128)(2,1)S(1)} %get-tuple-element.650) | copy-start | bytes 1572868
  213.0 34.6 %copy-start = (bf16[128,2048]{1,0:T(8,128)(2,1)S(1)}, bf16[128,2048]{1,0:T(8,128)(2,1)}, u32[]{:S(2)}) copy-start(bf16[128,2048]{1,0:T(8,128)(2,1)} %param.16) | copy-start | bytes 1572868
  217.4 42.5 %all-gather.18.cloned.1.call-start = ((), (), s32[]{:S(2)}) async-start(), calls=%async_computation.16 | async-start | bytes 2162688 | tf_op jit(solution)/shard_map/all_gather | solution.py:440
  218.0 84.4 %all-gather.20.cloned.1.call-start = ((), (), s32[]{:S(2)}) async-start(), calls=%async_computation.17 | async-start | bytes 2162688 | tf_op jit(solution)/shard_map/all_gather | solution.py:441
  218.6 126.3 %all-gather.22.cloned.1.call-start = ((), (), s32[]{:S(2)}) async-start(), calls=%async_computation.18 | async-start | bytes 2162688 | tf_op jit(solution)/shard_map/all_gather | solution.py:442
  219.2 176.4 %all-gather.16.cloned.1.call-start = ((), (), s32[]{:S(2)}) async-start(), calls=%async_computation.15 | async-start | bytes 8912896 | tf_op jit(solution)/shard_map/all_gather | solution.py:443
  220.0 328.2 %all-gather.24.cloned.1.call-start = ((), (), s32[]{:S(2)}) async-start(), calls=%async_computation.19 | async-start | bytes 2621440 | tf_op jit(solution)/shard_map/all_gather | solution.py:451
  523.4 134.9 %reduce-scatter.14.cloned.1.call-start = ((), (), s32[]{:S(2)}) async-start(), calls=%async_computation.20 | async-start | bytes 655360 | tf_op jit(solution)/shard_map/reduce_scatter | solution.py:466
  523.8 30.2 %copy-start.2 = (bf16[2048,64]{1,0:T(8,128)(2,1)S(1)}, bf16[2048,64]{1,0:T(8,128)(2,1)}, u32[]{:S(2)}) copy-start(bf16[2048,64]{1,0:T(8,128)(2,1)} %copy-done.1) | copy-start | bytes 786436
  523.8 30.2 %copy-start.4 = (bf16[2048,64]{1,0:T(8,128)(2,1)S(1)}, bf16[2048,64]{1,0:T(8,128)(2,1)}, u32[]{:S(2)}) copy-start(bf16[2048,64]{1,0:T(8,128)(2,1)} %copy-done.3) | copy-start | bytes 786436
  632.7 6.0 copy-start.12
  635.3 23.9 %copy-start.13 = (f32[512]{0:T(512)S(1)}, f32[512]{0:T(512)}, u32[]{:S(2)}) copy-start(f32[512]{0:T(512)} %subtract_convert_fusion.2) | copy-start | bytes 6148
  635.4 23.9 %copy-start.20 = (f32[32]{0:T(128)S(1)}, f32[32]{0:T(128)}, u32[]{:S(2)}) copy-start(f32[32]{0:T(128)} %multiply_power_fusion) | copy-start | bytes 388
  638.7 58.2 %reduce-scatter.16.cloned.1.call-start = ((), (), s32[]{:S(2)}) async-start(), calls=%async_computation.21 | async-start | bytes 2621440 | tf_op jit(solution)/shard_map/reduce_scatter | solution.py:477
  665.4 74.9 %reduce-scatter.26.cloned.1.call-start = ((), (), s32[]{:S(2)}) async-start(), calls=%async_computation.26 | async-start | bytes 2162688 | tf_op jit(solution)/shard_map/reduce_scatter | solution.py:445
  666.1 116.6 %reduce-scatter.24.cloned.1.call-start = ((), (), s32[]{:S(2)}) async-start(), calls=%async_computation.25 | async-start | bytes 2162688 | tf_op jit(solution)/shard_map/reduce_scatter | solution.py:445
  666.9 158.1 %reduce-scatter.22.cloned.1.call-start = ((), (), s32[]{:S(2)}) async-start(), calls=%async_computation.24 | async-start | bytes 2162688 | tf_op jit(solution)/shard_map/reduce_scatter | solution.py:445
  667.6 29.4 %copy-start.19 = (f32[128]{0:T(128)S(1)}, f32[128]{0:T(128)}, u32[]{:S(2)}) copy-start(f32[128]{0:T(128)} %copy-done.18) | copy-start | bytes 1540
  667.6 229.6 %reduce-scatter.18.cloned.1.call-start = ((), (), s32[]{:S(2)}) async-start(), calls=%async_computation.22 | async-start | bytes 2949120 | tf_op jit(solution)/shard_map/reduce_scatter | solution.py:470
  672.6 356.6 %reduce-scatter.28.cloned.1.call-start = ((), (), s32[]{:S(2)}) async-start(), calls=%async_computation.27 | async-start | bytes 1081344
  699.8 4.7 copy-start.11
  699.8 477.2 %reduce-scatter.20.cloned.1.call-start = ((), (), s32[]{:S(2)}) async-start(), calls=%async_computation.23 | async-start | bytes 8650752 | tf_op jit(solution)/shard_map/reduce_scatter | solution.py:476
  700.1 4.3 copy-start.23
  707.1 195.3 %copy-start.5 = (bf16[128,2048]{1,0:T(8,128)(2,1)S(1)}, bf16[128,2048]{1,0:T(8,128)(2,1)}, u32[]{:S(2)}) copy-start(bf16[128,2048]{1,0:T(8,128)(2,1)} %reduce-scatter.12.cloned.1.call-done) | copy-start | bytes 1572868
  707.1 195.3 %copy-start.6 = (f32[128,2048]{1,0:T(8,128)S(1)}, f32[128,2048]{1,0:T(8,128)}, u32[]{:S(2)}) copy-start(f32[128,2048]{1,0:T(8,128)} %get-tuple-element.110) | copy-start | bytes 3145732
  707.1 195.2 %copy-start.7 = (bf16[128,2048]{1,0:T(8,128)(2,1)S(1)}, bf16[128,2048]{1,0:T(8,128)(2,1)}, u32[]{:S(2)}) copy-start(bf16[128,2048]{1,0:T(8,128)(2,1)} %param.27) | copy-start | bytes 1572868
  707.1 195.2 %copy-start.22 = (f32[128]{0:T(128)S(1)}, f32[128]{0:T(128)}, u32[]{:S(2)}) copy-start(f32[128]{0:T(128)} %get-tuple-element.371) | copy-start | bytes 1540
  897.2 134.1 %all-to-all-start.1 = ((bf16[4,64,640]{2,1,0:T(8,128)(2,1)}), bf16[4,64,640]{2,1,0:T(8,128)(2,1)S(1)}, u32[]{:S(2)}, u32[]{:S(2)}) async-start(bf16[4,64,640]{2,1,0:T(8,128)(2,1)} %bitcast.162), calls=%async_computation.5 | async-start | bytes 655360 | tf_op jit(solution)/shard_map/all_to_all | solution.py:471
Sparse Core Ops, SparseCore 0:
  55.7 22.3 all-gather.9
  80.2 50.2 all-gather.11
  133.3 79.5 all-gather.13
  217.6 29.9 reduce-scatter.11
  523.6 24.5 all-gather.23
  665.5 31.4 reduce-scatter.15
  699.2 41.0 reduce-scatter.25
  742.6 40.0 reduce-scatter.23
  784.9 40.0 reduce-scatter.21
  828.7 68.3 reduce-scatter.17
  899.5 129.6 reduce-scatter.27
  1031.4 145.5 reduce-scatter.19
Sparse Core Ops, SparseCore 1:
  219.5 40.4 all-gather.17
  261.4 40.9 all-gather.19
  303.9 40.9 all-gather.21
  346.6 49.0 all-gather.15
  638.8 19.5 reduce-scatter.13

commit v2 on v1

--- a/solution.py
+++ b/solution.py
@@ -1,3 +1,5 @@
+import functools
+
 import jax
 import jax.numpy as jnp
 from jax import lax
@@ -69,6 +71,240 @@
 
 def order_of(p):
     return tuple(CDIMS[(p + s) % 3] for s in range(3))
+
+
+class Log:
+    def __init__(self):
+        self.open = []
+
+    def push(self, src, dst, ssem, rsem, device):
+        cp = pltpu.make_async_remote_copy(src, dst, ssem, rsem, device_id=device, device_id_type=MESH)
+        cp.start()
+        self.open.append(cp)
+
+    def close(self):
+        for cp in self.open:
+            cp.wait_send()
+
+
+def landed(dst, sem, device):
+    pltpu.make_async_remote_copy(dst, dst, sem, sem, device_id=device, device_id_type=MESH).wait_recv()
+
+
+def at_z(at, o, n):
+    i = lax.rem(at["zh"] * 2 + at["zl"] + o, n)
+    return tuple(i // 2 if a == "zh" else lax.rem(i, 2) if a == "zl" else at[a] for a in AXES), i
+
+
+def at_dp(at, o, n):
+    i = lax.rem(at["dh"] * 2 + at["dl"] + o, n)
+    return tuple(i // 2 if a == "dh" else lax.rem(i, 2) if a == "dl" else at[a] for a in AXES), i
+
+
+def at_rest(at, o, n):
+    i = lax.rem(at["dh"] * 2 + at["zh"] + o, n)
+    return tuple(i // 2 if a == "dh" else lax.rem(i, 2) if a == "zh" else at[a] for a in AXES), i
+
+
+def signal(device):
+    pl.semaphore_signal(pltpu.get_barrier_semaphore(), inc=1, device_id=device, device_id_type=MESH)
+
+
+def device_of(i, nz):
+    t, j = lax.rem(i, 4), i // 4
+    z, p = lax.rem(j, nz), j // nz
+    return (p // 2, lax.rem(p, 2), z // 2, lax.rem(z, 2), t // 2, lax.rem(t, 2))
+
+
+class Quad:
+    def __init__(self, at, log, buf, ssem, rsem):
+        self.at, self.log, self.buf, self.ssem, self.rsem = at, log, buf, ssem, rsem
+
+    def start(self):
+        at = self.at
+        own = self.buf.at[at["x"], at["c"]]
+        self.log.push(own, own, self.ssem.at[0], self.rsem.at[0], other(at, "x"))
+        self.log.push(own, own, self.ssem.at[1], self.rsem.at[1], other(at, "c"))
+
+    def forward(self):
+        at = self.at
+        far = self.buf.at[1 - at["x"], at["c"]]
+        landed(far, self.rsem.at[0], other(at, "x"))
+        self.log.push(far, far, self.ssem.at[2], self.rsem.at[2], other(at, "c"))
+
+    def finish(self):
+        at = self.at
+        landed(self.buf.at[at["x"], 1 - at["c"]], self.rsem.at[1], other(at, "c"))
+        landed(self.buf.at[1 - at["x"], 1 - at["c"]], self.rsem.at[2], other(at, "c"))
+
+
+class QuadSum:
+    def __init__(self, at, log, part, cin, xin, total, ssem, rsem, width):
+        self.at, self.log, self.part, self.cin, self.xin, self.total = at, log, part, cin, xin, total
+        self.ssem, self.rsem, self.width = ssem, rsem, width
+
+    def cols(self, n):
+        return slice(n * self.width, (n + 1) * self.width)
+
+    def start(self, n):
+        at, s = self.at, self.cols(n)
+        self.log.push(self.part.at[:, 1 - at["c"], :, s], self.cin.at[:, :, s], self.ssem.at[0, n], self.rsem.at[0, n], other(at, "c"))
+
+    def middle(self, n):
+        at, s = self.at, self.cols(n)
+        landed(self.cin.at[:, :, s], self.rsem.at[0, n], other(at, "c"))
+        far = self.part.at[1 - at["x"], at["c"], :, s]
+        far[...] = (far[...].astype(F32) + self.cin[1 - at["x"], :, s].astype(F32)).astype(BF)
+        self.log.push(far, self.xin.at[:, s], self.ssem.at[1, n], self.rsem.at[1, n], other(at, "x"))
+        near = self.part[at["x"], at["c"], :, s].astype(F32) + self.cin[at["x"], :, s].astype(F32)
+        self.total[:, s] = self.total[:, s] + near
+
+    def finish(self, n):
+        s = self.cols(n)
+        landed(self.xin.at[:, s], self.rsem.at[1, n], other(self.at, "x"))
+        self.total[:, s] = self.total[:, s] + self.xin[:, s].astype(F32)
+
+
+class Spread:
+    def __init__(self, at, log, buf, nrest, parts, sems):
+        self.at, self.log, self.buf, self.n, self.parts = at, log, buf, nrest, parts
+        self.s0, self.r0, self.s1, self.r1 = sems
+
+    def block(self, o, flip=(), part=None):
+        at = self.at
+        r = lax.rem(at["dh"] * (self.n_zh()) + at["zh"] + o, self.n)
+        dh, zh = r // self.n_zh(), lax.rem(r, self.n_zh())
+        dl = 1 - at["dl"] if "dl" in flip else at["dl"]
+        zl = 1 - at["zl"] if "zl" in flip else at["zl"]
+        ref = self.buf.at[dh * 2 + dl, zh * 2 + zl]
+        if part is None:
+            return ref
+        lo, w = self.parts[part][:2]
+        return ref.at[(slice(None),) * (len(ref.shape) - 1) + (slice(lo, lo + w),)]
+
+    def n_zh(self):
+        return self.buf.shape[1] // 2
+
+    def start(self):
+        for o in range(1, self.n):
+            ref = self.block(0)
+            self.log.push(ref, ref, self.s0.at[o - 1], self.r0.at[o - 1], at_rest(self.at, o, self.n)[0])
+
+    def arrive(self, o):
+        if o:
+            landed(self.block(self.n - o), self.r0.at[o - 1], other(self.at, "zl"))
+
+    def send(self, o, k, flip, part, dim):
+        ref = self.block((self.n - o) % self.n, flip, part)
+        self.log.push(ref, ref, self.s1.at[o, k], self.r1.at[o, k], other(self.at, dim))
+
+    def take(self, o, k, flip, part):
+        landed(self.block((self.n - o) % self.n, flip, part), self.r1.at[o, k], other(self.at, "zl"))
+
+    def stage1(self, o):
+        self.arrive(o)
+        for p, (_, _, a, b) in enumerate(self.parts):
+            self.send(o, 3 * p, (), p, a)
+        for p, (_, _, a, b) in enumerate(self.parts):
+            self.send(o, 3 * p + 1, (), p, b)
+
+    def stage2(self, o):
+        for p, (_, _, a, b) in enumerate(self.parts):
+            self.take(o, 3 * p, (a,), p)
+            self.send(o, 3 * p + 2, (a,), p, b)
+
+    def finish(self, o):
+        for p, (_, _, a, b) in enumerate(self.parts):
+            self.take(o, 3 * p + 1, (b,), p)
+            self.take(o, 3 * p + 2, (a, b), p)
+
+
+class Merge:
+    def __init__(self, at, log, buf, in1, in2, far, nrest, parts, sems):
+        self.at, self.log, self.buf, self.in1, self.in2, self.far = at, log, buf, in1, in2, far
+        self.n, self.parts = nrest, parts
+        self.s0, self.r0, self.s1, self.r1 = sems
+
+    def cut(self, ref, p):
+        lo, w = self.parts[p][:2]
+        return ref.at[(slice(None),) * (len(ref.shape) - 1) + (slice(lo, lo + w),)]
+
+    def block(self, o, flip, p):
+        at, nzh = self.at, self.buf.shape[1] // 2
+        r = lax.rem(at["dh"] * nzh + at["zh"] + o, self.n)
+        dl = 1 - at["dl"] if "dl" in flip else at["dl"]
+        zl = 1 - at["zl"] if "zl" in flip else at["zl"]
+        return self.cut(self.buf.at[(r // nzh) * 2 + dl, lax.rem(r, nzh) * 2 + zl], p)
+
+    def stage1(self, o):
+        for p, (_, _, a, b) in enumerate(self.parts):
+            for k, flip in enumerate(((a, b), (a,))):
+                self.log.push(self.block(o, flip, p), self.cut(self.in1.at[o, k], p), self.s1.at[o, 3 * p + k], self.r1.at[o, 3 * p + k],
+                              other(self.at, a))
+
+    def add(self, o, flip, p, ref):
+        blk = self.block(o, flip, p)
+        blk[...] = (blk[...].astype(F32) + ref[...].astype(F32)).astype(BF)
+
+    def stage2(self, o):
+        for p, (_, _, a, b) in enumerate(self.parts):
+            src = self.cut(self.in1.at[o, 0], p)
+            landed(src, self.r1.at[o, 3 * p], other(self.at, a))
+            self.add(o, (b,), p, src)
+            self.log.push(self.block(o, (b,), p), self.cut(self.in2.at[o], p), self.s1.at[o, 3 * p + 2], self.r1.at[o, 3 * p + 2],
+                          other(self.at, b))
+        for p, (_, _, a, b) in enumerate(self.parts):
+            src = self.cut(self.in1.at[o, 1], p)
+            landed(src, self.r1.at[o, 3 * p + 1], other(self.at, a))
+            self.add(o, (), p, src)
+
+    def stage3(self, o):
+        for p, (_, _, a, b) in enumerate(self.parts):
+            src = self.cut(self.in2.at[o], p)
+            landed(src, self.r1.at[o, 3 * p + 2], other(self.at, b))
+            self.add(o, (), p, src)
+        if o:
+            nzh = self.buf.shape[1] // 2
+            at = self.at
+            r = lax.rem(at["dh"] * nzh + at["zh"] + o, self.n)
+            ref = self.buf.at[(r // nzh) * 2 + at["dl"], lax.rem(r, nzh) * 2 + at["zl"]]
+            self.log.push(ref, self.far.at[o - 1], self.s0.at[o - 1], self.r0.at[o - 1], at_rest(at, o, self.n)[0])
+
+    def result(self):
+        at = self.at
+        nzh = self.buf.shape[1] // 2
+        total = self.buf[at["dh"] * 2 + at["dl"], at["zh"] * 2 + at["zl"]].astype(F32)
+        for o in range(1, self.n):
+            landed(self.far.at[o - 1], self.r0.at[o - 1], at_rest(at, self.n - o, self.n)[0])
+            total = total + self.far[o - 1].astype(F32)
+        return total
+
+
+class AllSum:
+    DIMS = ("c", "x", "dl", "zl")
+
+    def __init__(self, at, log, val, got, nrest, ssem, rsem):
+        self.at, self.log, self.val, self.got, self.n, self.ssem, self.rsem = at, log, val, got, nrest, ssem, rsem
+
+    def start(self, k):
+        if k < 4:
+            self.log.push(self.val.at[k], self.got.at[k], self.ssem.at[k], self.rsem.at[k], other(self.at, self.DIMS[k]))
+        else:
+            for o in range(1, self.n):
+                i = 3 + o
+                self.log.push(self.val.at[4], self.got.at[i], self.ssem.at[i], self.rsem.at[i], at_rest(self.at, o, self.n)[0])
+
+    def take(self, k):
+        if k < 4:
+            landed(self.got.at[k], self.rsem.at[k], other(self.at, self.DIMS[k]))
+            self.val[k + 1] = self.val[k] + self.got[k]
+            return None
+        total = self.val[4]
+        for o in range(1, self.n):
+            i = 3 + o
+            landed(self.got.at[i], self.rsem.at[i], other(self.at, "c"))
+            total = total + self.got[i]
+        return total
 
 
 class Gather:
@@ -251,20 +487,25 @@
             cp.wait_send()
 
 
-def mlp_kernel(n2_ref, cot_ref, wg_ref, wu_ref, wd_ref, down_out, dn2_out, gwd_out, gwg_out, gwu_out,
-               rows, wgu, zb, dgu, fa, fb, core_in, a0, a1, a2, b0, b1, b2,
+def mlp_kernel(m_ref, gain_ref, cot_ref, wg_own, wu_own, wd_own, wg_far, wu_far, wd_far, down_out, dn2_out, gwd_out, gwg_out, gwu_out,
+               rows, wgu, wd_ref, zb, dgu, fa, fb, core_in, a0, a1, a2, b0, b1, b2,
                lsem, gs, gr, gcs, gcr, sas, sar, sbs, sbr, credit):
     at = place()
     units = wd_ref.shape[0]
-    brows = n2_ref.shape[0]
-    copies = [pltpu.make_async_copy(wg_ref, wgu.at[:units, :], lsem.at[0]),
-              pltpu.make_async_copy(wu_ref, wgu.at[units:, :], lsem.at[1])]
+    brows = m_ref.shape[0]
+    part = wd_own.shape[0]
+    copies = []
+    for k, (own_w, far_w, dst, lo) in enumerate(((wg_own, wg_far, wgu, 0), (wu_own, wu_far, wgu, units), (wd_own, wd_far, wd_ref, 0))):
+        copies.append(pltpu.make_async_copy(own_w, dst.at[lo:lo + part, :], lsem.at[2 * k]))
+        copies.append(pltpu.make_async_copy(far_w, dst.at[lo + part:lo + units, :], lsem.at[2 * k + 1]))
     for cp in copies:
         cp.start()
     greet(at, (("c",), ("x",), ("zl",), ("dl",)))
     g = Gather(at, rows, gs, gr, gcs, gcr)
     own = pl.ds(pl.multiple_of(at["c"] * brows, brows), brows)
-    rows[at["dl"], at["zl"], at["x"], own, :] = n2_ref[...]
+    m = m_ref[...]
+    inv = lax.rsqrt(jnp.mean(m * m, axis=1, keepdims=True) + NORM_EPS)
+    rows[at["dl"], at["zl"], at["x"], own, :] = (m * inv * gain_ref[...]).astype(BF)
     g.first()
     for cp in copies:
         cp.wait()
@@ -354,9 +595,10 @@
     sb.close()
 
 
-def mlp(n2, cot_all, wg, wu, wd):
-    rows, d = n2.shape
-    units = wd.shape[0]
+def mlp(m, gain, cot_all, own, far):
+    rows, d = m.shape
+    far = tuple(a.reshape(-1, d) for a in far)
+    units = own[0].shape[0] + far[0].shape[0]
     vm = pl.BlockSpec(memory_space=pltpu.VMEM)
     hbm = pl.BlockSpec(memory_space=pl.ANY)
     cube = (2, 2, 2)
@@ -365,11 +607,12 @@
         mlp_kernel,
         out_shape=(jax.ShapeDtypeStruct((rows, d), BF), jax.ShapeDtypeStruct((rows, d), F32))
         + (jax.ShapeDtypeStruct((units, d), BF),) * 3,
-        in_specs=[vm, vm, hbm, hbm, vm],
+        in_specs=[vm, vm, vm] + [hbm] * 6,
         out_specs=(vm,) * 5,
         scratch_shapes=[
             pltpu.VMEM(cube + (2 * rows, d), BF),
             pltpu.VMEM((2 * units, d), BF),
+            pltpu.VMEM((units, d), BF),
             pltpu.VMEM(cube + (units, 2 * rows), BF),
             pltpu.VMEM(cube + (2 * units, 2 * rows), BF),
             pltpu.VMEM(cube + (2 * rows, d), BF),
@@ -377,109 +620,562 @@
             pltpu.VMEM(cube + (rows, d), BF),
             pltpu.VMEM((2, 2, rows, d), BF), pltpu.VMEM((2, rows, d), BF), pltpu.VMEM((rows, d), BF),
             pltpu.VMEM((2, 2, rows, d), BF), pltpu.VMEM((2, rows, d), BF), pltpu.VMEM((rows, d), BF),
-            dma((2,)), dma((3, 8)), dma((3, 8)), dma((8,)), dma((8,)),
+            dma((6,)), dma((3, 8)), dma((3, 8)), dma((8,)), dma((8,)),
             dma((3, 4)), dma((3, 4)), dma((3, 4)), dma((3, 4)), pltpu.SemaphoreType.REGULAR,
         ],
         compiler_params=pltpu.CompilerParams(collective_id=1, has_side_effects=True, vmem_limit_bytes=63 * 2**20),
         cost_estimate=pl.CostEstimate(flops=18 * 16 * rows * d * units, bytes_accessed=40 * 2**20, transcendentals=16 * rows * units),
         name="mlp",
-    )(n2, cot_all.reshape(cube + (2 * rows, d)), wg, wu, wd)
-
-
-def local(tokens, gain_attn, w_query, w_key, w_value, w_out, gain_mlp, w_gate_t, w_up_t, w_down, doc_ids, cotangent):
+    )(m, gain, cot_all, *own, *far)
+
+
+def rot_rows(v, cos, sin):
+    h = v.shape[0] // 2
+    a, b = v[:h], v[h:]
+    return jnp.concatenate([a * cos - b * sin, b * cos + a * sin], axis=0)
+
+
+def attn_kernel(nz, ndp, tok_ref, wpack, wout_ref, gpack, cos_ref, sin_ref, start_ref, cot_ref, wg_ref, wu_ref, wd_ref,
+                m_out, q_out, kv_out, o_out, lse_out, xg_out, wqkv_out, wo_out, gain_out, cot_out, wg_out, wu_out, wd_out,
+                xg, wbuf, wobuf, gbuf, kvbuf, qbuf, kn, vt, obuf, lbuf, bias, part, cin, xin, total,
+                lsem, s_disp, r_disp, s_gd, r_gd, s_w0, r_w0, s_w1, r_w1, s_g0, r_g0, s_g1, r_g1, s_o0, r_o0, s_o1, r_o1,
+                s_od, r_od, s_x, r_x, s_kv, r_kv, s_p, r_p, s_rest, r_rest, gs, gr, gcs, gcr):
+    at = place()
+    log = Log()
+    rows, d = tok_ref.shape
+    hd = HEAD_DIM
+    zi = at["zh"] * 2 + at["zl"]
+    di = at["dh"] * 2 + at["dl"]
+    t = at["x"] * 2 + at["c"]
+    nrest = nz * ndp // 4
+    wr = wpack.shape[1]
+    quad = (("c",), ("x",), ("x", "c"))
+    npeers = nz * ndp
+    lin = (di * nz + zi) * 4 + t
+    target = lax.rem(lin, npeers) * 4 + lin // npeers
+    source = lax.rem(lin, 4) * npeers + lin // 4
+    for f in quad:
+        signal(other(at, *f))
+    signal(other(at, "zl"))
+    signal(other(at, "dl"))
+    for o in range(1, nrest):
+        signal(at_rest(at, o, nrest)[0])
+
+    @pl.when(source != lin)
+    def _():
+        signal(device_of(source, nz))
+
+    pl.semaphore_wait(pltpu.get_barrier_semaphore(), 4 + nrest + (target != lin).astype(jnp.int32))
+    for k, f in enumerate(quad):
+        dev = other(at, *f)
+        tt = dev[4] * 2 + dev[5]
+        log.push(wpack.at[tt], wbuf.at[di, zi, pl.ds(pl.multiple_of(t * wr, wr), wr), :], s_disp.at[k], r_disp.at[k], dev)
+        log.push(gpack, gbuf.at[di, zi, t], s_gd.at[k], r_gd.at[k], dev)
+    wbuf[di, zi, pl.ds(pl.multiple_of(t * wr, wr), wr), :] = wpack[t]
+    gbuf[di, zi, t] = gpack[...]
+    x = tok_ref[...].astype(F32)
+    inv = lax.rsqrt(jnp.mean(x * x, axis=1, keepdims=True) + NORM_EPS)
+    xg[at["x"], at["c"]] = (x * inv).astype(BF)
+    total[...] = x
+    qx = Quad(at, log, xg, s_x, r_x)
+    qx.start()
+    for k, f in enumerate(quad):
+        dev = other(at, *f)
+        tt = dev[4] * 2 + dev[5]
+        landed(wbuf.at[di, zi, pl.ds(pl.multiple_of(tt * wr, wr), wr), :], r_disp.at[k], dev)
+        landed(gbuf.at[di, zi, tt], r_gd.at[k], dev)
+    half = 128 * (wbuf.shape[3] // 256)
+    sw = Spread(at, log, wbuf, nrest, ((0, half, "dl", "zl"), (half, wbuf.shape[3] - half, "zl", "dl")), (s_w0, r_w0, s_w1, r_w1))
+    sg = Spread(at, log, gbuf, nrest, ((0, 128, "zl", "dl"),), (s_g0, r_g0, s_g1, r_g1))
+    so = Spread(at, log, wobuf, nrest, ((0, d // 2, "dl", "zl"), (d // 2, d // 2, "zl", "dl")), (s_o0, r_o0, s_o1, r_o1))
+    for sp in (sw, sg):
+        sp.start()
+        sp.stage1(0)
+    qx.forward()
+    @pl.when(target != lin)
+    def _():
+        pltpu.make_async_remote_copy(wout_ref, wobuf.at[lax.rem(lin, npeers) // nz, lax.rem(lax.rem(lin, npeers), nz)], s_od, r_od,
+                                     device_id=device_of(target, nz), device_id_type=MESH).start()
+
+    @pl.when(target == lin)
+    def _():
+        wobuf[di, zi] = wout_ref[...]
+
+    qn = bias.shape[2]
+    nq = bias.shape[0]
+    keys = bias.shape[1]
+    kpos = lax.broadcasted_iota(jnp.int32, (keys, qn), 0)
+    for b in range(nq):
+        qpos = zi * (4 * rows) + b * qn + lax.broadcasted_iota(jnp.int32, (1, qn), 1)
+        first = start_ref[:, b * qn:(b + 1) * qn]
+        bias[b] = jnp.where((kpos >= first) & (kpos <= qpos), 0.0, MASKED)
+    for sp in (sw, sg):
+        sp.stage2(0)
+    for o in range(1, nrest):
+        for sp in (sw, sg):
+            sp.stage1(o)
+    outs = ((wg_ref, wg_out), (wu_ref, wu_out), (wd_ref, wd_out))
+
+    def push_rest(k):
+        a, b = outs[k]
+        for o in range(1, nrest):
+            dev, _ = at_rest(at, o, nrest)
+            log.push(a, b.at[o - 1], s_rest.at[k, o - 1], r_rest.at[k, o - 1], dev)
+
+    push_rest(0)
+    for o in range(1, nrest):
+        for sp in (sw, sg):
+            sp.stage2(o)
+    for o in range(nrest):
+        for sp in (sw, sg):
+            sp.finish(o)
+    qx.finish()
+    xa = xg[...].reshape(4 * rows, d)
+    qkv = jnp.transpose(nn(xa, wbuf[...].reshape(d, wbuf.shape[3])))
+    cos, sin = cos_ref[...], sin_ref[...]
+    kvbuf[zi, :hd, :] = rot_rows(qkv[GROUP * hd:(GROUP + 1) * hd], cos, sin).astype(BF)
+    kvbuf[zi, hd:, :] = qkv[(GROUP + 1) * hd:].astype(BF)
+    nzh = nz // 2
+    for o in range(1, nzh):
+        log.push(kvbuf.at[zi], kvbuf.at[zi], s_kv.at[0, o], r_kv.at[0, o], at_z(at, 2 * o, nz)[0])
+    log.push(kvbuf.at[zi], kvbuf.at[zi], s_kv.at[1, 0], r_kv.at[1, 0], other(at, "zl"))
+    for h in range(GROUP):
+        qbuf[h] = (rot_rows(qkv[h * hd:(h + 1) * hd], cos, sin).astype(BF) * 0.125).astype(BF)
+
+    @pl.when(source != lin)
+    def _():
+        pltpu.make_async_remote_copy(wobuf.at[di, zi], wobuf.at[di, zi], s_od, r_od,
+                                     device_id=device_of(source, nz), device_id_type=MESH).wait_recv()
+
+    so.start()
+    so.stage1(0)
+    g = Gather(at, cot_out, gs, gr, gcs, gcr)
+    here = [pltpu.make_async_copy(cot_ref, g.block((), at["c"]), lsem.at[0])]
+    for cp in here:
+        cp.start()
+    save = [pltpu.make_async_copy(xg, xg_out, lsem.at[4]), pltpu.make_async_copy(wbuf, wqkv_out, lsem.at[5]),
+            pltpu.make_async_copy(gbuf, gain_out, lsem.at[6]), pltpu.make_async_copy(qbuf, q_out, lsem.at[7])]
+    for cp in save:
+        cp.start()
+    for o in range(1, nzh):
+        dev, i = at_z(at, nz - 2 * o, nz)
+        landed(kvbuf.at[i], r_kv.at[0, o], dev)
+        log.push(kvbuf.at[i], kvbuf.at[i], s_kv.at[1, o], r_kv.at[1, o], other(at, "zl"))
+    for o in range(nzh):
+        landed(kvbuf.at[zi], r_kv.at[1, o], other(at, "zl"))
+    push_rest(1)
+    here[0].wait()
+    g.first()
+    save.append(pltpu.make_async_copy(kvbuf, kv_out, lsem.at[8]))
+    save[-1].start()
+    tl = kvbuf.shape[2]
+    for i in range(nz):
+        kn[i * tl:(i + 1) * tl, :] = jnp.transpose(kvbuf[i, :hd, :].astype(F32)).astype(BF)
+        vt[:hd, i * tl:(i + 1) * tl] = kvbuf[i, hd:, :]
+    vt[hd:, :] = jnp.ones((vt.shape[0] - hd, keys), BF)
+
+    def heads(b, lo, hi):
+        @pl.loop(lo, hi)
+        def _(h):
+            s = nn(kn[...], qbuf[h, :, b * qn:(b + 1) * qn]) + bias[b]
+            mx = jnp.max(s, axis=0, keepdims=True)
+            e = jnp.exp(s - mx).astype(BF)
+            oe = nn(vt[...], e)
+            tot = oe[hd:hd + 1]
+            obuf[h, :, b * qn:(b + 1) * qn] = (oe[:hd] / tot).astype(BF)
+            lbuf[h, :, b * qn:(b + 1) * qn] = mx + jnp.log(tot)
+
+    heads(0, 0, 4)
+    so.stage2(0)
+    for o in range(1, nrest):
+        so.stage1(o)
+    g.second()
+    heads(0, 4, 8)
+    for o in range(1, nrest):
+        so.stage2(o)
+    g.third()
+    push_rest(2)
+    heads(1, 0, 8)
+    for m in MASKS[1:4]:
+        g.complete(m)
+        g.pass_on(m)
+    for o in range(nrest):
+        so.finish(o)
+    save += [pltpu.make_async_copy(wobuf, wo_out, lsem.at[9]), pltpu.make_async_copy(obuf, o_out, lsem.at[10]),
+             pltpu.make_async_copy(lbuf, lse_out, lsem.at[11])]
+    for cp in save[-3:]:
+        cp.start()
+    cw = 512
+    nc = d // cw
+    oT = obuf[...].reshape(GROUP * hd, 4 * rows)
+    red = QuadSum(at, log, part, cin, xin, total, s_p, r_p, cw)
+    for n in range(nc):
+        s = slice(n * cw, (n + 1) * cw)
+        wo = wobuf[:, :, :, s].reshape(GROUP * hd, cw)
+        part[:, :, :, s] = tn(oT, wo).astype(BF).reshape(2, 2, rows, cw)
+        red.start(n)
+        if n:
+            red.middle(n - 1)
+    red.middle(nc - 1)
+    for m in MASKS[4:]:
+        g.complete(m)
+        g.pass_on(m)
+    for n in range(nc):
+        red.finish(n)
+    m_out[...] = total[...]
+    for m in MASKS:
+        g.sibling_arrived(m)
+    for k, (a, b) in enumerate(outs):
+        for o in range(1, nrest):
+            dev, _ = at_rest(at, nrest - o, nrest)
+            landed(b.at[o - 1], r_rest.at[k, o - 1], dev)
+    for cp in save:
+        cp.wait()
+
+    @pl.when(target != lin)
+    def _():
+        pltpu.make_async_remote_copy(wout_ref, wobuf.at[di, zi], s_od, r_od,
+                                     device_id=device_of(target, nz), device_id_type=MESH).wait_send()
+
+    g.close()
+    log.close()
+
+
+def attn(nz, ndp, tokens, wpack, w_out, gpack, cosT, sinT, starts, cot, wg, wu, wd):
     rows, d = tokens.shape
-    wrows = w_query.shape[0]
+    wr, wc = wpack.shape[1:]
+    hd = HEAD_DIM
+    units = wd.shape[0]
+    nrest = nz * ndp // 4
+    keys = nz * 4 * rows
+    qn = 2 * rows
+    vm = pl.BlockSpec(memory_space=pltpu.VMEM)
+    hbm = pl.BlockSpec(memory_space=pl.ANY)
+    dma = pltpu.SemaphoreType.DMA
+    sd = jax.ShapeDtypeStruct
+    sh = dict(
+        xg=(2, 2, rows, d), w=(ndp, nz, 4 * wr, wc), wo=(ndp, nz, wr, d), g=(ndp, nz, 4, 16, 128),
+        kv=(nz, 2 * hd, 4 * rows), q=(GROUP, hd, 4 * rows), lse=(GROUP, 1, 4 * rows))
+    outs = (sd((rows, d), F32), sd(sh["q"], BF), sd(sh["kv"], BF), sd(sh["q"], BF), sd(sh["lse"], F32), sd(sh["xg"], BF),
+            sd(sh["w"], BF), sd(sh["wo"], BF), sd(sh["g"], BF), sd((2, 2, 2, 2 * rows, d), BF)) + (sd((nrest - 1, units, d), BF),) * 3
+    nq = 4 * rows // qn
+    zz = (max(nrest - 1, 1),)
+    return pl.pallas_call(
+        functools.partial(attn_kernel, nz, ndp),
+        out_shape=outs,
+        in_specs=[vm] * 8 + [hbm] * 3,
+        out_specs=(vm,) + (hbm,) * (len(outs) - 1),
+        scratch_shapes=[
+            pltpu.VMEM(sh["xg"], BF), pltpu.VMEM(sh["w"], BF), pltpu.VMEM(sh["wo"], BF), pltpu.VMEM(sh["g"], BF),
+            pltpu.VMEM(sh["kv"], BF), pltpu.VMEM(sh["q"], BF), pltpu.VMEM((keys, hd), BF), pltpu.VMEM((hd + 16, keys), BF),
+            pltpu.VMEM(sh["q"], BF), pltpu.VMEM(sh["lse"], F32), pltpu.VMEM((nq, keys, qn), F32),
+            pltpu.VMEM((2, 2, rows, d), BF), pltpu.VMEM((2, rows, d), BF), pltpu.VMEM((rows, d), BF), pltpu.VMEM((rows, d), F32),
+            dma((12,)), dma((3,)), dma((3,)), dma((3,)), dma((3,))] + [dma(zz), dma(zz), dma((nrest, 6)), dma((nrest, 6))] * 3 + [
+            dma, dma, dma((3,)), dma((3,)), dma((2, nz // 2)), dma((2, nz // 2)), dma((2, 4)), dma((2, 4)),
+            dma((3,) + zz), dma((3,) + zz), dma((3, 8)), dma((3, 8)), dma((8,)), dma((8,)),
+        ],
+        compiler_params=pltpu.CompilerParams(collective_id=2, has_side_effects=True, vmem_limit_bytes=58 * 2**20),
+        name="attention",
+    )(tokens, wpack, w_out, gpack, cosT, sinT, starts, cot, wg, wu, wd)
+
+
+def back_kernel(nz, ndp, m_ref, dn2_ref, gain_ref, cot_ref, tok_ref, cos_ref, sin_ref, start_ref,
+                xg_in, wqkv_in, wo_in, q_in, kv_in, o_in, lse_in, gd_in, gg_in, gu_in,
+                dx_out, gq_out, gkv_out, gwo_out, gain_out, fd_out, fg_out, fu_out,
+                xg, wqkv, wo, qbuf, kvbuf, obuf, lbuf, dag, dob, delta, kn, vn, kt, bias, dkv, dqb, kvp, kvin, dqkv,
+                gob, go1, go2, gof, gqb, gq1, gq2, gqf, gkb, gk1, gk2, gkf, gsend, gpart, part, cin, xin, total, ogot, val, got,
+                lsem, s_x, r_x, s_o0, r_o0, s_o1, r_o1, s_q0, r_q0, s_q1, r_q1, s_k0, r_k0, s_k1, r_k1,
+                s_kv, r_kv, s_p, r_p, s_rest, r_rest, s_od, r_od, s_gq, r_gq, s_gk, r_gk, s_v, r_v):
+    at = place()
+    log = Log()
+    rows, d = m_ref.shape
+    hd = HEAD_DIM
+    qc = GROUP * hd
+    zi = at["zh"] * 2 + at["zl"]
+    di = at["dh"] * 2 + at["dl"]
+    t = at["x"] * 2 + at["c"]
+    nrest = nz * ndp // 4
+    npeers = nz * ndp
+    nzh = nz // 2
+    wr = gwo_out.shape[0]
+    keys = kn.shape[0]
+    tl = 4 * rows
+    lin = (di * nz + zi) * 4 + t
+    target = lax.rem(lin, npeers) * 4 + lin // npeers
+    source = lax.rem(lin, 4) * npeers + lin // 4
+    loads = [pltpu.make_async_copy(a, b, lsem.at[k]) for k, (a, b) in enumerate((
+        (kv_in, kvbuf), (wo_in, wo), (o_in, obuf), (q_in, qbuf), (lse_in, lbuf), (xg_in, xg), (wqkv_in, wqkv)))]
+    for cp in loads:
+        cp.start()
+    quad = (("c",), ("x",), ("x", "c"))
+    for f in quad:
+        signal(other(at, *f))
+    signal(other(at, "zl"))
+    signal(other(at, "dl"))
+    for o in range(1, nrest):
+        signal(at_rest(at, o, nrest)[0])
+
+    @pl.when(target != lin)
+    def _():
+        signal(device_of(target, nz))
+
+    m = m_ref[...]
+    inv2 = lax.rsqrt(jnp.mean(m * m, axis=1, keepdims=True) + NORM_EPS)
+    mh = m * inv2
+    dn2 = dn2_ref[...].astype(F32)
+    dy = dn2 * gain_ref[...]
+    dm = cot_ref[...].astype(F32) + inv2 * (dy - mh * jnp.mean(dy * mh, axis=1, keepdims=True))
+    dx_out[...] = dm
+    dag[at["x"], at["c"]] = dm.astype(BF)
+    total[...] = jnp.zeros_like(total)
+    gsum = jnp.sum(dn2 * mh, axis=0, keepdims=True)
+    for i in range(d // 128):
+        val[0, i:i + 1, :] = gsum[:, i * 128:(i + 1) * 128]
+    pl.semaphore_wait(pltpu.get_barrier_semaphore(), 4 + nrest + (source != lin).astype(jnp.int32))
+    qx = Quad(at, log, dag, s_x, r_x)
+    qx.start()
+    gs = AllSum(at, log, val, got, nrest, s_v, r_v)
+    gs.start(0)
+    fars = ((gd_in, fd_out), (gg_in, fg_out), (gu_in, fu_out))
+    units = fd_out.shape[1]
+    for k, (a, b) in enumerate(fars):
+        for o in range(1, nrest):
+            dev, _ = at_rest(at, nrest - o, nrest)
+            log.push(a.at[pl.ds(o * units, units), :], b.at[o - 1], s_rest.at[k, o - 1], r_rest.at[k, o - 1], dev)
+    loads[0].wait()
+    for i in range(nz):
+        kn[i * tl:(i + 1) * tl, :] = jnp.transpose(kvbuf[i, :hd, :].astype(F32)).astype(BF)
+        vn[i * tl:(i + 1) * tl, :] = jnp.transpose(kvbuf[i, hd:, :].astype(F32)).astype(BF)
+        kt[:, i * tl:(i + 1) * tl] = kvbuf[i, :hd, :]
+    kpos = lax.broadcasted_iota(jnp.int32, (keys, tl), 0)
+    qpos = zi * tl + lax.broadcasted_iota(jnp.int32, (1, tl), 1)
+    bias[...] = jnp.where((kpos >= start_ref[...]) & (kpos <= qpos), 0.0, MASKED)
+    dkv[...] = jnp.zeros_like(dkv)
+    for cp in loads[1:]:
+        cp.wait()
+    gs.take(0)
+    gs.start(1)
+    qx.forward()
+    qx.finish()
+    da = dag[...].reshape(tl, d)
+    doT = nt(wo[...].reshape(qc, d), da).astype(BF)
+    dob[...] = doT.reshape(GROUP, hd, tl)
+    delta[...] = jnp.sum((dob[...].astype(F32) * obuf[...].astype(F32)), axis=1, keepdims=True)
+    gs.take(1)
+    gs.start(2)
+    cw = 512
+    oT = obuf[...].reshape(qc, tl)
+    for n in range(d // cw):
+        s = slice(n * cw, (n + 1) * cw)
+        gob[:, :, :, s] = nn(oT, dag[:, :, :, s].reshape(tl, cw)).astype(BF).reshape(ndp, nz, wr, cw)
+    mo = Merge(at, log, gob, go1, go2, gof, nrest, ((0, d // 2, "dl", "zl"), (d // 2, d // 2, "zl", "dl")), (s_o0, r_o0, s_o1, r_o1))
+    far_first = tuple(range(1, nrest)) + (0,)
+    for o in far_first:
+        mo.stage1(o)
+
+    def heads(lo, hi):
+        @pl.loop(lo, hi)
+        def _(h):
+            qT, dT = qbuf[h], dob[h]
+            p = jnp.exp(nn(kn[...], qT) + bias[...] - lbuf[h])
+            ds = (p * (nn(vn[...], dT) - delta[h])).astype(BF)
+            pb = p.astype(BF)
+            dkv[:hd, :] += nt(qT, ds)
+            dkv[hd:, :] += nt(dT, pb)
+            dqb[pl.ds(pl.multiple_of(h * hd, hd), hd), :] = rot_rows(nn(kt[...], ds) * 0.125, cos_ref[...], -sin_ref[...])
+
+    heads(0, 3)
+    gs.take(2)
+    gs.start(3)
+    for o in far_first:
+        mo.stage2(o)
+    heads(3, 6)
+    gs.take(3)
+    gs.start(4)
+    for o in far_first:
+        mo.stage3(o)
+    heads(6, 8)
+    for i in range(nz):
+        kvp[i] = dkv[:, i * tl:(i + 1) * tl].astype(BF)
+    for o in range(1, nz):
+        dev, i = at_z(at, o, nz)
+        log.push(kvp.at[i], kvin.at[o - 1], s_kv.at[o - 1], r_kv.at[o - 1], dev)
+    dqkv[:, :qc] = jnp.transpose(dqb[...]).astype(BF)
+    mq = Merge(at, log, gqb, gq1, gq2, gqf, nrest, ((0, qc // 2, "dl", "zl"), (qc // 2, qc // 2, "zl", "dl")), (s_q0, r_q0, s_q1, r_q1))
+    mk = Merge(at, log, gkb, gk1, gk2, gkf, nrest, ((0, 2 * hd, "zl", "dl"),), (s_k0, r_k0, s_k1, r_k1))
+
+    def weight_grad(dst, lo, hi):
+        step = 256
+        per = step // (4 * wr)
+        for n in range(d // step):
+            xs = xg[:, :, :, n * step:(n + 1) * step].reshape(tl, step)
+            v = tn(xs, dqkv[:, lo:hi]).astype(BF)
+            for b in range(per):
+                f = n * per + b
+                dst[f // nz, f % nz] = v[b * 4 * wr:(b + 1) * 4 * wr]
+
+    weight_grad(gqb, 0, qc)
+    for o in far_first:
+        mq.stage1(o)
+    acc = dkv[:, pl.ds(pl.multiple_of(zi * tl, tl), tl)]
+    for o in range(1, nz):
+        dev, _ = at_z(at, nz - o, nz)
+        landed(kvin.at[o - 1], r_kv.at[o - 1], dev)
+        acc = acc + kvin[o - 1].astype(F32)
+    dk = rot_rows(acc[:hd], cos_ref[...], -sin_ref[...])
+    dqkv[:, qc:] = jnp.transpose(jnp.concatenate([dk, acc[hd:]], axis=0)).astype(BF)
+    weight_grad(gkb, qc, qc + 2 * hd)
+    for o in far_first:
+        mk.stage1(o)
+    red = QuadSum(at, log, part, cin, xin, total, s_p, r_p, cw)
+    w = wqkv[...].reshape(d, qc + 2 * hd)
+    nc = d // cw
+    for n in range(nc):
+        part[:, :, :, n * cw:(n + 1) * cw] = nt(dqkv[...], w[n * cw:(n + 1) * cw]).astype(BF).reshape(2, 2, rows, cw)
+        red.start(n)
+        if n:
+            red.middle(n - 1)
+    for o in far_first:
+        mq.stage2(o)
+    red.middle(nc - 1)
+    for o in far_first:
+        mk.stage2(o)
+    for o in far_first:
+        mq.stage3(o)
+    for o in far_first:
+        mk.stage3(o)
+    gsend[...] = mo.result().astype(BF)
+
+    @pl.when(source != lin)
+    def _():
+        pltpu.make_async_remote_copy(gsend, ogot, s_od, r_od, device_id=device_of(source, nz), device_id_type=MESH).start()
+
+    @pl.when(source == lin)
+    def _():
+        ogot[...] = gsend[...]
+
+    for n in range(nc):
+        red.finish(n)
+    x = tok_ref[...].astype(F32)
+    inv1 = lax.rsqrt(jnp.mean(x * x, axis=1, keepdims=True) + NORM_EPS)
+    xh = x * inv1
+    dy1 = total[...]
+    dx_out[...] = dx_out[...] + inv1 * (dy1 - xh * jnp.mean(dy1 * xh, axis=1, keepdims=True))
+    gain_out[...] = gs.take(4)
+    for merge, dst, sp, ss, rs, lo, hi in ((mq, gq_out, gpart.at[:, :qc], s_gq, r_gq, 0, qc), (mk, gkv_out, gpart.at[:, qc:], s_gk, r_gk, qc, qc + 2 * hd)):
+        gpart[:, lo:hi] = merge.result().astype(BF)
+        dst[t] = gpart[pl.ds(pl.multiple_of(t * wr, wr), wr), lo:hi]
+        for k, f in enumerate(quad):
+            dev = other(at, *f)
+            tt = dev[4] * 2 + dev[5]
+            log.push(gpart.at[pl.ds(pl.multiple_of(tt * wr, wr), wr), lo:hi], dst.at[t], ss.at[k], rs.at[k], dev)
+    @pl.when(target != lin)
+    def _():
+        pltpu.make_async_remote_copy(gsend, ogot, s_od, r_od, device_id=device_of(target, nz), device_id_type=MESH).wait_recv()
+
+    gwo_out[...] = ogot[...].astype(F32)
+    for dst, rs in ((gq_out, r_gq), (gkv_out, r_gk)):
+        for k, f in enumerate(quad):
+            dev = other(at, *f)
+            tt = dev[4] * 2 + dev[5]
+            landed(dst.at[tt], rs.at[k], dev)
+    for k, (a, b) in enumerate(fars):
+        for o in range(1, nrest):
+            dev, _ = at_rest(at, o, nrest)
+            landed(b.at[o - 1], r_rest.at[k, o - 1], dev)
+
+    @pl.when(source != lin)
+    def _():
+        pltpu.make_async_remote_copy(gsend, ogot, s_od, r_od, device_id=device_of(source, nz), device_id_type=MESH).wait_send()
+
+    log.close()
+
+
+def back(nz, ndp, m, dn2, gain, cot, tokens, cosT, sinT, starts, xg, wqkv, wo, q, kv, o, lse, grads):
+    rows, d = m.shape
+    hd = HEAD_DIM
+    qc = GROUP * hd
+    nrest = nz * ndp // 4
+    wr = wo.shape[2]
+    keys = nz * 4 * rows
+    tl = 4 * rows
+    units = grads[0].shape[0] // nrest
+    vm = pl.BlockSpec(memory_space=pltpu.VMEM)
+    hbm = pl.BlockSpec(memory_space=pl.ANY)
+    dma = pltpu.SemaphoreType.DMA
+    sd = jax.ShapeDtypeStruct
+    nf = max(nrest - 1, 1)
+    outs = (sd((rows, d), F32), sd((4, wr, qc), BF), sd((4, wr, 2 * hd), BF), sd((wr, d), F32), sd((16, 128), F32)) + (
+        sd((nrest - 1, units, d), BF),) * 3
+    V = pltpu.VMEM
+
+    def merge_bufs(r, c):
+        return [V((ndp, nz, r, c), BF), V((nrest, 2, r, c), BF), V((nrest, r, c), BF), V((nf, r, c), BF)]
+
+    return pl.pallas_call(
+        functools.partial(back_kernel, nz, ndp),
+        out_shape=outs,
+        in_specs=[vm] * 8 + [hbm] * 10,
+        out_specs=(vm,) * 5 + (hbm,) * 3,
+        scratch_shapes=[
+            V(xg.shape, BF), V(wqkv.shape, BF), V(wo.shape, BF), V(q.shape, BF), V(kv.shape, BF), V(o.shape, BF), V(lse.shape, F32),
+            V((2, 2, rows, d), BF), V(q.shape, BF), V(lse.shape, F32), V((keys, hd), BF), V((keys, hd), BF), V((hd, keys), BF),
+            V((keys, tl), F32), V((2 * hd, keys), F32), V((qc, tl), F32), V(kv.shape, BF), V((max(nz - 1, 1), 2 * hd, tl), BF),
+            V((tl, qc + 2 * hd), BF)]
+        + merge_bufs(wr, d) + merge_bufs(4 * wr, qc) + merge_bufs(4 * wr, 2 * hd) + [
+            V((wr, d), BF), V((4 * wr, qc + 2 * hd), BF), V((2, 2, rows, d), BF), V((2, rows, d), BF), V((rows, d), BF), V((rows, d), F32),
+            V((wr, d), BF), V((5, 16, 128), F32), V((4 + nf, 16, 128), F32),
+            dma((7,)), dma((3,)), dma((3,))] + [dma((nf,)), dma((nf,)), dma((nrest, 6)), dma((nrest, 6))] * 3 + [
+            dma((nz,)), dma((nz,)), dma((2, 4)), dma((2, 4)), dma((3, nf)), dma((3, nf)), dma, dma, dma((3,)), dma((3,)), dma((3,)), dma((3,)),
+            dma((4 + nf,)), dma((4 + nf,))],
+        compiler_params=pltpu.CompilerParams(collective_id=3, has_side_effects=True, vmem_limit_bytes=62 * 2**20),
+        name="backward",
+    )(m, dn2, gain, cot, tokens, cosT, sinT, starts, xg, wqkv, wo, q, kv, o, lse, *grads)
+
+
+def local(tokens, gain_attn, w_query, w_key, w_value, w_out, gain_mlp, w_gate_t, w_up_t, w_down, doc_ids, cotangent, nz, ndp):
+    rows, d = tokens.shape
+    wr = w_query.shape[0]
     grows = rows * 4
     seq_ids = doc_ids[0]
     length = seq_ids.shape[0]
-    t = lax.axis_index(T)
     zi = lax.axis_index(Z)
     hd = HEAD_DIM
     qc = GROUP * hd
-    gains = lax.all_gather(jnp.stack([gain_attn, gain_mlp]), AXES, axis=1, tiled=True).astype(F32)
-    ga, gm = gains[0], gains[1]
-    wall = jnp.concatenate([w_query.reshape(wrows, 4, qc), w_key.reshape(wrows, 4, hd), w_value.reshape(wrows, 4, hd)], axis=2).transpose(1, 0, 2)
-    wsl = lax.all_to_all(wall, T, 0, 0, tiled=True)
-    wqkv = lax.all_gather(wsl.reshape(4 * wrows, qc + 2 * hd), DP + Z, axis=0, tiled=True)
-    wo = lax.dynamic_slice_in_dim(lax.all_gather(w_out, AXES, axis=0, tiled=True), t * qc, qc, 0)
+    ga = gain_attn.astype(F32)[:, None]
+    wall = jnp.concatenate([w_query.reshape(wr, 4, qc), w_key.reshape(wr, 4, hd), w_value.reshape(wr, 4, hd)], axis=2).transpose(1, 0, 2)
+    wpack = (wall.astype(F32) * ga[None]).astype(BF)
+    gpack = jnp.pad(gain_mlp[None], ((0, 15), (0, 128 - wr)))
     first = zi * grows
     own_ids = lax.dynamic_slice_in_dim(seq_ids, first, grows, 0)
     qpos = first + jnp.arange(grows, dtype=jnp.int32)
-    kpos = jnp.arange(length, dtype=jnp.int32)
-    starts = jnp.sum((seq_ids[None, :] < own_ids[:, None]).astype(jnp.int32), axis=1)
+    starts = jnp.sum((seq_ids[:, None] < own_ids[None, :]).astype(jnp.int32), axis=0)
     freq = 10000.0 ** (-jnp.arange(hd // 2, dtype=F32) / (hd // 2))
-    ph = (qpos - starts).astype(F32)[:, None] * freq[None, :]
-    cos, sin = jnp.cos(ph), jnp.sin(ph)
-    allowed = (seq_ids[None, :] == own_ids[:, None]) & (kpos[None, :] <= qpos[:, None])
-    x = tokens.astype(F32)
-    inv1 = lax.rsqrt(jnp.mean(x * x, axis=-1, keepdims=True) + NORM_EPS)
-    n1 = (x * inv1 * ga).astype(BF)
-    n1g = lax.all_gather(n1, T, axis=0, tiled=True)
-    qkv = nn(n1g, wqkv)
-    q = rotate(qkv[:, :qc].reshape(grows, GROUP, hd), cos[:, None], sin[:, None], 1.0).astype(BF)
-    k = rotate(qkv[:, qc:qc + hd], cos, sin, 1.0).astype(BF)
-    v = qkv[:, qc + hd:].astype(BF)
-    kv = lax.all_gather(jnp.concatenate([k, v], axis=1), Z, axis=0, tiled=True)
-    ka, va = kv[:, :hd], kv[:, hd:]
-    scale = hd ** -0.5
-    qh = q.transpose(1, 0, 2)
-
-    def fwd(qq):
-        s = jnp.where(allowed, nt(qq, ka) * scale, MASKED)
-        mx = jnp.max(s, axis=1, keepdims=True)
-        e = jnp.exp(s - mx)
-        tot = jnp.sum(e, axis=1, keepdims=True)
-        return nn((e / tot).astype(BF), va), mx + jnp.log(tot)
-
-    o, lse = lax.map(fwd, qh)
-    o = o.transpose(1, 0, 2).reshape(grows, qc).astype(BF)
-    part = nn(o, wo).astype(BF)
-    m = x + lax.psum_scatter(part, T, scatter_dimension=0, tiled=True).astype(F32)
-    inv2 = lax.rsqrt(jnp.mean(m * m, axis=-1, keepdims=True) + NORM_EPS)
-    n2 = (m * inv2 * gm).astype(BF)
-    wgt = lax.all_gather(w_gate_t, REST, axis=0, tiled=True)
-    wut = lax.all_gather(w_up_t, REST, axis=0, tiled=True)
-    wdn = lax.all_gather(w_down, REST, axis=0, tiled=True)
-    cot_all = lax.all_gather(cotangent, CUBE, axis=0, tiled=True)
-    down, dn2, gwd, gwg, gwu = mlp(n2, cot_all, wgt, wut, wdn)
-    rs = lambda a: lax.psum_scatter(a, REST, scatter_dimension=0, tiled=True).astype(F32)
-    gwd, gwg, gwu = rs(gwd), rs(gwg), rs(gwu)
+    ph = (qpos - starts).astype(F32)[None, :] * freq[:, None]
+    cosT, sinT = jnp.cos(ph), jnp.sin(ph)
+    units = w_down.shape[0]
+    fill = -units % 16
+    if fill:
+        w_gate_t, w_up_t, w_down = (jnp.pad(w, ((0, fill), (0, 0))) for w in (w_gate_t, w_up_t, w_down))
+    m, q, kv, o, lse, xg, wqkv, wo, gains, cot_all, wgt, wut, wdn = attn(
+        nz, ndp, tokens, wpack, w_out, gpack, cosT, sinT, starts[None], cotangent, w_gate_t, w_up_t, w_down)
+    gm = gains[:, :, :, 0, :wr].reshape(1, d).astype(F32)
+    down, dn2, gwd, gwg, gwu = mlp(m, gm, cot_all, (w_gate_t, w_up_t, w_down), (wgt, wut, wdn))
+    dx, gq, gkv, gwo, gsum, fd, fg, fu = back(
+        nz, ndp, m, dn2, gm, cotangent, tokens, cosT, sinT, starts[None], xg, wqkv, wo, q, kv, o, lse, (gwd, gwg, gwu))
     block_out = (m + down.astype(F32)).astype(BF)
-    ggm = jnp.sum(dn2 * m * inv2, axis=0)
-    dy = dn2 * gm
-    dm = cotangent.astype(F32) + inv2 * (dy - m * (inv2 * inv2) * jnp.mean(dy * m, axis=-1, keepdims=True))
-    da = lax.all_gather(dm.astype(BF), T, axis=0, tiled=True)
-    do = nt(da, wo).astype(BF)
-    gwo = tn(o, da)
-    doh = do.reshape(grows, GROUP, hd).transpose(1, 0, 2)
-
-    def bwd(a):
-        qq, dd, ls = a
-        s = jnp.where(allowed, nt(qq, ka) * scale, MASKED)
-        p = jnp.exp(s - ls)
-        dp = nt(dd, va)
-        ds = (p * (dp - jnp.sum(p * dp, axis=1, keepdims=True))).astype(BF)
-        return nn(ds, ka) * scale, tn(ds, qq) * scale, tn(p.astype(BF), dd)
-
-    dq, dk, dv = lax.map(bwd, (qh, doh, lse))
-    dkv = jnp.concatenate([jnp.sum(dk, 0), jnp.sum(dv, 0)], axis=1).astype(BF)
-    dkv = lax.psum_scatter(dkv, Z, scatter_dimension=0, tiled=True).astype(F32)
-    dqr = rotate(dq.transpose(1, 0, 2), cos[:, None], sin[:, None], -1.0).reshape(grows, qc).astype(BF)
-    dkr = rotate(dkv[:, :hd], cos, sin, -1.0).astype(BF)
-    dqkv = jnp.concatenate([dqr, dkr, dkv[:, hd:].astype(BF)], axis=1)
-    gw = lax.psum_scatter(tn(n1g, dqkv).astype(BF), DP + Z, scatter_dimension=0, tiled=True)
-    gw = lax.all_to_all(gw.reshape(4, wrows, qc + 2 * hd), T, 0, 0, tiled=True).transpose(1, 0, 2).astype(F32)
-    gwq = gw[:, :, :qc].reshape(wrows, 4 * qc)
-    gwk = gw[:, :, qc:qc + hd].reshape(wrows, 4 * hd)
-    gwv = gw[:, :, qc + hd:].reshape(wrows, 4 * hd)
-    full = lax.dynamic_update_slice(jnp.zeros((4 * qc, d), BF), gwo.astype(BF), (t * qc, 0))
-    gwo = lax.psum_scatter(full, AXES, scatter_dimension=0, tiled=True).astype(F32)
-    dn1 = lax.psum_scatter(nt(dqkv, wqkv).astype(BF), T, scatter_dimension=0, tiled=True).astype(F32)
-    gga = jnp.sum(dn1 * x * inv1, axis=0)
-    dy1 = dn1 * ga
-    dx1 = inv1 * (dy1 - x * (inv1 * inv1) * jnp.mean(dy1 * x, axis=-1, keepdims=True))
-    gg = lax.psum_scatter(jnp.stack([gga, ggm]), AXES, scatter_dimension=1, tiled=True)
-    return block_out, dm + dx1, gg[0], gwq, gwk, gwv, gwo, gg[1], gwg, gwu, gwd
+
+    def own(a, far):
+        return (a[:units + fill].astype(F32) + jnp.sum(far.astype(F32), axis=0))[:units]
+
+    gw = jnp.concatenate([gq, gkv], axis=2).astype(F32)
+    gga = jnp.sum(gw * wall.astype(F32), axis=(0, 2))
+    gw = (gw * ga[None]).transpose(1, 0, 2)
+    gwq = gw[:, :, :qc].reshape(wr, 4 * qc)
+    gwk = gw[:, :, qc:qc + hd].reshape(wr, 4 * hd)
+    gwv = gw[:, :, qc + hd:].reshape(wr, 4 * hd)
+    ggm = lax.dynamic_slice_in_dim(gsum.reshape(d), lax.axis_index(AXES) * wr, wr, 0)
+    return block_out, dx, gga, gwq, gwk, gwv, gwo, ggm, own(gwg, fg), own(gwu, fu), own(gwd, fd)
 
 
 def solution(mesh):
@@ -489,7 +1185,7 @@
     vec = P(AXES)
     col = P(None, AXES)
     inner = jax.shard_map(
-        local, mesh=m6,
+        functools.partial(local, nz=seq // 4, ndp=dp), mesh=m6,
         in_specs=(row, vec, row, row, row, row, vec, row, row, row, P(DP, None), row),
         out_specs=(row, row, vec, row, row, row, row, vec, row, row, row),
         check_vma=False,

time: 1200 us -> 489 us (0.41)
  waiting for transfers between devices: 777 us -> 0 us
  Pallas kernels: 123 us -> 457 us
  matrix products: 114 us -> 0 us
  blocking collectives: 73.9 us -> 0 us
  other arithmetic: 47.1 us -> 12.3 us
  local copies, waits for them, and re-layouts: 27.9 us -> 11.7 us
  between operations: 16.9 us -> 1.05 us
    reduce_scatter x8 -> x0, waiting for transfers between devices: 397 us -> none  [the longest x1 143 us: local(): lax.psum_scatter(full, AXES, scatter_dimension=0, tiled=True).astype(F32)]
    pallas_call x0 -> x2, Pallas kernels: none -> 328 us  [the longest x1 164 us: back(): pl.pallas_call(functools.partial(back_kernel, nz, ndp), out_shape=outs, i...]
    all_gather x8 -> x0, waiting for transfers between devices: 251 us -> none  [the longest x1 52.4 us: local(): lax.all_gather(wsl.reshape(4 * wrows, qc + 2 * hd), DP + Z, axis=0, tiled...]
    unnamed x18 -> x0, waiting for transfers between devices: 129 us -> none
    dot_general x62 -> x0, matrix products: 114 us -> none  [the longest x26 49 us: nt(): lax.dot_general(a, b, (((1,), (1,)), ((), ())), preferred_element_type=F32)]
    all_gather x2 -> x0, blocking collectives: 61 us -> none  [the longest x1 42.9 us: local(): lax.all_gather(jnp.stack([gain_attn, gain_mlp]), AXES, axis=1, tiled=True)]
    reduce_sum x15 -> x1, other arithmetic: 17 us -> 1.25 us  [local(): jnp.sum((seq_ids[:, None] < own_ids[None, :]).astype(jnp.int32), axis=0)]
    all_to_all x1 -> x0, blocking collectives: 12.9 us -> none  [local(): wsl = lax.all_to_all(wall, T, 0, 0, tiled=True)]
  transfers between devices with their start and end apart: 18 -> 0, of which waited for: 17 -> 0; matrix products, arithmetic and copies ran while one was open for 6% -> 0% of each run, Pallas kernels for 0% -> 0%
where the time goes in v2:
time: 489 us; the launch traced here: 482 us
  Pallas kernels  457 us (93%)
  other arithmetic  12.3 us (3%)
  local copies, waits for them, and re-layouts  11.7 us (2%)
    pallas_call x1, Pallas kernels, back(): pl.pallas_call(functools.partial(back_kernel, nz, ndp), out_shape=outs, i...  164 us
    pallas_call x1, Pallas kernels, attn(): pl.pallas_call(functools.partial(attn_kernel, nz, ndp), out_shape=outs, i...  164 us
    pallas_call x1, Pallas kernels, mlp(): pl.pallas_call(mlp_kernel, out_shape=(jax.ShapeDtypeStruct((rows, d), BF)...  129 us

profile of v2, /device:TPU:1, one launch (start us, length us, event | category | flops | bytes accessed | tf_op | source)
XLA Modules:
  0.0 482.0 jit_solution(14896045546392163276)
XLA Ops:
  0.7 0.7 convert_element_type.53
  1.3 0.7 constant_dynamic-slice_fusion
  2.0 1.3 convert_reduce_fusion
  3.3 0.0 copy-start.9
  3.3 1.3 pad.4.gpack
  4.6 0.9 reshape.93
  5.4 0.9 reshape.94
  6.3 1.0 multiply_sine_fusion
  7.3 1.0 copy.38
  8.3 0.9 fusion.4.wpack
  9.1 0.0 copy-done.9
  9.1 163.8 %attention.1 = (f32[128,2048]{1,0:T(8,128)}, bf16[8,64,512]{2,1,0:T(8,128)(2,1)}, bf16[4,128,512]{2,1,0:T(8,128)(2,1)}, bf16[8,64,512]{2,1,0:T(8,128)(2,1)}, f32...) custom-call(bf16[128,2048]{1,0:T(8,128)(2,1)} %tok_ref.3, ...), custom_call_target="tpu_custom_call" | custom-call | tf_op jit(solution)/shard_map/attention/pallas_call | solution.py:863
  172.9 0.9 convert_reduce_fusion.1
  173.8 0.7 reshape.102.gain_ref
  174.5 129.1 %mlp.1 = (bf16[128,2048]{1,0:T(8,128)(2,1)}, f32[128,2048]{1,0:T(8,128)}, bf16[352,2048]{1,0:T(8,128)(2,1)}, bf16[352,2048]{1,0:T(8,128)(2,1)}, bf16[352,2048]{1,0:T(8,128)(2,1)}) custom-call(f32[128,2048]{1,0:T(8,128)} %get-tuple-element.37.m_ref, f32[1,2048]{1,0:T(1,128)} %reshape.102.gain_ref, bf16[2,2,2,256,2048]{4,3,2,1,0:T(8,128)(2,1)} %get-tuple-element.39.cot_ref, ...), custom_call_target="tpu_custom_call" | custom-call | flops 26575110144 | bytes 41943040 | tf_op jit(solution)/shard_map/mlp/pallas_call | solution.py:606
  303.6 0.0 copy-start
  303.6 0.0 copy-start.6
  303.6 164.0 %backward.1 = (f32[128,2048]{1,0:T(8,128)}, bf16[4,64,512]{2,1,0:T(8,128)(2,1)}, bf16[4,64,128]{2,1,0:T(8,128)(2,1)}, f32[64,2048]{1,0:T(8,128)}, f32[16,128]{1,...) custom-call(f32[128,2048]{1,0:T(8,128)} %get-tuple-element.37.m_ref, ...), custom_call_target="tpu_custom_call" | custom-call | tf_op jit(solution)/shard_map/backward/pallas_call | solution.py:1115
  467.7 0.0 copy-start.3
  467.7 0.0 copy-done
  467.7 0.0 copy-done.6
  467.7 0.9 add_convert_fusion
  468.6 0.6 copy-done.3
  469.2 0.0 copy-start.1
  469.2 0.0 copy-start.2
  469.2 2.5 fusion.1
  471.8 1.3 dynamic_slice.7
  473.0 0.0 copy-done.1
  473.0 0.0 copy-done.2
  473.0 0.0 copy-start.7
  473.0 0.0 copy-start.8
  473.0 3.5 convert_add_fusion
  476.5 0.0 copy-done.7
  476.5 0.0 copy-done.8
  476.5 0.7 fusion.3
  477.2 0.1 fusion.5
  477.3 0.0 copy-start.4
  477.4 0.1 slice_bitcast_fusion
  477.4 0.8 copy.36
  478.3 0.1 copy.34
  478.3 0.0 copy-start.5
  478.4 0.8 reshape.100
  479.1 0.1 copy.33
  479.2 0.8 reshape.99
  480.0 0.0 copy-done.4
  480.0 1.0 copy.41
  480.9 0.0 copy-done.5
  481.0 0.8 copy.42
  (4 shorter events, 0.0 us)
Async XLA Ops:
  3.3 5.8 %copy-start.9 = (s32[512]{0:T(512)}, s32[512]{0:T(512)S(1)}, u32[]{:S(2)}) copy-start(s32[512]{0:T(512)S(1)} %convert_reduce_fusion) | copy-start | bytes 6148
  303.6 164.0 %copy-start = (f32[128,2048]{1,0:T(8,128)S(1)}, f32[128,2048]{1,0:T(8,128)}, u32[]{:S(2)}) copy-start(f32[128,2048]{1,0:T(8,128)} %get-tuple-element.37.m_ref) | copy-start | bytes 3145732
  303.6 164.0 %copy-start.6 = (bf16[128,2048]{1,0:T(8,128)(2,1)S(1)}, bf16[128,2048]{1,0:T(8,128)(2,1)}, u32[]{:S(2)}) copy-start(bf16[128,2048]{1,0:T(8,128)(2,1)} %get-tuple-element.43) | copy-start | bytes 1572868
  467.7 1.6 copy-start.3
  469.2 3.8 copy-start.1
  469.2 3.8 copy-start.2
  473.0 3.5 copy-start.7
  473.0 3.5 copy-start.8
  477.3 2.6 copy-start.4
  478.3 2.6 copy-start.5

commit v3 on v2

--- a/solution.py
+++ b/solution.py
@@ -69,8 +69,7 @@
     return tuple(1 - at[a] if a in mask else at[a] for a in ("dl", "zl", "x"))
 
 
-def order_of(p):
-    return tuple(CDIMS[(p + s) % 3] for s in range(3))
+ORDERS = tuple(tuple(CDIMS[(p + s) % 3] for s in range(3)) for p in range(3))
 
 
 class Log:
@@ -307,6 +306,22 @@
         return total
 
 
+class Pushes:
+    def __init__(self, at, log, nrest, src, dst, ssem, rsem, back):
+        self.args = at, log, nrest, src, dst, ssem, rsem, back
+
+    def start(self):
+        at, log, n, src, dst, ssem, rsem, back = self.args
+        for o in range(1, n):
+            dev, _ = at_rest(at, n - o if back else o, n)
+            log.push(src(o), dst.at[o - 1], ssem.at[o - 1], rsem.at[o - 1], dev)
+
+    def finish(self):
+        at, log, n, src, dst, ssem, rsem, back = self.args
+        for o in range(1, n):
+            landed(dst.at[o - 1], rsem.at[o - 1], at_rest(at, o if back else n - o, n)[0])
+
+
 class Gather:
     def __init__(self, at, buf, ssem, rsem, csend, crecv):
         self.at, self.buf, self.ssem, self.rsem, self.csend, self.crecv = at, buf, ssem, rsem, csend, crecv
@@ -351,37 +366,37 @@
 
     def first(self):
         for p in range(3):
-            self.send(p, (), order_of(p)[0])
+            self.send(p, (), ORDERS[p][0])
         self.pass_on(())
 
     def second(self):
         for p in range(3):
-            a, b, _ = order_of(p)
+            a, b, _ = ORDERS[p]
             self.send(p, (), b)
         for p in range(3):
-            a, b, _ = order_of(p)
+            a, b, _ = ORDERS[p]
             self.arrived(p, (a,))
             self.send(p, (a,), b)
 
     def third(self):
         for p in range(3):
-            a, b, c = order_of(p)
+            a, b, c = ORDERS[p]
             self.send(p, (), c)
         for p in range(3):
-            a, b, c = order_of(p)
+            a, b, c = ORDERS[p]
             self.send(p, (a,), c)
         for p in range(3):
-            a, b, c = order_of(p)
+            a, b, c = ORDERS[p]
             self.arrived(p, (b,))
             self.send(p, (b,), c)
         for p in range(3):
-            a, b, c = order_of(p)
+            a, b, c = ORDERS[p]
             self.arrived(p, mask_sorted((a, b)))
             self.send(p, mask_sorted((a, b)), c)
 
     def complete(self, mask):
         for p in range(3):
-            if order_of(p)[2] in mask:
+            if ORDERS[p][2] in mask:
                 self.arrived(p, mask)
 
     def close(self):
@@ -400,10 +415,12 @@
     def __init__(self, at, full, core_in, r0, r1, r2, ssem, rsem):
         self.at, self.full, self.core_in, self.r = at, full, core_in, (r0, r1, r2)
         self.ssem, self.rsem = ssem, rsem
-        self.rows = full.shape[3] // 2
+        self.rows = r2.shape[0]
         self.open = []
 
     def own(self, core):
+        if self.full.shape[3] == self.rows:
+            return slice(None)
         return pl.ds(pl.multiple_of(core * self.rows, self.rows), self.rows)
 
     def core_copy(self, p):
@@ -414,7 +431,7 @@
 
     def stage_copy(self, p, s):
         lo, w = PARTS[p]
-        dims = order_of(p)
+        dims = ORDERS[p]
         ix = []
         for a in ("dl", "zl", "x"):
             if a == dims[s]:
@@ -434,7 +451,7 @@
         self.open.append(cp)
 
     def blocks(self, p, s):
-        dims = order_of(p)
+        dims = ORDERS[p]
         rest = dims[s:]
         out = []
         for m in MASKS:
@@ -444,17 +461,17 @@
             out.sort(key=lambda m: 0 if rest[0] in m else 1)
         return out
 
-    def add_core(self, p):
-        lo, w = PARTS[p]
+    def add_core(self, p, go=True):
         cp = self.core_copy(p)
         cp.wait_recv()
         self.add_loop(p, 0, None)
-        self.start(self.stage_copy(p, 0))
+        if go:
+            self.start(self.stage_copy(p, 0))
         self.add_loop(p, 0, None, tail=True)
 
     def add_loop(self, p, s, src, tail=False):
         lo, w = PARTS[p]
-        dims = order_of(p)
+        dims = ORDERS[p]
         for m in self.blocks(p, s):
             first = s < 3 and dims[s] in m
             if first == tail:
@@ -475,67 +492,90 @@
             self.start(self.stage_copy(p, s + 1))
             self.add_loop(p, s + 1, self.r[s], tail=True)
 
-    def finish(self, p, out):
+    def finish(self, p, out, base=None):
         lo, w = PARTS[p]
         self.stage_copy(p, 2).wait_recv()
         i = cube_index(self.at, ())
         ref = self.full.at[i[0], i[1], i[2], self.own(self.at["c"]), lo:lo + w]
-        out[:, lo:lo + w] = (ref[...].astype(F32) + self.r[2][:, lo:lo + w].astype(F32)).astype(out.dtype)
+        total = ref[...].astype(F32) + self.r[2][:, lo:lo + w].astype(F32)
+        if base is not None:
+            total = total + base[:, lo:lo + w]
+        out[:, lo:lo + w] = total.astype(out.dtype)
 
     def close(self):
         for cp in self.open:
             cp.wait_send()
 
 
-def mlp_kernel(m_ref, gain_ref, cot_ref, wg_own, wu_own, wd_own, wg_far, wu_far, wd_far, down_out, dn2_out, gwd_out, gwg_out, gwu_out,
-               rows, wgu, wd_ref, zb, dgu, fa, fb, core_in, a0, a1, a2, b0, b1, b2,
-               lsem, gs, gr, gcs, gcr, sas, sar, sbs, sbr, credit):
+def mlp_kernel(nrest, m_ref, gain_ref, cot_ref, wg_own, wu_own, wd_own, wg_far, wu_far, down_out, dn2_out, gwd_out, gwg_out, gwu_out, fd_out,
+               rows, wgu, wd, gus, zb, dgu, fa, fb, core_in, a0, a1, a2,
+               lsem, gs, gr, gcs, gcr, sas, sar, sbs, sbr, s_wd, r_wd, s_fd, r_fd, credit):
     at = place()
-    units = wd_ref.shape[0]
+    log = Log()
+    units = wd.shape[0]
     brows = m_ref.shape[0]
     part = wd_own.shape[0]
-    copies = []
-    for k, (own_w, far_w, dst, lo) in enumerate(((wg_own, wg_far, wgu, 0), (wu_own, wu_far, wgu, units), (wd_own, wd_far, wd_ref, 0))):
-        copies.append(pltpu.make_async_copy(own_w, dst.at[lo:lo + part, :], lsem.at[2 * k]))
-        copies.append(pltpu.make_async_copy(far_w, dst.at[lo + part:lo + units, :], lsem.at[2 * k + 1]))
+    far = units - part
+    copies = [pltpu.make_async_copy(wd_own, wd.at[:part, :], lsem.at[4])]
+    for k, (own_w, far_w, lo) in enumerate(((wg_own, wg_far, 0), (wu_own, wu_far, units))):
+        copies.append(pltpu.make_async_copy(own_w, wgu.at[lo:lo + part, :], lsem.at[2 * k]))
+        copies.append(pltpu.make_async_copy(far_w, wgu.at[lo + part:lo + units, :], lsem.at[2 * k + 1]))
     for cp in copies:
         cp.start()
-    greet(at, (("c",), ("x",), ("zl",), ("dl",)))
+    for flip in ("c", "x", "zl", "dl"):
+        signal(other(at, flip))
+    for o in range(1, nrest):
+        signal(at_rest(at, o, nrest)[0])
     g = Gather(at, rows, gs, gr, gcs, gcr)
     own = pl.ds(pl.multiple_of(at["c"] * brows, brows), brows)
     m = m_ref[...]
     inv = lax.rsqrt(jnp.mean(m * m, axis=1, keepdims=True) + NORM_EPS)
     rows[at["dl"], at["zl"], at["x"], own, :] = (m * inv * gain_ref[...]).astype(BF)
+    pl.semaphore_wait(pltpu.get_barrier_semaphore(), 3 + nrest)
     g.first()
+    for o in range(1, nrest):
+        log.push(wd_own, wd.at[o * part:(o + 1) * part, :], s_wd.at[o - 1], r_wd.at[o - 1], at_rest(at, o, nrest)[0])
     for cp in copies:
         cp.wait()
 
+    def swiglu(i, gate, up, dz, lo, hi):
+        sg = jax.nn.sigmoid(gate)
+        sl = gate * sg
+        zb[i[0], i[1], i[2], lo:hi, :] = (sl * up).astype(BF)
+        dgu[i[0], i[1], i[2], lo:hi, :] = (dz * up * (sg * (1.0 + gate * (1.0 - sg)))).astype(BF)
+        dgu[i[0], i[1], i[2], units + lo:units + hi, :] = (dz * sl).astype(BF)
+
     def units_of(mask):
         i = cube_index(at, mask)
-        r = rows[i[0], i[1], i[2]]
-        gu = nt(wgu[...], r)
-        dz = nt(wd_ref[...], cot_ref[i[0], i[1], i[2]])
+        gu = nt(wgu[...], rows[i[0], i[1], i[2]])
+        dz = nt(wd[:part, :], cot_ref[i[0], i[1], i[2]])
         gate, up = gu[:units], gu[units:]
-        sg = jax.nn.sigmoid(gate)
-        sl = gate * sg
-        zb[i[0], i[1], i[2]] = (sl * up).astype(BF)
-        dgu[i[0], i[1], i[2], :units, :] = (dz * up * (sg * (1.0 + gate * (1.0 - sg)))).astype(BF)
-        dgu[i[0], i[1], i[2], units:, :] = (dz * sl).astype(BF)
+        gus[i[0], i[1], i[2], :far, :] = gate[part:]
+        gus[i[0], i[1], i[2], far:, :] = up[part:]
+        swiglu(i, gate[:part], up[:part], dz, 0, part)
 
     g.second()
     g.sibling_arrived(())
     units_of(())
     g.third()
     last = None
-    for m in MASKS[1:]:
-        g.complete(m)
-        g.pass_on(m)
+    for k in MASKS[1:]:
+        g.complete(k)
+        g.pass_on(k)
         if last is not None:
             g.sibling_arrived(last)
             units_of(last)
-        last = m
+        last = k
     g.sibling_arrived(last)
     units_of(last)
+    for o in range(1, nrest):
+        landed(wd.at[o * part:(o + 1) * part, :], r_wd.at[o - 1], at_rest(at, nrest - o, nrest)[0])
+
+    @pl.loop(0, 8)
+    def _(q):
+        i = (q // 4, (q // 2) % 2, q % 2)
+        dz = nt(wd[part:, :], cot_ref[i[0], i[1], i[2]])
+        swiglu(i, gus[i[0], i[1], i[2], :far, :], gus[i[0], i[1], i[2], far:, :], dz, part, units)
 
     def partial(dst, lhs, rhs, p):
         lo, w = PARTS[p]
@@ -545,8 +585,22 @@
             a, b, c = q // 4, (q // 2) % 2, q % 2
             dst[a, b, c, :, lo:lo + w] = tn(lhs[a, b, c], rhs[:, lo:lo + w]).astype(BF)
 
+    cw = 512
+
+    def grads(lhs, rhs, outs):
+        @pl.loop(0, rows.shape[4] // cw)
+        def _(n):
+            s = pl.ds(pl.multiple_of(n * cw, cw), cw)
+            acc = None
+            for q in range(8):
+                a, b, c = q // 4, (q // 2) % 2, q % 2
+                v = nn(lhs[a, b, c], rhs[a, b, c, :, s])
+                acc = v if acc is None else acc + v
+            for k, o in enumerate(outs):
+                o[:, s] = acc[k * units:(k + 1) * units].astype(BF)
+
     sa = Scatter(at, fa, core_in, a0, a1, a2, sas, sar)
-    sb = Scatter(at, fb, core_in, b0, b1, b2, sbs, sbr)
+    sb = Scatter(at, fb, core_in, a0, a1, a2, sbs, sbr)
     for p in range(3):
         partial(fa, dgu, wgu, p)
         sa.start(sa.core_copy(p))
@@ -554,77 +608,66 @@
             sa.add_core(p - 1)
     sa.add_core(2)
     pl.semaphore_signal(credit, inc=1, device_id=other(at, "c"), device_id_type=MESH)
-    for p in range(3):
-        partial(fb, zb, wd_ref, p)
+    grads(zb, cot_ref, (gwd_out,))
+    for o in range(1, nrest):
+        log.push(gwd_out.at[o * part:(o + 1) * part, :], fd_out.at[o - 1], s_fd.at[o - 1], r_fd.at[o - 1], at_rest(at, nrest - o, nrest)[0])
+    partial(fb, zb, wd, 0)
     for p in range(3):
         sa.step(p, 0)
     pl.semaphore_wait(credit, 1)
-    for p in range(3):
+    sb.start(sb.core_copy(0))
+    for p in range(1, 3):
+        partial(fb, zb, wd, p)
         sb.start(sb.core_copy(p))
-    cw = 512
-
-    def grads(lhs_list):
-        @pl.loop(0, rows.shape[4] // cw)
-        def _(n):
-            s = pl.ds(pl.multiple_of(n * cw, cw), cw)
-            for lhs, rhs, outs in lhs_list:
-                acc = None
-                for q in range(8):
-                    a, b, c = q // 4, (q // 2) % 2, q % 2
-                    v = nn(lhs[a, b, c], rhs[a, b, c, :, s])
-                    acc = v if acc is None else acc + v
-                for k, o in enumerate(outs):
-                    o[:, s] = acc[k * units:(k + 1) * units].astype(BF)
-
-    for p in range(3):
-        sb.add_core(p)
     for p in range(3):
         sa.step(p, 1)
-    grads([(zb, cot_ref, (gwd_out,))])
+    for p in range(3):
+        sb.add_core(p, go=False)
+    save = pltpu.make_async_copy(fb.at[:, :, :, own, :], down_out, lsem.at[5])
+    save.start()
     for p in range(3):
         sa.finish(p, dn2_out)
-    grads([(dgu, rows, (gwg_out, gwu_out))])
-    for p in range(3):
-        sb.step(p, 0)
-    for p in range(3):
-        sb.step(p, 1)
-    for p in range(3):
-        sb.finish(p, down_out)
+    grads(dgu, rows, (gwg_out, gwu_out))
+    save.wait()
+    for o in range(1, nrest):
+        landed(fd_out.at[o - 1], r_fd.at[o - 1], at_rest(at, o, nrest)[0])
     g.close()
     sa.close()
     sb.close()
-
-
-def mlp(m, gain, cot_all, own, far):
+    log.close()
+
+
+def mlp(nrest, m, gain, cot_all, own, far):
     rows, d = m.shape
     far = tuple(a.reshape(-1, d) for a in far)
-    units = own[0].shape[0] + far[0].shape[0]
+    part = own[0].shape[0]
+    units = part * nrest
     vm = pl.BlockSpec(memory_space=pltpu.VMEM)
     hbm = pl.BlockSpec(memory_space=pl.ANY)
     cube = (2, 2, 2)
     dma = pltpu.SemaphoreType.DMA
+    sd = jax.ShapeDtypeStruct
+    nf = max(nrest - 1, 1)
     return pl.pallas_call(
-        mlp_kernel,
-        out_shape=(jax.ShapeDtypeStruct((rows, d), BF), jax.ShapeDtypeStruct((rows, d), F32))
-        + (jax.ShapeDtypeStruct((units, d), BF),) * 3,
-        in_specs=[vm, vm, vm] + [hbm] * 6,
-        out_specs=(vm,) * 5,
+        functools.partial(mlp_kernel, nrest),
+        out_shape=(sd(cube + (rows, d), BF), sd((rows, d), F32)) + (sd((units, d), BF),) * 3 + (sd((nrest - 1, part, d), BF),),
+        in_specs=[vm, vm, vm] + [hbm] * 5,
+        out_specs=(hbm,) + (vm,) * 4 + (hbm,),
         scratch_shapes=[
             pltpu.VMEM(cube + (2 * rows, d), BF),
             pltpu.VMEM((2 * units, d), BF),
             pltpu.VMEM((units, d), BF),
+            pltpu.VMEM(cube + (2 * (units - part), 2 * rows), F32),
             pltpu.VMEM(cube + (units, 2 * rows), BF),
             pltpu.VMEM(cube + (2 * units, 2 * rows), BF),
             pltpu.VMEM(cube + (2 * rows, d), BF),
             pltpu.VMEM(cube + (2 * rows, d), BF),
             pltpu.VMEM(cube + (rows, d), BF),
             pltpu.VMEM((2, 2, rows, d), BF), pltpu.VMEM((2, rows, d), BF), pltpu.VMEM((rows, d), BF),
-            pltpu.VMEM((2, 2, rows, d), BF), pltpu.VMEM((2, rows, d), BF), pltpu.VMEM((rows, d), BF),
             dma((6,)), dma((3, 8)), dma((3, 8)), dma((8,)), dma((8,)),
-            dma((3, 4)), dma((3, 4)), dma((3, 4)), dma((3, 4)), pltpu.SemaphoreType.REGULAR,
+            dma((3, 4)), dma((3, 4)), dma((3, 4)), dma((3, 4)), dma((nf,)), dma((nf,)), dma((nf,)), dma((nf,)), pltpu.SemaphoreType.REGULAR,
         ],
         compiler_params=pltpu.CompilerParams(collective_id=1, has_side_effects=True, vmem_limit_bytes=63 * 2**20),
-        cost_estimate=pl.CostEstimate(flops=18 * 16 * rows * d * units, bytes_accessed=40 * 2**20, transcendentals=16 * rows * units),
         name="mlp",
     )(m, gain, cot_all, *own, *far)
 
@@ -635,8 +678,8 @@
     return jnp.concatenate([a * cos - b * sin, b * cos + a * sin], axis=0)
 
 
-def attn_kernel(nz, ndp, tok_ref, wpack, wout_ref, gpack, cos_ref, sin_ref, start_ref, cot_ref, wg_ref, wu_ref, wd_ref,
-                m_out, q_out, kv_out, o_out, lse_out, xg_out, wqkv_out, wo_out, gain_out, cot_out, wg_out, wu_out, wd_out,
+def attn_kernel(nz, ndp, tok_ref, wpack, wout_ref, gpack, cos_ref, sin_ref, start_ref, cot_ref, wg_ref, wu_ref,
+                m_out, q_out, kv_out, o_out, lse_out, xg_out, wqkv_out, wo_out, gain_out, cot_out, wg_out, wu_out,
                 xg, wbuf, wobuf, gbuf, kvbuf, qbuf, kn, vt, obuf, lbuf, bias, part, cin, xin, total,
                 lsem, s_disp, r_disp, s_gd, r_gd, s_w0, r_w0, s_w1, r_w1, s_g0, r_g0, s_g1, r_g1, s_o0, r_o0, s_o1, r_o1,
                 s_od, r_od, s_x, r_x, s_kv, r_kv, s_p, r_p, s_rest, r_rest, gs, gr, gcs, gcr):
@@ -666,6 +709,10 @@
         signal(device_of(source, nz))
 
     pl.semaphore_wait(pltpu.get_barrier_semaphore(), 4 + nrest + (target != lin).astype(jnp.int32))
+    g = Gather(at, cot_out, gs, gr, gcs, gcr)
+    here = [pltpu.make_async_copy(cot_ref, g.block((), at["c"]), lsem.at[0])]
+    for cp in here:
+        cp.start()
     for k, f in enumerate(quad):
         dev = other(at, *f)
         tt = dev[4] * 2 + dev[5]
@@ -684,14 +731,14 @@
         tt = dev[4] * 2 + dev[5]
         landed(wbuf.at[di, zi, pl.ds(pl.multiple_of(tt * wr, wr), wr), :], r_disp.at[k], dev)
         landed(gbuf.at[di, zi, tt], r_gd.at[k], dev)
-    half = 128 * (wbuf.shape[3] // 256)
-    sw = Spread(at, log, wbuf, nrest, ((0, half, "dl", "zl"), (half, wbuf.shape[3] - half, "zl", "dl")), (s_w0, r_w0, s_w1, r_w1))
+    sw = Spread(at, log, wbuf, nrest, ((0, wbuf.shape[3], "zl", "dl"),), (s_w0, r_w0, s_w1, r_w1))
     sg = Spread(at, log, gbuf, nrest, ((0, 128, "zl", "dl"),), (s_g0, r_g0, s_g1, r_g1))
-    so = Spread(at, log, wobuf, nrest, ((0, d // 2, "dl", "zl"), (d // 2, d // 2, "zl", "dl")), (s_o0, r_o0, s_o1, r_o1))
+    so = Spread(at, log, wobuf, nrest, ((0, d, "zl", "dl"),), (s_o0, r_o0, s_o1, r_o1))
     for sp in (sw, sg):
         sp.start()
         sp.stage1(0)
     qx.forward()
+    here[0].wait()
     @pl.when(target != lin)
     def _():
         pltpu.make_async_remote_copy(wout_ref, wobuf.at[lax.rem(lin, npeers) // nz, lax.rem(lax.rem(lin, npeers), nz)], s_od, r_od,
@@ -714,21 +761,22 @@
     for o in range(1, nrest):
         for sp in (sw, sg):
             sp.stage1(o)
-    outs = ((wg_ref, wg_out), (wu_ref, wu_out), (wd_ref, wd_out))
-
-    def push_rest(k):
-        a, b = outs[k]
-        for o in range(1, nrest):
-            dev, _ = at_rest(at, o, nrest)
-            log.push(a, b.at[o - 1], s_rest.at[k, o - 1], r_rest.at[k, o - 1], dev)
-
-    push_rest(0)
+    swaps = [Pushes(at, log, nrest, (lambda o, a=a: a), b, s_rest.at[k], r_rest.at[k], False)
+             for k, (a, b) in enumerate(((wg_ref, wg_out), (wu_ref, wu_out)))]
     for o in range(1, nrest):
         for sp in (sw, sg):
             sp.stage2(o)
+    @pl.when(source != lin)
+    def _():
+        pltpu.make_async_remote_copy(wobuf.at[di, zi], wobuf.at[di, zi], s_od, r_od,
+                                     device_id=device_of(source, nz), device_id_type=MESH).wait_recv()
+
+    so.start()
+    so.stage1(0)
     for o in range(nrest):
         for sp in (sw, sg):
             sp.finish(o)
+    g.first()
     qx.finish()
     xa = xg[...].reshape(4 * rows, d)
     qkv = jnp.transpose(nn(xa, wbuf[...].reshape(d, wbuf.shape[3])))
@@ -742,17 +790,6 @@
     for h in range(GROUP):
         qbuf[h] = (rot_rows(qkv[h * hd:(h + 1) * hd], cos, sin).astype(BF) * 0.125).astype(BF)
 
-    @pl.when(source != lin)
-    def _():
-        pltpu.make_async_remote_copy(wobuf.at[di, zi], wobuf.at[di, zi], s_od, r_od,
-                                     device_id=device_of(source, nz), device_id_type=MESH).wait_recv()
-
-    so.start()
-    so.stage1(0)
-    g = Gather(at, cot_out, gs, gr, gcs, gcr)
-    here = [pltpu.make_async_copy(cot_ref, g.block((), at["c"]), lsem.at[0])]
-    for cp in here:
-        cp.start()
     save = [pltpu.make_async_copy(xg, xg_out, lsem.at[4]), pltpu.make_async_copy(wbuf, wqkv_out, lsem.at[5]),
             pltpu.make_async_copy(gbuf, gain_out, lsem.at[6]), pltpu.make_async_copy(qbuf, q_out, lsem.at[7])]
     for cp in save:
@@ -763,9 +800,9 @@
         log.push(kvbuf.at[i], kvbuf.at[i], s_kv.at[1, o], r_kv.at[1, o], other(at, "zl"))
     for o in range(nzh):
         landed(kvbuf.at[zi], r_kv.at[1, o], other(at, "zl"))
-    push_rest(1)
-    here[0].wait()
-    g.first()
+    g.second()
+    swaps[0].start()
+    swaps[1].start()
     save.append(pltpu.make_async_copy(kvbuf, kv_out, lsem.at[8]))
     save[-1].start()
     tl = kvbuf.shape[2]
@@ -785,17 +822,16 @@
             obuf[h, :, b * qn:(b + 1) * qn] = (oe[:hd] / tot).astype(BF)
             lbuf[h, :, b * qn:(b + 1) * qn] = mx + jnp.log(tot)
 
-    heads(0, 0, 4)
     so.stage2(0)
     for o in range(1, nrest):
         so.stage1(o)
-    g.second()
+    heads(0, 0, 4)
+    g.third()
     heads(0, 4, 8)
     for o in range(1, nrest):
         so.stage2(o)
-    g.third()
-    push_rest(2)
-    heads(1, 0, 8)
+    heads(1, 0, 4)
+    heads(1, 4, 8)
     for m in MASKS[1:4]:
         g.complete(m)
         g.pass_on(m)
@@ -825,10 +861,8 @@
     m_out[...] = total[...]
     for m in MASKS:
         g.sibling_arrived(m)
-    for k, (a, b) in enumerate(outs):
-        for o in range(1, nrest):
-            dev, _ = at_rest(at, nrest - o, nrest)
-            landed(b.at[o - 1], r_rest.at[k, o - 1], dev)
+    for sw_ in swaps:
+        sw_.finish()
     for cp in save:
         cp.wait()
 
@@ -841,11 +875,11 @@
     log.close()
 
 
-def attn(nz, ndp, tokens, wpack, w_out, gpack, cosT, sinT, starts, cot, wg, wu, wd):
+def attn(nz, ndp, tokens, wpack, w_out, gpack, cosT, sinT, starts, cot, wg, wu):
     rows, d = tokens.shape
     wr, wc = wpack.shape[1:]
     hd = HEAD_DIM
-    units = wd.shape[0]
+    units = wg.shape[0]
     nrest = nz * ndp // 4
     keys = nz * 4 * rows
     qn = 2 * rows
@@ -857,35 +891,35 @@
         xg=(2, 2, rows, d), w=(ndp, nz, 4 * wr, wc), wo=(ndp, nz, wr, d), g=(ndp, nz, 4, 16, 128),
         kv=(nz, 2 * hd, 4 * rows), q=(GROUP, hd, 4 * rows), lse=(GROUP, 1, 4 * rows))
     outs = (sd((rows, d), F32), sd(sh["q"], BF), sd(sh["kv"], BF), sd(sh["q"], BF), sd(sh["lse"], F32), sd(sh["xg"], BF),
-            sd(sh["w"], BF), sd(sh["wo"], BF), sd(sh["g"], BF), sd((2, 2, 2, 2 * rows, d), BF)) + (sd((nrest - 1, units, d), BF),) * 3
+            sd(sh["w"], BF), sd(sh["wo"], BF), sd(sh["g"], BF), sd((2, 2, 2, 2 * rows, d), BF)) + (sd((nrest - 1, units, d), BF),) * 2
     nq = 4 * rows // qn
     zz = (max(nrest - 1, 1),)
     return pl.pallas_call(
         functools.partial(attn_kernel, nz, ndp),
         out_shape=outs,
-        in_specs=[vm] * 8 + [hbm] * 3,
+        in_specs=[vm] * 8 + [hbm] * 2,
         out_specs=(vm,) + (hbm,) * (len(outs) - 1),
         scratch_shapes=[
             pltpu.VMEM(sh["xg"], BF), pltpu.VMEM(sh["w"], BF), pltpu.VMEM(sh["wo"], BF), pltpu.VMEM(sh["g"], BF),
             pltpu.VMEM(sh["kv"], BF), pltpu.VMEM(sh["q"], BF), pltpu.VMEM((keys, hd), BF), pltpu.VMEM((hd + 16, keys), BF),
             pltpu.VMEM(sh["q"], BF), pltpu.VMEM(sh["lse"], F32), pltpu.VMEM((nq, keys, qn), F32),
             pltpu.VMEM((2, 2, rows, d), BF), pltpu.VMEM((2, rows, d), BF), pltpu.VMEM((rows, d), BF), pltpu.VMEM((rows, d), F32),
-            dma((12,)), dma((3,)), dma((3,)), dma((3,)), dma((3,))] + [dma(zz), dma(zz), dma((nrest, 6)), dma((nrest, 6))] * 3 + [
+            dma((12,)), dma((3,)), dma((3,)), dma((3,)), dma((3,))] + [dma((nrest,)), dma((nrest,)), dma((nrest, 6)), dma((nrest, 6))] * 3 + [
             dma, dma, dma((3,)), dma((3,)), dma((2, nz // 2)), dma((2, nz // 2)), dma((2, 4)), dma((2, 4)),
-            dma((3,) + zz), dma((3,) + zz), dma((3, 8)), dma((3, 8)), dma((8,)), dma((8,)),
+            dma((2, nrest)), dma((2, nrest)), dma((3, 8)), dma((3, 8)), dma((8,)), dma((8,)),
         ],
         compiler_params=pltpu.CompilerParams(collective_id=2, has_side_effects=True, vmem_limit_bytes=58 * 2**20),
         name="attention",
-    )(tokens, wpack, w_out, gpack, cosT, sinT, starts, cot, wg, wu, wd)
+    )(tokens, wpack, w_out, gpack, cosT, sinT, starts, cot, wg, wu)
 
 
 def back_kernel(nz, ndp, m_ref, dn2_ref, gain_ref, cot_ref, tok_ref, cos_ref, sin_ref, start_ref,
-                xg_in, wqkv_in, wo_in, q_in, kv_in, o_in, lse_in, gd_in, gg_in, gu_in,
-                dx_out, gq_out, gkv_out, gwo_out, gain_out, fd_out, fg_out, fu_out,
+                xg_in, wqkv_in, wo_in, q_in, kv_in, o_in, lse_in, down_in, gg_in, gu_in,
+                dx_out, block_out, gq_out, gkv_out, gwo_out, gain_out, fg_out, fu_out,
                 xg, wqkv, wo, qbuf, kvbuf, obuf, lbuf, dag, dob, delta, kn, vn, kt, bias, dkv, dqb, kvp, kvin, dqkv,
-                gob, go1, go2, gof, gqb, gq1, gq2, gqf, gkb, gk1, gk2, gkf, gsend, gpart, part, cin, xin, total, ogot, val, got,
+                gob, go1, go2, gof, gqb, gq1, gq2, gqf, gkb, gk1, gk2, gkf, gsend, gpart, part, cin, xin, total, ogot, val, got, fb, b0, b1, b2,
                 lsem, s_x, r_x, s_o0, r_o0, s_o1, r_o1, s_q0, r_q0, s_q1, r_q1, s_k0, r_k0, s_k1, r_k1,
-                s_kv, r_kv, s_p, r_p, s_rest, r_rest, s_od, r_od, s_gq, r_gq, s_gk, r_gk, s_v, r_v):
+                s_kv, r_kv, s_p, r_p, s_rest, r_rest, s_od, r_od, s_gq, r_gq, s_gk, r_gk, s_v, r_v, s_b, r_b):
     at = place()
     log = Log()
     rows, d = m_ref.shape
@@ -904,7 +938,7 @@
     target = lax.rem(lin, npeers) * 4 + lin // npeers
     source = lax.rem(lin, 4) * npeers + lin // 4
     loads = [pltpu.make_async_copy(a, b, lsem.at[k]) for k, (a, b) in enumerate((
-        (kv_in, kvbuf), (wo_in, wo), (o_in, obuf), (q_in, qbuf), (lse_in, lbuf), (xg_in, xg), (wqkv_in, wqkv)))]
+        (kv_in, kvbuf), (wo_in, wo), (o_in, obuf), (q_in, qbuf), (lse_in, lbuf), (down_in, fb), (xg_in, xg), (wqkv_in, wqkv)))]
     for cp in loads:
         cp.start()
     quad = (("c",), ("x",), ("x", "c"))
@@ -936,12 +970,11 @@
     qx.start()
     gs = AllSum(at, log, val, got, nrest, s_v, r_v)
     gs.start(0)
-    fars = ((gd_in, fd_out), (gg_in, fg_out), (gu_in, fu_out))
-    units = fd_out.shape[1]
-    for k, (a, b) in enumerate(fars):
-        for o in range(1, nrest):
-            dev, _ = at_rest(at, nrest - o, nrest)
-            log.push(a.at[pl.ds(o * units, units), :], b.at[o - 1], s_rest.at[k, o - 1], r_rest.at[k, o - 1], dev)
+    units = fg_out.shape[1]
+    swaps = [Pushes(at, log, nrest, (lambda o, a=a: a.at[pl.ds(o * units, units), :]), c, s_rest.at[k], r_rest.at[k], True)
+             for k, (a, c) in enumerate(((gg_in, fg_out), (gu_in, fu_out)))]
+    swaps[0].start()
+    swaps[1].start()
     loads[0].wait()
     for i in range(nz):
         kn[i * tl:(i + 1) * tl, :] = jnp.transpose(kvbuf[i, :hd, :].astype(F32)).astype(BF)
@@ -956,6 +989,9 @@
     gs.take(0)
     gs.start(1)
     qx.forward()
+    sb = Scatter(at, fb, None, b0, b1, b2, s_b, r_b)
+    for p in range(3):
+        sb.start(sb.stage_copy(p, 0))
     qx.finish()
     da = dag[...].reshape(tl, d)
     doT = nt(wo[...].reshape(qc, d), da).astype(BF)
@@ -985,16 +1021,22 @@
             dqb[pl.ds(pl.multiple_of(h * hd, hd), hd), :] = rot_rows(nn(kt[...], ds) * 0.125, cos_ref[...], -sin_ref[...])
 
     heads(0, 3)
+    for p in range(3):
+        sb.step(p, 0)
     gs.take(2)
     gs.start(3)
     for o in far_first:
         mo.stage2(o)
     heads(3, 6)
+    for p in range(3):
+        sb.step(p, 1)
     gs.take(3)
     gs.start(4)
     for o in far_first:
         mo.stage3(o)
     heads(6, 8)
+    for p in range(3):
+        sb.finish(p, block_out, m_ref)
     for i in range(nz):
         kvp[i] = dkv[:, i * tl:(i + 1) * tl].astype(BF)
     for o in range(1, nz):
@@ -1002,7 +1044,7 @@
         log.push(kvp.at[i], kvin.at[o - 1], s_kv.at[o - 1], r_kv.at[o - 1], dev)
     dqkv[:, :qc] = jnp.transpose(dqb[...]).astype(BF)
     mq = Merge(at, log, gqb, gq1, gq2, gqf, nrest, ((0, qc // 2, "dl", "zl"), (qc // 2, qc // 2, "zl", "dl")), (s_q0, r_q0, s_q1, r_q1))
-    mk = Merge(at, log, gkb, gk1, gk2, gkf, nrest, ((0, 2 * hd, "zl", "dl"),), (s_k0, r_k0, s_k1, r_k1))
+    mk = Merge(at, log, gkb, gk1, gk2, gkf, nrest, ((0, 2 * hd, "dl", "zl"),), (s_k0, r_k0, s_k1, r_k1))
 
     def weight_grad(dst, lo, hi):
         step = 256
@@ -1079,19 +1121,18 @@
             dev = other(at, *f)
             tt = dev[4] * 2 + dev[5]
             landed(dst.at[tt], rs.at[k], dev)
-    for k, (a, b) in enumerate(fars):
-        for o in range(1, nrest):
-            dev, _ = at_rest(at, o, nrest)
-            landed(b.at[o - 1], r_rest.at[k, o - 1], dev)
+    for sw_ in swaps:
+        sw_.finish()
 
     @pl.when(source != lin)
     def _():
         pltpu.make_async_remote_copy(gsend, ogot, s_od, r_od, device_id=device_of(source, nz), device_id_type=MESH).wait_send()
 
+    sb.close()
     log.close()
 
 
-def back(nz, ndp, m, dn2, gain, cot, tokens, cosT, sinT, starts, xg, wqkv, wo, q, kv, o, lse, grads):
+def back(nz, ndp, m, dn2, gain, cot, tokens, cosT, sinT, starts, xg, wqkv, wo, q, kv, o, lse, down, grads):
     rows, d = m.shape
     hd = HEAD_DIM
     qc = GROUP * hd
@@ -1105,8 +1146,8 @@
     dma = pltpu.SemaphoreType.DMA
     sd = jax.ShapeDtypeStruct
     nf = max(nrest - 1, 1)
-    outs = (sd((rows, d), F32), sd((4, wr, qc), BF), sd((4, wr, 2 * hd), BF), sd((wr, d), F32), sd((16, 128), F32)) + (
-        sd((nrest - 1, units, d), BF),) * 3
+    outs = (sd((rows, d), F32), sd((rows, d), BF), sd((4, wr, qc), BF), sd((4, wr, 2 * hd), BF), sd((wr, d), F32), sd((16, 128), F32)) + (
+        sd((nrest - 1, units, d), BF),) * 2
     V = pltpu.VMEM
 
     def merge_bufs(r, c):
@@ -1116,7 +1157,7 @@
         functools.partial(back_kernel, nz, ndp),
         out_shape=outs,
         in_specs=[vm] * 8 + [hbm] * 10,
-        out_specs=(vm,) * 5 + (hbm,) * 3,
+        out_specs=(vm,) * 6 + (hbm,) * 2,
         scratch_shapes=[
             V(xg.shape, BF), V(wqkv.shape, BF), V(wo.shape, BF), V(q.shape, BF), V(kv.shape, BF), V(o.shape, BF), V(lse.shape, F32),
             V((2, 2, rows, d), BF), V(q.shape, BF), V(lse.shape, F32), V((keys, hd), BF), V((keys, hd), BF), V((hd, keys), BF),
@@ -1125,12 +1166,13 @@
         + merge_bufs(wr, d) + merge_bufs(4 * wr, qc) + merge_bufs(4 * wr, 2 * hd) + [
             V((wr, d), BF), V((4 * wr, qc + 2 * hd), BF), V((2, 2, rows, d), BF), V((2, rows, d), BF), V((rows, d), BF), V((rows, d), F32),
             V((wr, d), BF), V((5, 16, 128), F32), V((4 + nf, 16, 128), F32),
-            dma((7,)), dma((3,)), dma((3,))] + [dma((nf,)), dma((nf,)), dma((nrest, 6)), dma((nrest, 6))] * 3 + [
-            dma((nz,)), dma((nz,)), dma((2, 4)), dma((2, 4)), dma((3, nf)), dma((3, nf)), dma, dma, dma((3,)), dma((3,)), dma((3,)), dma((3,)),
-            dma((4 + nf,)), dma((4 + nf,))],
+            V(down.shape, BF), V((2, 2, rows, d), BF), V((2, rows, d), BF), V((rows, d), BF),
+            dma((8,)), dma((3,)), dma((3,))] + [dma((nf,)), dma((nf,)), dma((nrest, 6)), dma((nrest, 6))] * 3 + [
+            dma((nz,)), dma((nz,)), dma((2, 4)), dma((2, 4)), dma((2, nrest)), dma((2, nrest)), dma, dma, dma((3,)), dma((3,)), dma((3,)), dma((3,)),
+            dma((4 + nf,)), dma((4 + nf,)), dma((3, 4)), dma((3, 4))],
         compiler_params=pltpu.CompilerParams(collective_id=3, has_side_effects=True, vmem_limit_bytes=62 * 2**20),
         name="backward",
-    )(m, dn2, gain, cot, tokens, cosT, sinT, starts, xg, wqkv, wo, q, kv, o, lse, *grads)
+    )(m, dn2, gain, cot, tokens, cosT, sinT, starts, xg, wqkv, wo, q, kv, o, lse, down, *grads)
 
 
 def local(tokens, gain_attn, w_query, w_key, w_value, w_out, gain_mlp, w_gate_t, w_up_t, w_down, doc_ids, cotangent, nz, ndp):
@@ -1157,13 +1199,12 @@
     fill = -units % 16
     if fill:
         w_gate_t, w_up_t, w_down = (jnp.pad(w, ((0, fill), (0, 0))) for w in (w_gate_t, w_up_t, w_down))
-    m, q, kv, o, lse, xg, wqkv, wo, gains, cot_all, wgt, wut, wdn = attn(
-        nz, ndp, tokens, wpack, w_out, gpack, cosT, sinT, starts[None], cotangent, w_gate_t, w_up_t, w_down)
+    m, q, kv, o, lse, xg, wqkv, wo, gains, cot_all, wgt, wut = attn(
+        nz, ndp, tokens, wpack, w_out, gpack, cosT, sinT, starts[None], cotangent, w_gate_t, w_up_t)
     gm = gains[:, :, :, 0, :wr].reshape(1, d).astype(F32)
-    down, dn2, gwd, gwg, gwu = mlp(m, gm, cot_all, (w_gate_t, w_up_t, w_down), (wgt, wut, wdn))
-    dx, gq, gkv, gwo, gsum, fd, fg, fu = back(
-        nz, ndp, m, dn2, gm, cotangent, tokens, cosT, sinT, starts[None], xg, wqkv, wo, q, kv, o, lse, (gwd, gwg, gwu))
-    block_out = (m + down.astype(F32)).astype(BF)
+    down, dn2, gwd, gwg, gwu, fd = mlp(nz * ndp // 4, m, gm, cot_all, (w_gate_t, w_up_t, w_down), (wgt, wut))
+    dx, block_out, gq, gkv, gwo, gsum, fg, fu = back(
+        nz, ndp, m, dn2, gm, cotangent, tokens, cosT, sinT, starts[None], xg, wqkv, wo, q, kv, o, lse, down, (gwg, gwu))
 
     def own(a, far):
         return (a[:units + fill].astype(F32) + jnp.sum(far.astype(F32), axis=0))[:units]

time: 489 us -> 453 us (0.926)
  Pallas kernels: 457 us -> 423 us
    pallas_call x1, Pallas kernels: 164 us -> 129 us  [attn(): pl.pallas_call(functools.partial(attn_kernel, nz, ndp), out_shape=outs, i...]
    pallas_call x1, Pallas kernels: 129 us -> 143 us  [mlp(): pl.pallas_call(functools.partial(mlp_kernel, nrest), out_shape=(sd(cube +...]
    pallas_call x1, Pallas kernels: 164 us -> 151 us  [back(): pl.pallas_call(functools.partial(back_kernel, nz, ndp), out_shape=outs, i...]
where the time goes in v3:
time: 453 us; the launch traced here: 447 us
  Pallas kernels  423 us (93%)
  local copies, waits for them, and re-layouts  11.9 us (3%)
  other arithmetic  10.5 us (2%)
    pallas_call x1, Pallas kernels, back(): pl.pallas_call(functools.partial(back_kernel, nz, ndp), out_shape=outs, i...  151 us
    pallas_call x1, Pallas kernels, mlp(): pl.pallas_call(functools.partial(mlp_kernel, nrest), out_shape=(sd(cube +...  143 us
    pallas_call x1, Pallas kernels, attn(): pl.pallas_call(functools.partial(attn_kernel, nz, ndp), out_shape=outs, i...  129 us

profile of v3, /device:TPU:1, one launch (start us, length us, event | category | flops | bytes accessed | tf_op | source)
XLA Modules:
  0.0 446.7 jit_solution(2854205632496347490)
XLA Ops:
  0.7 0.7 convert_element_type.47
  1.3 0.7 constant_dynamic-slice_fusion
  2.0 1.3 convert_reduce_fusion
  3.3 0.0 copy-start.8
  3.3 1.3 pad.4.gpack
  4.6 0.9 reshape.90
  5.4 0.9 reshape.91
  6.3 1.0 multiply_sine_fusion
  7.3 1.0 copy.38
  8.3 0.9 fusion.4.wpack
  9.1 0.0 copy-done.8
  9.1 129.2 %attention.1 = (f32[128,2048]{1,0:T(8,128)}, bf16[8,64,512]{2,1,0:T(8,128)(2,1)}, bf16[4,128,512]{2,1,0:T(8,128)(2,1)}, bf16[8,64,512]{2,1,0:T(8,128)(2,1)}, f32...) custom-call(bf16[128,2048]{1,0:T(8,128)(2,1)} %tok_ref.3, ...), custom_call_target="tpu_custom_call" | custom-call | tf_op jit(solution)/shard_map/attention/pallas_call | solution.py:897
  138.3 0.9 convert_reduce_fusion.1
  139.2 0.7 reshape.98.gain_ref
  139.9 143.0 %mlp.1 = (bf16[2,2,2,128,2048]{4,3,2,1,0:T(8,128)(2,1)}, f32[128,2048]{1,0:T(8,128)}, bf16[352,2048]{1,0:T(8,128)(2,1)}, bf16[352,2048]{1,0:T(8,128)(2,1)}, bf16...) custom-call(f32[128,2048]{1,0:T(8,128)} %get-tuple-element.37.m_ref, f32[1,2048]{1,0:T(1,128)} %reshape.98.gain_ref, ...), custom_call_target="tpu_custom_call" | custom-call | tf_op jit(solution)/shard_map/mlp/pallas_call | solution.py:651
  282.9 0.0 copy-start.1
  283.0 151.0 %backward.1 = (f32[128,2048]{1,0:T(8,128)}, bf16[128,2048]{1,0:T(8,128)(2,1)}, bf16[4,64,512]{2,1,0:T(8,128)(2,1)}, bf16[4,64,128]{2,1,0:T(8,128)(2,1)}, f32[64,...) custom-call(f32[128,2048]{1,0:T(8,128)} %get-tuple-element.37.m_ref, ...), custom_call_target="tpu_custom_call" | custom-call | tf_op jit(solution)/shard_map/backward/pallas_call | solution.py:1156
  434.0 0.0 copy-done.1
  434.0 0.0 copy-start
  434.0 0.0 copy-start.3
  434.0 3.8 convert_add_fusion
  437.9 0.0 copy-done
  437.9 0.0 copy-done.3
  437.9 0.0 copy-start.6
  437.9 0.0 copy-start.7
  437.9 1.3 fusion.1
  439.2 1.3 dynamic_slice.7
  440.4 0.0 copy-done.6
  440.4 0.0 copy-done.7
  440.4 0.7 fusion.3
  441.2 0.1 fusion.5
  441.3 0.0 copy-start.5
  441.3 0.1 slice_bitcast_fusion
  441.3 0.0 copy-start.2
  441.3 0.8 copy.36
  442.2 0.1 copy.34
  442.3 0.8 reshape.96
  443.0 0.1 copy.33
  443.1 0.8 reshape.95
  443.9 0.0 copy-done.5
  443.9 0.0 copy-start.4
  443.9 0.8 copy.42
  444.7 0.0 copy-done.2
  444.7 1.0 copy.43
  445.7 0.0 copy-done.4
  445.7 0.8 copy.44
  (4 shorter events, 0.0 us)
Async XLA Ops:
  3.3 5.8 %copy-start.8 = (s32[512]{0:T(512)}, s32[512]{0:T(512)S(1)}, u32[]{:S(2)}) copy-start(s32[512]{0:T(512)S(1)} %convert_reduce_fusion) | copy-start | bytes 6148
  282.9 151.1 %copy-start.1 = (bf16[352,2048]{1,0:T(8,128)(2,1)S(1)}, bf16[352,2048]{1,0:T(8,128)(2,1)}, u32[]{:S(2)}) copy-start(bf16[352,2048]{1,0:T(8,128)(2,1)} %get-tuple-element.52.gu_in) | copy-start | bytes 4325380
  434.0 3.8 copy-start
  434.0 3.8 copy-start.3
  437.9 2.6 copy-start.6
  437.9 2.6 copy-start.7
  441.3 2.6 copy-start.5
  441.3 3.4 copy-start.2
  443.9 1.8 copy-start.4

commit v4 on v3

--- a/solution.py
+++ b/solution.py
@@ -507,8 +507,8 @@
             cp.wait_send()
 
 
-def mlp_kernel(nrest, m_ref, gain_ref, cot_ref, wg_own, wu_own, wd_own, wg_far, wu_far, down_out, dn2_out, gwd_out, gwg_out, gwu_out, fd_out,
-               rows, wgu, wd, gus, zb, dgu, fa, fb, core_in, a0, a1, a2,
+def mlp_kernel(nrest, m_ref, gain_ref, cot_in, wg_own, wu_own, wd_own, wg_far, wu_far, down_out, dn2_out, gwd_out, gwg_out, gwu_out, fd_out,
+               cot_ref, rows, wgu, wd, gus, zb, dgu, fa, fb, core_in, a0, a1, a2,
                lsem, gs, gr, gcs, gcr, sas, sar, sbs, sbr, s_wd, r_wd, s_fd, r_fd, credit):
     at = place()
     log = Log()
@@ -520,6 +520,7 @@
     for k, (own_w, far_w, lo) in enumerate(((wg_own, wg_far, 0), (wu_own, wu_far, units))):
         copies.append(pltpu.make_async_copy(own_w, wgu.at[lo:lo + part, :], lsem.at[2 * k]))
         copies.append(pltpu.make_async_copy(far_w, wgu.at[lo + part:lo + units, :], lsem.at[2 * k + 1]))
+    copies.append(pltpu.make_async_copy(cot_in, cot_ref, lsem.at[6]))
     for cp in copies:
         cp.start()
     for flip in ("c", "x", "zl", "dl"):
@@ -651,9 +652,10 @@
     return pl.pallas_call(
         functools.partial(mlp_kernel, nrest),
         out_shape=(sd(cube + (rows, d), BF), sd((rows, d), F32)) + (sd((units, d), BF),) * 3 + (sd((nrest - 1, part, d), BF),),
-        in_specs=[vm, vm, vm] + [hbm] * 5,
+        in_specs=[vm, vm] + [hbm] * 6,
         out_specs=(hbm,) + (vm,) * 4 + (hbm,),
         scratch_shapes=[
+            pltpu.VMEM(cube + (2 * rows, d), BF),
             pltpu.VMEM(cube + (2 * rows, d), BF),
             pltpu.VMEM((2 * units, d), BF),
             pltpu.VMEM((units, d), BF),
@@ -664,7 +666,7 @@
             pltpu.VMEM(cube + (2 * rows, d), BF),
             pltpu.VMEM(cube + (rows, d), BF),
             pltpu.VMEM((2, 2, rows, d), BF), pltpu.VMEM((2, rows, d), BF), pltpu.VMEM((rows, d), BF),
-            dma((6,)), dma((3, 8)), dma((3, 8)), dma((8,)), dma((8,)),
+            dma((7,)), dma((3, 8)), dma((3, 8)), dma((8,)), dma((8,)),
             dma((3, 4)), dma((3, 4)), dma((3, 4)), dma((3, 4)), dma((nf,)), dma((nf,)), dma((nf,)), dma((nf,)), pltpu.SemaphoreType.REGULAR,
         ],
         compiler_params=pltpu.CompilerParams(collective_id=1, has_side_effects=True, vmem_limit_bytes=63 * 2**20),
@@ -678,9 +680,9 @@
     return jnp.concatenate([a * cos - b * sin, b * cos + a * sin], axis=0)
 
 
-def attn_kernel(nz, ndp, tok_ref, wpack, wout_ref, gpack, cos_ref, sin_ref, start_ref, cot_ref, wg_ref, wu_ref,
+def attn_kernel(nz, ndp, tok_ref, wpack, wout_ref, gain_ref, cos_ref, sin_ref, start_ref, cot_ref, wg_ref, wu_ref,
                 m_out, q_out, kv_out, o_out, lse_out, xg_out, wqkv_out, wo_out, gain_out, cot_out, wg_out, wu_out,
-                xg, wbuf, wobuf, gbuf, kvbuf, qbuf, kn, vt, obuf, lbuf, bias, part, cin, xin, total,
+                xg, wbuf, wobuf, gbuf, kvbuf, qbuf, kn, vt, obuf, lbuf, bias, part, cin, xin, total, gpack,
                 lsem, s_disp, r_disp, s_gd, r_gd, s_w0, r_w0, s_w1, r_w1, s_g0, r_g0, s_g1, r_g1, s_o0, r_o0, s_o1, r_o1,
                 s_od, r_od, s_x, r_x, s_kv, r_kv, s_p, r_p, s_rest, r_rest, gs, gr, gcs, gcr):
     at = place()
@@ -713,6 +715,8 @@
     here = [pltpu.make_async_copy(cot_ref, g.block((), at["c"]), lsem.at[0])]
     for cp in here:
         cp.start()
+    gpack[...] = jnp.zeros_like(gpack)
+    gpack[:, :wr] = jnp.broadcast_to(gain_ref[...].astype(F32), (16, wr)).astype(BF)
     for k, f in enumerate(quad):
         dev = other(at, *f)
         tt = dev[4] * 2 + dev[5]
@@ -802,7 +806,6 @@
         landed(kvbuf.at[zi], r_kv.at[1, o], other(at, "zl"))
     g.second()
     swaps[0].start()
-    swaps[1].start()
     save.append(pltpu.make_async_copy(kvbuf, kv_out, lsem.at[8]))
     save[-1].start()
     tl = kvbuf.shape[2]
@@ -826,6 +829,7 @@
     for o in range(1, nrest):
         so.stage1(o)
     heads(0, 0, 4)
+    swaps[1].start()
     g.third()
     heads(0, 4, 8)
     for o in range(1, nrest):
@@ -904,6 +908,7 @@
             pltpu.VMEM(sh["kv"], BF), pltpu.VMEM(sh["q"], BF), pltpu.VMEM((keys, hd), BF), pltpu.VMEM((hd + 16, keys), BF),
             pltpu.VMEM(sh["q"], BF), pltpu.VMEM(sh["lse"], F32), pltpu.VMEM((nq, keys, qn), F32),
             pltpu.VMEM((2, 2, rows, d), BF), pltpu.VMEM((2, rows, d), BF), pltpu.VMEM((rows, d), BF), pltpu.VMEM((rows, d), F32),
+            pltpu.VMEM((16, 128), BF),
             dma((12,)), dma((3,)), dma((3,)), dma((3,)), dma((3,))] + [dma((nrest,)), dma((nrest,)), dma((nrest, 6)), dma((nrest, 6))] * 3 + [
             dma, dma, dma((3,)), dma((3,)), dma((2, nz // 2)), dma((2, nz // 2)), dma((2, 4)), dma((2, 4)),
             dma((2, nrest)), dma((2, nrest)), dma((3, 8)), dma((3, 8)), dma((8,)), dma((8,)),
@@ -1187,7 +1192,7 @@
     ga = gain_attn.astype(F32)[:, None]
     wall = jnp.concatenate([w_query.reshape(wr, 4, qc), w_key.reshape(wr, 4, hd), w_value.reshape(wr, 4, hd)], axis=2).transpose(1, 0, 2)
     wpack = (wall.astype(F32) * ga[None]).astype(BF)
-    gpack = jnp.pad(gain_mlp[None], ((0, 15), (0, 128 - wr)))
+    gpack = gain_mlp[None]
     first = zi * grows
     own_ids = lax.dynamic_slice_in_dim(seq_ids, first, grows, 0)
     qpos = first + jnp.arange(grows, dtype=jnp.int32)

time: 453 us -> 442 us (0.976)
  Pallas kernels: 423 us -> 414 us
    pallas_call x1, Pallas kernels: 143 us -> 133 us  [mlp(): pl.pallas_call(functools.partial(mlp_kernel, nrest), out_shape=(sd(cube +...]
where the time goes in v4:
time: 442 us; the launch traced here: 436 us
  Pallas kernels  414 us (94%)
  local copies, waits for them, and re-layouts  10.6 us (2%)
  other arithmetic  10.5 us (2%)
    pallas_call x1, Pallas kernels, back(): pl.pallas_call(functools.partial(back_kernel, nz, ndp), out_shape=outs, i...  152 us
    pallas_call x1, Pallas kernels, mlp(): pl.pallas_call(functools.partial(mlp_kernel, nrest), out_shape=(sd(cube +...  133 us
    pallas_call x1, Pallas kernels, attn(): pl.pallas_call(functools.partial(attn_kernel, nz, ndp), out_shape=outs, i...  129 us

profile of v4, /device:TPU:1, one launch (start us, length us, event | category | flops | bytes accessed | tf_op | source)
XLA Modules:
  0.0 436.1 jit_solution(7422710308511322468)
XLA Ops:
  0.7 0.7 convert_element_type.45
  1.3 0.7 constant_dynamic-slice_fusion
  2.0 1.3 convert_reduce_fusion
  3.3 0.0 copy-start.8
  3.3 0.9 reshape.90
  4.2 0.9 reshape.91
  5.1 1.0 multiply_sine_fusion
  6.0 1.0 copy.38
  7.0 0.9 fusion.4.wpack
  7.9 0.0 copy-done.8
  7.9 129.2 %attention.1 = (f32[128,2048]{1,0:T(8,128)}, bf16[8,64,512]{2,1,0:T(8,128)(2,1)}, bf16[4,128,512]{2,1,0:T(8,128)(2,1)}, bf16[8,64,512]{2,1,0:T(8,128)(2,1)}, f32...) custom-call(bf16[128,2048]{1,0:T(8,128)(2,1)} %tok_ref.3, ...), custom_call_target="tpu_custom_call" | custom-call | tf_op jit(solution)/shard_map/attention/pallas_call | solution.py:901
  137.1 0.9 convert_reduce_fusion.1
  138.0 0.7 reshape.98.gain_ref
  138.7 132.8 %mlp.1 = (bf16[2,2,2,128,2048]{4,3,2,1,0:T(8,128)(2,1)}, f32[128,2048]{1,0:T(8,128)}, bf16[352,2048]{1,0:T(8,128)(2,1)}, bf16[352,2048]{1,0:T(8,128)(2,1)}, bf16...) custom-call(f32[128,2048]{1,0:T(8,128)} %get-tuple-element.37.m_ref, f32[1,2048]{1,0:T(1,128)} %reshape.98.gain_ref, ...), custom_call_target="tpu_custom_call" | custom-call | tf_op jit(solution)/shard_map/mlp/pallas_call | solution.py:652
  271.5 0.0 copy-start.1
  271.5 151.9 %backward.1 = (f32[128,2048]{1,0:T(8,128)}, bf16[128,2048]{1,0:T(8,128)(2,1)}, bf16[4,64,512]{2,1,0:T(8,128)(2,1)}, bf16[4,64,128]{2,1,0:T(8,128)(2,1)}, f32[64,...) custom-call(f32[128,2048]{1,0:T(8,128)} %get-tuple-element.37.m_ref, ...), custom_call_target="tpu_custom_call" | custom-call | tf_op jit(solution)/shard_map/backward/pallas_call | solution.py:1161
  423.4 0.0 copy-done.1
  423.4 0.0 copy-start
  423.4 0.0 copy-start.3
  423.4 3.8 convert_add_fusion
  427.2 0.0 copy-done
  427.2 0.0 copy-done.3
  427.2 0.0 copy-start.6
  427.2 0.0 copy-start.7
  427.3 1.3 fusion.1
  428.6 1.3 dynamic_slice.7
  429.8 0.0 copy-done.6
  429.8 0.0 copy-done.7
  429.8 0.7 fusion.3
  430.6 0.1 fusion.5
  430.7 0.0 copy-start.5
  430.7 0.1 slice_bitcast_fusion
  430.7 0.0 copy-start.2
  430.7 0.8 copy.36
  431.6 0.1 copy.34
  431.7 0.8 reshape.96
  432.4 0.1 copy.33
  432.5 0.8 reshape.95
  433.3 0.0 copy-done.5
  433.3 0.0 copy-start.4
  433.3 0.8 copy.42
  434.1 0.0 copy-done.2
  434.1 1.0 copy.43
  435.1 0.0 copy-done.4
  435.1 0.8 copy.44
  (4 shorter events, 0.0 us)
Async XLA Ops:
  3.3 4.6 %copy-start.8 = (s32[512]{0:T(512)}, s32[512]{0:T(512)S(1)}, u32[]{:S(2)}) copy-start(s32[512]{0:T(512)S(1)} %convert_reduce_fusion) | copy-start | bytes 6148
  271.5 151.9 %copy-start.1 = (bf16[352,2048]{1,0:T(8,128)(2,1)S(1)}, bf16[352,2048]{1,0:T(8,128)(2,1)}, u32[]{:S(2)}) copy-start(bf16[352,2048]{1,0:T(8,128)(2,1)} %get-tuple-element.52.gu_in) | copy-start | bytes 4325380
  423.4 3.8 copy-start
  423.4 3.8 copy-start.3
  427.2 2.6 copy-start.6
  427.2 2.6 copy-start.7
  430.7 2.6 copy-start.5
  430.7 3.4 copy-start.2
  433.3 1.8 copy-start.4

commit v5 on v4

--- a/solution.py
+++ b/solution.py
@@ -534,8 +534,6 @@
     rows[at["dl"], at["zl"], at["x"], own, :] = (m * inv * gain_ref[...]).astype(BF)
     pl.semaphore_wait(pltpu.get_barrier_semaphore(), 3 + nrest)
     g.first()
-    for o in range(1, nrest):
-        log.push(wd_own, wd.at[o * part:(o + 1) * part, :], s_wd.at[o - 1], r_wd.at[o - 1], at_rest(at, o, nrest)[0])
     for cp in copies:
         cp.wait()
 
@@ -559,6 +557,8 @@
     g.sibling_arrived(())
     units_of(())
     g.third()
+    for o in range(1, nrest):
+        log.push(wd_own, wd.at[o * part:(o + 1) * part, :], s_wd.at[o - 1], r_wd.at[o - 1], at_rest(at, o, nrest)[0])
     last = None
     for k in MASKS[1:]:
         g.complete(k)
@@ -829,11 +829,11 @@
     for o in range(1, nrest):
         so.stage1(o)
     heads(0, 0, 4)
-    swaps[1].start()
     g.third()
     heads(0, 4, 8)
     for o in range(1, nrest):
         so.stage2(o)
+    swaps[1].start()
     heads(1, 0, 4)
     heads(1, 4, 8)
     for m in MASKS[1:4]:

time: 442 us -> 440 us (level)
    pallas_call x1, Pallas kernels: 133 us -> 123 us  [mlp(): pl.pallas_call(functools.partial(mlp_kernel, nrest), out_shape=(sd(cube +...]
where the time goes in v5:
time: 440 us; the launch traced here: 434 us
  Pallas kernels  412 us (94%)
  local copies, waits for them, and re-layouts  10.6 us (2%)
  other arithmetic  10.5 us (2%)
    pallas_call x1, Pallas kernels, back(): pl.pallas_call(functools.partial(back_kernel, nz, ndp), out_shape=outs, i...  156 us
    pallas_call x1, Pallas kernels, attn(): pl.pallas_call(functools.partial(attn_kernel, nz, ndp), out_shape=outs, i...  133 us
    pallas_call x1, Pallas kernels, mlp(): pl.pallas_call(functools.partial(mlp_kernel, nrest), out_shape=(sd(cube +...  123 us

profile of v5, /device:TPU:1, one launch (start us, length us, event | category | flops | bytes accessed | tf_op | source)
XLA Modules:
  0.0 433.7 jit_solution(10991741523411095639)
XLA Ops:
  0.7 0.7 convert_element_type.45
  1.3 0.7 constant_dynamic-slice_fusion
  2.0 1.3 convert_reduce_fusion
  3.3 0.0 copy-start.8
  3.3 0.9 reshape.90
  4.2 0.9 reshape.91
  5.1 1.0 multiply_sine_fusion
  6.0 1.0 copy.38
  7.0 0.9 fusion.4.wpack
  7.9 0.0 copy-done.8
  7.9 132.7 %attention.1 = (f32[128,2048]{1,0:T(8,128)}, bf16[8,64,512]{2,1,0:T(8,128)(2,1)}, bf16[4,128,512]{2,1,0:T(8,128)(2,1)}, bf16[8,64,512]{2,1,0:T(8,128)(2,1)}, f32...) custom-call(bf16[128,2048]{1,0:T(8,128)(2,1)} %tok_ref.3, ...), custom_call_target="tpu_custom_call" | custom-call | tf_op jit(solution)/shard_map/attention/pallas_call | solution.py:901
  140.6 0.9 convert_reduce_fusion.1
  141.5 0.7 reshape.98.gain_ref
  142.2 122.7 %mlp.1 = (bf16[2,2,2,128,2048]{4,3,2,1,0:T(8,128)(2,1)}, f32[128,2048]{1,0:T(8,128)}, bf16[352,2048]{1,0:T(8,128)(2,1)}, bf16[352,2048]{1,0:T(8,128)(2,1)}, bf16...) custom-call(f32[128,2048]{1,0:T(8,128)} %get-tuple-element.37.m_ref, f32[1,2048]{1,0:T(1,128)} %reshape.98.gain_ref, ...), custom_call_target="tpu_custom_call" | custom-call | tf_op jit(solution)/shard_map/mlp/pallas_call | solution.py:652
  264.9 0.0 copy-start.1
  264.9 156.1 %backward.1 = (f32[128,2048]{1,0:T(8,128)}, bf16[128,2048]{1,0:T(8,128)(2,1)}, bf16[4,64,512]{2,1,0:T(8,128)(2,1)}, bf16[4,64,128]{2,1,0:T(8,128)(2,1)}, f32[64,...) custom-call(f32[128,2048]{1,0:T(8,128)} %get-tuple-element.37.m_ref, ...), custom_call_target="tpu_custom_call" | custom-call | tf_op jit(solution)/shard_map/backward/pallas_call | solution.py:1161
  421.0 0.0 copy-done.1
  421.0 0.0 copy-start
  421.0 0.0 copy-start.3
  421.0 3.8 convert_add_fusion
  424.8 0.0 copy-done
  424.9 0.0 copy-done.3
  424.9 0.0 copy-start.6
  424.9 0.0 copy-start.7
  424.9 1.3 fusion.1
  426.2 1.3 dynamic_slice.7
  427.4 0.0 copy-done.6
  427.4 0.0 copy-done.7
  427.4 0.7 fusion.3
  428.2 0.1 fusion.5
  428.3 0.0 copy-start.5
  428.3 0.1 slice_bitcast_fusion
  428.3 0.0 copy-start.2
  428.3 0.8 copy.36
  429.2 0.1 copy.34
  429.3 0.8 reshape.96
  430.0 0.1 copy.33
  430.1 0.8 reshape.95
  430.9 0.0 copy-done.5
  430.9 0.0 copy-start.4
  430.9 0.8 copy.42
  431.7 0.0 copy-done.2
  431.7 1.0 copy.43
  432.7 0.0 copy-done.4
  432.7 0.8 copy.44
  (4 shorter events, 0.0 us)
Async XLA Ops:
  3.3 4.6 %copy-start.8 = (s32[512]{0:T(512)}, s32[512]{0:T(512)S(1)}, u32[]{:S(2)}) copy-start(s32[512]{0:T(512)S(1)} %convert_reduce_fusion) | copy-start | bytes 6148
  264.9 156.1 %copy-start.1 = (bf16[352,2048]{1,0:T(8,128)(2,1)S(1)}, bf16[352,2048]{1,0:T(8,128)(2,1)}, u32[]{:S(2)}) copy-start(bf16[352,2048]{1,0:T(8,128)(2,1)} %get-tuple-element.52.gu_in) | copy-start | bytes 4325380
  421.0 3.8 copy-start
  421.0 3.8 copy-start.3
  424.9 2.6 copy-start.6
  424.9 2.6 copy-start.7
  428.3 2.6 copy-start.5
  428.3 3.4 copy-start.2
  430.9 1.8 copy-start.4
